TPU v7x, 32 devices: a whole 2x2x4 slice. The times are simulated.
32 devices in a mesh: occ: 4 (over y, x), vir: 8 (over z, core).
Axes of the slice: x: 2, y: 2, z: 4, core: 2. Of those that a mesh axis runs over, the one named last changes fastest.
Arguments:
- amplitudes: bfloat16 [8, 8, 768, 768], P('occ', None, 'vir'), may hold values from -6 to 6
- integrals: bfloat16 [768, 768], P('vir'), may hold values from -0.21875 to 0.21875
- occ_fock: bfloat16 [8, 8], replicated, may hold values from -2 to 2
- amp_mask: int32 [48, 48], replicated, may hold values 0 or 1
- int_mask: int32 [48, 48], replicated, may hold values 0 or 1
- occ_energy: float32 [8], replicated, may hold values from -2 to -0.5
- vir_energy: float32 [768], replicated, may hold values from 0.5 to 4
Outputs:
- update: float32 [8, 8, 768, 768], P('occ', None, 'vir')
All inputs are finite; a program needn't handle non-finite values.
Results may differ from a plain program's by a relative error of at most 0.002.
Values may be sent and summed in bfloat16 or wider, within the bound.
No kernel may reach another device: no remote copies, remote signals or barrier semaphores. Data moves between devices by JAX's collectives and lax.ppermute only.
A program may use at most 128 MiB of HBM per device.

v0:
```python
import jax
import jax.numpy as jnp
from jax import lax
from jax.sharding import PartitionSpec as P

VB = 16


def expand_rows(mask, first_block, blocks):
    rows_here = lax.dynamic_slice_in_dim(mask, first_block, blocks, 0)
    return jnp.repeat(jnp.repeat(rows_here, VB, axis=0), VB, axis=1).astype(jnp.bfloat16)


def local(amplitudes, integrals, occ_fock, amp_mask, int_mask, occ_energy, vir_energy):
    occ_rows, occ_all, vir_rows, vir_all = amplitudes.shape
    vir_start = lax.axis_index("vir") * vir_rows
    occ_start = lax.axis_index("occ") * occ_rows
    blocks = vir_rows // VB
    first_block = vir_start // VB
    masked = amplitudes * expand_rows(amp_mask, first_block, blocks)[None, None]
    masked_w = integrals * expand_rows(int_mask, first_block, blocks)
    flat_amps = masked.reshape(-1, vir_all)
    full_w = lax.all_gather(masked_w, "vir", axis=0, tiled=True)
    ladder = jnp.dot(flat_amps, full_w, preferred_element_type=jnp.float32)
    ladder = ladder.reshape(occ_rows, occ_all, vir_rows, vir_all)
    holes = jnp.einsum("ikab,kj->ijab", masked, occ_fock, preferred_element_type=jnp.float32)
    mixed = ladder + holes
    outgoing = mixed.astype(jnp.bfloat16)
    halfway = lax.all_to_all(outgoing, "vir", split_axis=3, concat_axis=2, tiled=True)
    arrived = lax.all_to_all(halfway, "occ", split_axis=1, concat_axis=0, tiled=True)
    mirrored = arrived.transpose(1, 0, 3, 2).astype(jnp.float32)
    vir_here = lax.dynamic_slice_in_dim(vir_energy, vir_start, vir_rows, 0)
    occ_here = lax.dynamic_slice_in_dim(occ_energy, occ_start, occ_rows, 0)
    denominator = (
        vir_here[None, None, :, None]
        + vir_energy[None, None, None, :]
        - occ_here[:, None, None, None]
        - occ_energy[None, :, None, None]
    )
    return (mixed + mirrored) / denominator


def solution(mesh):
    in_specs = (P("occ", None, "vir", None), P("vir", None), P(), P(), P(), P(), P())
    out_specs = P("occ", None, "vir", None)
    return jax.shard_map(local, mesh=mesh, in_specs=in_specs, out_specs=out_specs, check_vma=False)
```

profile of v0, /device:TPU:0, one launch (start us, length us, event | category | flops | bytes accessed | tf_op | source)
XLA Modules:
  0.0 174.7 jit_solution(481197463783207924)
XLA Ops:
  6.5 0.0 copy-start
  6.5 0.0 all-gather.2.cloned.1.call-start
  6.5 0.7 dynamic-slice_convert_fusion
  7.3 0.1 copy.31
  7.4 0.1 copy.32
  7.6 1.6 mul.20
  9.2 0.0 all-gather.2.cloned.1.call-update
  9.2 0.1 copy.29
  9.3 0.1 copy.30
  9.5 1.9 %broadcast_multiply_fusion = bf16[2,8,96,768]{3,2,1,0:T(8,128)(2,1)S(1)} fusion(bf16[2,8,96,768]{3,2,1,0:T(8,128)(2,1)} %param.7, bf16[96,768]{1,0:T(8,128)(2,1)S(1)} %copy.30), kind=kLoop, calls=%fused_computation.7 | loop fusion | flops 1179648 | bytes 4866048 | tf_op jit(solution)/shard_map/mul | solution.py:20
  11.4 0.0 copy-done
  11.4 3.7 %fusion = f32[2,96,768,8]{2,3,1,0:T(8,128)} fusion(bf16[2,8,96,768]{3,2,1,0:T(8,128)(2,1)S(1)} %broadcast_multiply_fusion, bf16[8,8]{1,0:T(8,128)(2,1)S(1)} %copy-done), kind=kOutput, calls=%fused_computation.4 | convolution fusion | flops 18874368 | bytes 7078016 | tf_op jit(solution)/shard_map/ikab,kj->ijab/dot_general | solution.py:26
  15.1 19.6 %all-gather.2.cloned.1.call-done = bf16[768,768]{1,0:T(8,128)(2,1)} async-done(((bf16[96,768]{1,0:T(8,128)(2,1)}), bf16[768,768]{1,0:T(8,128)(2,1)}) %all-gather.2.cloned.1.call-update) | async-done | bytes 1179664 | tf_op jit(solution)/shard_map/all_gather | solution.py:23
  34.7 8.5 %fusion.4 = (bf16[2,8,96,768]{3,2,1,0:T(8,128)(2,1)}, f32[2,8,96,768]{3,2,1,0:T(8,128)}) fusion(f32[2,96,768,8]{2,3,1,0:T(8,128)} %fusion, bf16[2,8,96,768]{3,2,1,0:T(8,128)(2,1)S(1)} %broadcast_multiply_fusion, bf16[768,768]{1,0:T(8,128)(2,1)} %all-gather.2.cloned.1.call-done), kind=kOutput, calls=%fused_computation.13 | convolution fusion | flops 1814298624 | bytes 15335424 | tf_op jit(solution)/shard_map/dot_general | solution.py:24
  43.2 4.0 %copy.36 = bf16[2,8,96,768]{2,1,0,3:T(8,128)(2,1)S(1)} copy(bf16[2,8,96,768]{3,2,1,0:T(8,128)(2,1)} %get-tuple-element.5) | data formatting | bytes 4718592 | tf_op jit(solution)/shard_map/convert_element_type | solution.py:28
  47.1 74.8 %all_to_all.27 = bf16[2,8,96,768]{2,1,0,3:T(8,128)(2,1)S(1)} all-to-all(bf16[2,8,96,768]{2,1,0,3:T(8,128)(2,1)S(1)} %copy.36), channel_id=1, replica_groups=mesh['occ'=4,'vir'=8] {'vir'}, dimensions={3} | all-to-all | bytes 4718592 | tf_op jit(solution)/shard_map/all_to_all | solution.py:29
  121.9 2.0 %copy.48 = bf16[2,8,96,8,96]{2,3,4,1,0:T(8,128)(2,1)S(1)} copy(bf16[2,8,96,8,96]{2,1,0,4,3:T(8,128)(2,1)S(1)} %bitcast.35) | data formatting | bytes 4718592 | tf_op jit(solution)/shard_map/all_to_all | solution.py:29
  124.0 3.6 %all_to_all.23 = bf16[2,8,768,96]{2,3,1,0:T(8,128)(2,1)} reshape(bf16[2,8,8,96,96]{3,2,4,1,0:T(8,128)(2,1)S(1)} %bitcast.36) | data formatting | bytes 4718592 | tf_op jit(solution)/shard_map/all_to_all | solution.py:29
  127.6 3.3 %copy.38 = bf16[2,8,768,96]{2,3,0,1:T(8,128)(2,1)} copy(bf16[2,8,768,96]{2,3,1,0:T(8,128)(2,1)} %all_to_all.23) | data formatting | bytes 4718592 | tf_op jit(solution)/shard_map/all_to_all | solution.py:29
  130.8 0.0 copy-start.1
  130.8 0.0 copy-start.2
  130.8 3.8 %all-to-all-start.1 = ((bf16[2,8,768,96]{2,3,0,1:T(8,128)(2,1)}), bf16[2,8,768,96]{2,3,0,1:T(8,128)(2,1)S(1)}, u32[]{:S(2)}, u32[]{:S(2)}) async-start(bf16[2,8,768,96]{2,3,0,1:T(8,128)(2,1)} %copy.38), calls=%async_computation.1 | async-start | bytes 4718592 | tf_op jit(solution)/shard_map/all_to_all | solution.py:30
  134.6 0.0 copy-done.1
  134.6 0.1 dynamic_slice.14
  134.7 0.0 copy-done.2
  134.7 0.1 dynamic_slice.15
  134.8 0.1 broadcast_add_fusion
  134.9 0.1 broadcast_subtract_fusion
  135.0 27.2 %all-to-all-done.1 = bf16[2,8,768,96]{2,3,0,1:T(8,128)(2,1)S(1)} async-done(((bf16[2,8,768,96]{2,3,0,1:T(8,128)(2,1)}), bf16[2,8,768,96]{2,3,0,1:T(8,128)(2,1)S(1)}, u32[]{:S(2)}, u32[]{:S(2)}) %all-to-all-start.1) | async-done | bytes 2359328 | tf_op jit(solution)/shard_map/all_to_all | solution.py:30
  162.2 0.2 copy.39
  162.3 0.0 slice-start
  162.4 0.5 convert_bitcast_fusion
  162.9 0.0 slice-start.1
  162.9 0.4 copy.40
  163.3 1.2 slice-done
  164.5 0.2 slice-done.1
  164.8 3.1 %subtract_divide_fusion = f32[2,8,96,768]{3,2,1,0:T(8,128)} fusion(f32[2,8,96,768]{3,2,1,0:T(8,128)S(1)} %bitcast.34, f32[2,8,96,768]{3,2,1,0:T(8,128)S(1)} %bitcast.32, f32[8]{0:T(128)S(1)} %copy-done.2, f32[2,96,768]{2,1,0:T(8,128)S(1)} %broadcast_subtract_fusion), kind=kLoop, calls=%fused_computation.2 | loop fusion | flops 3538944 | bytes 14745632 | tf_op jit(solution)/shard_map/div | solution.py:40
  (5 shorter events, 0.1 us)
Async XLA Ops:
  6.5 4.9 %copy-start = (bf16[8,8]{1,0:T(8,128)(2,1)S(1)}, bf16[8,8]{1,0:T(8,128)(2,1)}, u32[]{:S(2)}) copy-start(bf16[8,8]{1,0:T(8,128)(2,1)} %param.9) | copy-start | bytes 388
  6.5 28.2 %all-gather.2.cloned.1.call-start = ((), (), s32[]{:S(2)}) async-start(), calls=%async_computation.2 | async-start | bytes 1327104 | tf_op jit(solution)/shard_map/all_gather | solution.py:23
  130.8 3.8 %copy-start.1 = (f32[768]{0:T(1024)S(1)}, f32[768]{0:T(1024)}, u32[]{:S(2)}) copy-start(f32[768]{0:T(1024)} %param.13) | copy-start | bytes 9220
  130.8 3.9 %copy-start.2 = (f32[8]{0:T(128)S(1)}, f32[8]{0:T(128)}, u32[]{:S(2)}) copy-start(f32[8]{0:T(128)} %param.12) | copy-start | bytes 100
  130.8 31.3 %all-to-all-start.1 = ((bf16[2,8,768,96]{2,3,0,1:T(8,128)(2,1)}), bf16[2,8,768,96]{2,3,0,1:T(8,128)(2,1)S(1)}, u32[]{:S(2)}, u32[]{:S(2)}) async-start(bf16[2,8,768,96]{2,3,0,1:T(8,128)(2,1)} %copy.38), calls=%async_computation.1 | async-start | bytes 4718592 | tf_op jit(solution)/shard_map/all_to_all | solution.py:30
  162.3 2.2 %slice-start = ((s8[4718592]{0:T(1024)(128)(4,1)}), s8[4194304]{0:T(1024)(128)(4,1)S(1)}, s32[]{:S(2)}) async-start(s8[4718592]{0:T(1024)(128)(4,1)} %bitcast.33), calls=%async_computation.3 | async-start | bytes 8388608
  162.9 1.9 %slice-start.1 = ((s8[4718592]{0:T(1024)(128)(4,1)}), s8[524288]{0:T(1024)(128)(4,1)S(1)}, s32[]{:S(2)}) async-start(s8[4718592]{0:T(1024)(128)(4,1)} %bitcast.33), calls=%async_computation.4 | async-start | bytes 1048576
Sparse Core Ops, SparseCore 0:
  9.3 25.3 all-gather.1
where the time goes:
time: 175 us
  blocking collectives  74.8 us (43%)
  waiting for transfers between devices  46.8 us (27%)
  local copies, waits for them, and re-layouts  15.6 us (9%)
  between operations  13.5 us (8%)
  matrix products  12.2 us (7%)
  other arithmetic  8.05 us (5%)
  starting transfers between devices  3.77 us (2%)
    all_to_all x1, blocking collectives, local(): lax.all_to_all(outgoing, 'vir', split_axis=3, concat_axis=2, tiled=True)  74.8 us
    all_to_all x1, waiting for transfers between devices, local(): lax.all_to_all(halfway, 'occ', split_axis=1, concat_axis=0, tiled=True)  27.2 us
    all_gather x1, waiting for transfers between devices, local(): full_w = lax.all_gather(masked_w, 'vir', axis=0, tiled=True)  19.6 us
    all_to_all x3, local copies, waits for them, and re-layouts, local(): lax.all_to_all(outgoing, 'vir', split_axis=3, concat_axis=2, tiled=True)  8.89 us
    dot_general x1, matrix products, local(): ladder = jnp.dot(flat_amps, full_w, preferred_element_type=jnp.float32)  8.47 us
    convert_element_type x1, local copies, waits for them, and re-layouts, local(): outgoing = mixed.astype(jnp.bfloat16)  3.96 us
    all_to_all x1, starting transfers between devices, local(): lax.all_to_all(halfway, 'occ', split_axis=1, concat_axis=0, tiled=True)  3.77 us
    dot_general x1, matrix products, local(): jnp.einsum('ikab,kj->ijab', masked, occ_fock, preferred_element_type=jnp....  3.68 us
  transfers between devices with their start and end apart: 2, of which 2 were waited for; matrix products, arithmetic and copies ran while one was open for 4% of the time, Pallas kernels for 0%

commit v1 on v0

v1 whole, which is shorter than its diff:
```python
import functools

import jax
import jax.numpy as jnp
from jax import lax
from jax.experimental import pallas as pl
from jax.experimental.pallas import tpu as pltpu
from jax.sharding import PartitionSpec as P

CORES = 2
LIMIT = 40 * 1024 * 1024


def expand_rows(mask, first_block, blocks, block):
    rows_here = lax.dynamic_slice_in_dim(mask, first_block, blocks, 0)
    return jnp.repeat(jnp.repeat(rows_here, block, axis=0), block, axis=1).astype(jnp.bfloat16)


def plain(amplitudes, integrals, occ_fock, amp_mask, int_mask, occ_energy, vir_energy):
    occ_rows, occ_all, vir_rows, vir_all = amplitudes.shape
    block = vir_all // amp_mask.shape[0]
    vir_start = lax.axis_index("vir") * vir_rows
    occ_start = lax.axis_index("occ") * occ_rows
    blocks = vir_rows // block
    first_block = vir_start // block
    masked = amplitudes * expand_rows(amp_mask, first_block, blocks, block)[None, None]
    masked_w = integrals * expand_rows(int_mask, first_block, blocks, block)
    flat_amps = masked.reshape(-1, vir_all)
    full_w = lax.all_gather(masked_w, "vir", axis=0, tiled=True)
    ladder = jnp.dot(flat_amps, full_w, preferred_element_type=jnp.float32)
    ladder = ladder.reshape(occ_rows, occ_all, vir_rows, vir_all)
    holes = jnp.einsum("ikab,kj->ijab", masked, occ_fock, preferred_element_type=jnp.float32)
    mixed = ladder + holes
    outgoing = mixed.astype(jnp.bfloat16)
    halfway = lax.all_to_all(outgoing, "vir", split_axis=3, concat_axis=2, tiled=True)
    arrived = lax.all_to_all(halfway, "occ", split_axis=1, concat_axis=0, tiled=True)
    mirrored = arrived.transpose(1, 0, 3, 2).astype(jnp.float32)
    vir_here = lax.dynamic_slice_in_dim(vir_energy, vir_start, vir_rows, 0)
    occ_here = lax.dynamic_slice_in_dim(occ_energy, occ_start, occ_rows, 0)
    denominator = (
        vir_here[None, None, :, None]
        + vir_energy[None, None, None, :]
        - occ_here[:, None, None, None]
        - occ_energy[None, :, None, None]
    )
    return (mixed + mirrored) / denominator


def one_hot(shape, row_of, column_of):
    rows = lax.broadcasted_iota(jnp.int32, shape, 0)
    columns = lax.broadcasted_iota(jnp.int32, shape, 1)
    return (row_of(rows) == column_of(columns)).astype(jnp.float32).astype(jnp.bfloat16)


def mask_kernel(block, meta, amp_mask, int_mask, amp_out, int_out):
    blocks, width = amp_mask.shape[0], int_out.shape[1]
    chip_rows = amp_out.shape[0]
    first = meta[1] * chip_rows
    spread = one_hot((blocks, width), lambda r: r, lambda c: c // block)
    mine = one_hot((chip_rows, blocks), lambda r: (r + first) // block, lambda c: c)
    every = one_hot((width, blocks), lambda r: r // block, lambda c: c)

    def wide(rows, mask):
        tall = jnp.dot(rows, mask[...].astype(jnp.float32).astype(jnp.bfloat16), preferred_element_type=jnp.float32)
        return jnp.dot(tall.astype(jnp.bfloat16), spread, preferred_element_type=jnp.float32).astype(jnp.bfloat16)

    amp_out[...] = wide(mine, amp_mask)
    int_out[...] = wide(every, int_mask)


def gather_kernel(meta, own, near, middle, far, sibling, mask, out):
    rows = own.shape[0]
    z, core = meta[1], meta[2]
    for k, piece in enumerate((own, near, middle, far)):
        for part, at in ((piece[...], core), (sibling[k], 1 - core)):
            start = pl.multiple_of(((z ^ k) * CORES + at) * rows, rows)
            out[pl.ds(start, rows), :] = part * mask[pl.ds(start, rows), :]


def dressing(amps, fock, first_j, i, put):
    occ_rows, occ_all, rows, _ = amps.shape

    def step(s, carry):
        row = pl.multiple_of(s * 16, 16)
        pieces = [amps[i, k, pl.ds(row, 16), :].astype(jnp.float32) for k in range(occ_all)]
        for jj in range(occ_rows):
            total = pieces[0] * fock[0, first_j + jj]
            for k in range(1, occ_all):
                total = total + pieces[k] * fock[k, first_j + jj]
            put(jj, row, total)
        return carry

    lax.fori_loop(0, rows // 16, step, 0)


def send_kernel(meta, fock, own_x, sib_x, own_h, sib_h, w, amp_mask, mask_h, out0, out1, x, h, flipped):
    occ_rows, _, rows, width = own_x.shape
    z, core, first_j = meta[1], meta[2], meta[3] * occ_rows
    for source, holes, at in ((own_x, own_h, core), (sib_x, sib_h, 1 - core)):
        start = pl.multiple_of(at * rows, rows)
        mask = amp_mask[pl.ds(start, rows), :]
        for i in range(occ_rows):
            for jj in range(occ_rows):
                x[i, jj, at] = source[i, jj] * mask

            def put(jj, row, value, i=i, at=at):
                h[i, jj, at, pl.ds(row, 16), :] = value

            dressing(holes, fock, first_j, i, put)
    columns = w.shape[1]
    chip = CORES * rows
    for i in range(occ_rows):
        for jj in range(occ_rows):
            ladder = jnp.dot(x[i, jj].reshape(chip, width), w[...], preferred_element_type=jnp.float32)
            mixed = ladder + h[i, jj].reshape(chip, columns) * mask_h[...].astype(jnp.float32)
            lane = (i * occ_rows + jj) * chip
            flipped[:, lane : lane + chip] = mixed.astype(jnp.bfloat16).T
    for s, out in ((0, out0), (1, out1)):
        start = pl.multiple_of((((z & 1) ^ s) * CORES + core) * rows, rows)
        out[...] = flipped[pl.ds(start, rows), :]


def finish_kernel(meta, fock, occ_energy, own_x, own_h, w_far, w_near, amp_mask, row_energy, all_energy, r0, r1, r2, r3, *rest):
    out, h, arrived = rest[-3:]
    occ_rows, _, rows, width = own_x.shape
    o, z, core, partner = meta[0], meta[1], meta[2], meta[3]
    mask = amp_mask[pl.ds(pl.multiple_of(core * rows, rows), rows), :]
    for k, block in enumerate((r0, r1, r2, r3)):
        arrived[z ^ k] = block[...]
    for i in range(occ_rows):
        def put(jj, row, value, i=i):
            h[i, jj, pl.ds(row, 16), :] = value

        dressing(own_h, fock, partner * occ_rows, i, put)
    x = jnp.concatenate([own_x[i, jj] * mask for i in range(occ_rows) for jj in range(occ_rows)], axis=0)
    half = width // 2
    near_at = z // 2
    chip = CORES * rows
    for side, w in ((0, w_near), (1, w_far)):
        ladder = jnp.dot(x, w[...], preferred_element_type=jnp.float32)
        lanes = pl.ds(pl.multiple_of((near_at ^ side) * half, half), half)
        for i in range(occ_rows):
            for jj in range(occ_rows):
                n = i * occ_rows + jj
                out[i, jj, :, lanes] = ladder[n * rows : (n + 1) * rows]
    for i in range(occ_rows):
        for jj in range(occ_rows):
            lane = (jj * occ_rows + i) * chip
            mirror = jnp.concatenate([arrived[zz, :, lane : lane + chip] for zz in range(width // chip)], axis=1)
            mixed = out[i, jj] + h[i, jj] * mask.astype(jnp.float32)
            below = row_energy[...] + all_energy[...] - occ_energy[o * occ_rows + i] - occ_energy[partner * occ_rows + jj]
            out[i, jj] = (mixed + mirror.astype(jnp.float32)) / below


def whole(shape):
    return pl.BlockSpec(shape, lambda s, meta: (0,) * len(shape))


def paired(occ, vir, amplitudes, integrals, occ_fock, amp_mask, int_mask, occ_energy, vir_energy):
    occ_rows, occ_all, rows, width = amplitudes.shape
    block = width // amp_mask.shape[0]
    chip = CORES * rows
    half = width // 2
    axes = ("occ", "vir")
    o, v = lax.axis_index("occ"), lax.axis_index("vir")
    z, core = v // CORES, v % CORES
    near_at = z // 2
    devices = occ * vir

    def swap(a, k):
        return lax.ppermute(a, axes, [(d, d ^ k) for d in range(devices)])

    def meta(partner=0, side=0):
        return jnp.stack([o, z, core, o ^ partner, near_at ^ side]).astype(jnp.int32)

    params = pltpu.CompilerParams(vmem_limit_bytes=LIMIT)
    smem = pl.BlockSpec(memory_space=pltpu.SMEM)

    def call(kernel, grid_meta, in_specs, out_specs, out_shape, args, scratch=(), aliases={}, flops=0, moved=0):
        return pl.pallas_call(
            kernel,
            grid_spec=pltpu.PrefetchScalarGridSpec(
                num_scalar_prefetch=1, grid=(1,), in_specs=in_specs, out_specs=out_specs, scratch_shapes=list(scratch)
            ),
            out_shape=out_shape,
            input_output_aliases=aliases,
            compiler_params=params,
            cost_estimate=pl.CostEstimate(flops=flops, bytes_accessed=moved, transcendentals=0),
        )(grid_meta, *args)

    bf16, f32 = jnp.bfloat16, jnp.float32
    side_of = [lax.dynamic_slice_in_dim(integrals, (near_at ^ side) * half, half, 1) for side in (0, 1)]
    first = {k: swap(side_of[1 - (k >> 1)], 2 * k) for k in (3, 2, 1)}
    sibling = swap(amplitudes, 1)
    wide_amp, wide_int = call(
        functools.partial(mask_kernel, block),
        meta(),
        [whole(amp_mask.shape), whole(int_mask.shape)],
        [whole((chip, width)), whole((width, width))],
        [jax.ShapeDtypeStruct((chip, width), bf16), jax.ShapeDtypeStruct((width, width), bf16)],
        (amp_mask, int_mask),
    )

    def gathered(own, got, side):
        other = swap(jnp.stack([own, got[1], got[2], got[3]]), 1)
        piece = whole((rows, half))
        return call(
            gather_kernel,
            meta(0, side),
            [piece] * 4 + [whole((4, rows, half)), pl.BlockSpec((width, half), lambda s, m: (0, m[4]))],
            whole((width, half)),
            jax.ShapeDtypeStruct((width, half), bf16),
            (own, got[1], got[2], got[3], other, wide_int),
        )

    fock = occ_fock.astype(f32)

    def tiles(partner, side, w):
        x_spec = pl.BlockSpec((occ_rows, occ_rows, rows, width), lambda s, m: (0, m[3], 0, 0))
        h_spec = pl.BlockSpec((occ_rows, occ_all, rows, half), lambda s, m: (0, 0, 0, m[4]))
        return call(
            send_kernel,
            meta(partner, side),
            [smem, x_spec, x_spec, h_spec, h_spec, whole((width, half)), whole((chip, width)),
             pl.BlockSpec((chip, half), lambda s, m: (0, m[4]))],
            [whole((rows, occ_rows * occ_rows * chip))] * 2,
            [jax.ShapeDtypeStruct((rows, occ_rows * occ_rows * chip), bf16)] * 2,
            (fock, amplitudes, sibling, amplitudes, sibling, w, wide_amp, wide_amp),
            [
                pltpu.VMEM((occ_rows, occ_rows, CORES, rows, width), bf16),
                pltpu.VMEM((occ_rows, occ_rows, CORES, rows, half), f32),
                pltpu.VMEM((half, occ_rows * occ_rows * chip), bf16),
            ],
            flops=2 * occ_rows * occ_rows * chip * width * half,
            moved=8 * 1024 * 1024,
        )

    w_far = gathered(side_of[1], first, 1)
    arrived = {}
    for partner in range(occ):
        t0, t1 = tiles(partner, 1, w_far)
        arrived[partner, 3] = swap(t1, partner * vir + 6)
        arrived[partner, 2] = swap(t0, partner * vir + 4)
    second = {k: swap(side_of[k >> 1], 2 * k) for k in (3, 2, 1)}
    w_near = gathered(side_of[0], second, 0)
    for partner in range(occ):
        t0, t1 = tiles(partner, 0, w_near)
        arrived[partner, 1] = swap(t1, partner * vir + 2)
        arrived[partner, 0] = swap(t0, partner * vir) if partner else t0
    row_energy = lax.dynamic_slice_in_dim(vir_energy, v * rows, rows, 0).reshape(rows, 1)
    all_energy = vir_energy.reshape(1, width)
    out = None
    tile = (rows, occ_rows * occ_rows * chip)
    for partner in range(occ):
        x_spec = pl.BlockSpec((occ_rows, occ_rows, rows, width), lambda s, m: (0, m[3], 0, 0))
        args = [fock, occ_energy, amplitudes, amplitudes, w_far, w_near, wide_amp, row_energy, all_energy]
        specs = [smem, smem, x_spec, whole(amplitudes.shape), whole((width, half)), whole((width, half)),
                 whole((chip, width)), whole((rows, 1)), whole((1, width))]
        args += [arrived[partner, k] for k in range(4)]
        specs += [whole(tile)] * 4
        aliases = {}
        if out is not None:
            aliases = {len(args) + 1: 0}
            args.append(out)
            specs.append(pl.BlockSpec(memory_space=pl.ANY))
        out = call(
            finish_kernel,
            meta(partner),
            specs,
            x_spec,
            jax.ShapeDtypeStruct(amplitudes.shape, f32),
            args,
            [
                pltpu.VMEM((occ_rows, occ_rows, rows, width), f32),
                pltpu.VMEM((4,) + tile, bf16),
            ],
            aliases,
            flops=2 * occ_rows * occ_rows * rows * width * width,
            moved=8 * 1024 * 1024,
        )
    return out


def solution(mesh):
    occ, vir = mesh.shape["occ"], mesh.shape["vir"]

    def local(amplitudes, *others):
        occ_rows, _, rows, width = amplitudes.shape
        fits = (
            occ & (occ - 1) == 0
            and vir == 4 * CORES
            and rows % 16 == 0
            and width % 256 == 0
            and (occ_rows * occ_rows * CORES * rows) % 128 == 0
        )
        if fits:
            return paired(occ, vir, amplitudes, *others)
        return plain(amplitudes, *others)

    in_specs = (P("occ", None, "vir", None), P("vir", None), P(), P(), P(), P(), P())
    out_specs = P("occ", None, "vir", None)
    return jax.shard_map(local, mesh=mesh, in_specs=in_specs, out_specs=out_specs, check_vma=False)
```

time: 175 us -> 120 us (0.69)
  blocking collectives: 74.8 us -> 0 us
  Pallas kernels: 0 us -> 62.8 us
  waiting for transfers between devices: 46.8 us -> 5.57 us
  starting transfers between devices: 3.77 us -> 36.4 us
  between operations: 13.5 us -> 0.16 us
  matrix products: 12.2 us -> 0 us
  other arithmetic: 8.05 us -> 2.24 us
  local copies, waits for them, and re-layouts: 15.6 us -> 11.7 us
    all_to_all x1 -> x0, blocking collectives: 74.8 us -> none  [local(): lax.all_to_all(outgoing, 'vir', split_axis=3, concat_axis=2, tiled=True)]
    pallas_call x0 -> x15, Pallas kernels: none -> 62.8 us  [call(): pl.pallas_call(kernel, grid_spec=pltpu.PrefetchScalarGridSpec(num_scalar_...]
    ppermute x0 -> x24, starting transfers between devices: none -> 36.4 us  [swap(): return lax.ppermute(a, axes, [(d, d ^ k) for d in range(devices)])]
    all_to_all x1 -> x0, waiting for transfers between devices: 27.2 us -> none  [local(): lax.all_to_all(halfway, 'occ', split_axis=1, concat_axis=0, tiled=True)]
    all_gather x1 -> x0, waiting for transfers between devices: 19.6 us -> none  [local(): full_w = lax.all_gather(masked_w, 'vir', axis=0, tiled=True)]
    dot_general x2 -> x0, matrix products: 12.2 us -> none  [the longest x1 8.47 us: local(): ladder = jnp.dot(flat_amps, full_w, preferred_element_type=jnp.float32)]
    all_to_all x4 -> x0, local copies, waits for them, and re-layouts: 9.05 us -> none  [the longest x3 8.89 us: local(): lax.all_to_all(outgoing, 'vir', split_axis=3, concat_axis=2, tiled=True)]
    unnamed x10 -> x44, local copies, waits for them, and re-layouts: 1.49 us -> 9.73 us
  transfers between devices with their start and end apart: 2 -> 24, of which waited for: 2 -> 3; matrix products, arithmetic and copies ran while one was open for 4% -> 4% of each run, Pallas kernels for 0% -> 49%
where the time goes in v1:
time: 120 us; the launch traced here: 119 us
  Pallas kernels  62.8 us (52%)
  starting transfers between devices  36.4 us (30%)
  local copies, waits for them, and re-layouts  11.7 us (10%)
  waiting for transfers between devices  5.57 us (5%)
  other arithmetic  2.24 us (2%)
    pallas_call x15, Pallas kernels, call(): pl.pallas_call(kernel, grid_spec=pltpu.PrefetchScalarGridSpec(num_scalar_...  62.8 us
    ppermute x24, starting transfers between devices, swap(): return lax.ppermute(a, axes, [(d, d ^ k) for d in range(devices)])  36.4 us
    unnamed x44, local copies, waits for them, and re-layouts  9.73 us
    ppermute x24, waiting for transfers between devices, swap(): return lax.ppermute(a, axes, [(d, d ^ k) for d in range(devices)])  5.57 us
  transfers between devices with their start and end apart: 24, of which 3 were waited for; matrix products, arithmetic and copies ran while one was open for 4% of the time, Pallas kernels for 49%

profile of v1, /device:TPU:0, one launch (start us, length us, event | category | flops | bytes accessed | tf_op | source)
XLA Modules:
  0.0 118.9 jit_solution(13926958841569473506)
XLA Ops:
  0.0 0.5 collective-permute-start.8
  0.5 1.2 constant_dynamic-slice_fusion
  1.6 4.6 %collective-permute-start.2 = (bf16[96,384]{1,0:T(8,128)(2,1)S(1)}, bf16[96,384]{1,0:T(8,128)(2,1)S(1)}, u32[]{:S(2)}, u32[]{:S(2)}) collective-permute-start(bf16[96,384]{1,0:T(8,128)(2,1)S(1)} %get-tuple-element.41.own), channel_id=1, source_target_pairs={{0,6},{1,7},{2,4},{3,5},{4,2},{5,3},{6,0},{7,1},{8,14},{9,15},{10,... | collective-permute-start | bytes 221192 | tf_op jit(solution)/shard_map/ppermute | solution.py:171
  6.2 0.6 collective-permute-start
  6.9 1.4 %collective-permute-start.4 = (bf16[96,384]{1,0:T(8,128)(2,1)S(1)}, bf16[96,384]{1,0:T(8,128)(2,1)S(1)}, u32[]{:S(2)}, u32[]{:S(2)}) collective-permute-start(bf16[96,384]{1,0:T(8,128)(2,1)S(1)} %get-tuple-element.41.own), channel_id=1, source_target_pairs={{0,2},{1,3},{2,0},{3,1},{4,6},{5,7},{6,4},{7,5},{8,10},{9,11},{10,... | collective-permute-start | bytes 221192 | tf_op jit(solution)/shard_map/ppermute | solution.py:171
  8.3 1.1 collective-permute-done.2.far
  9.4 3.8 %collective-permute-start.6 = (bf16[96,384]{1,0:T(8,128)(2,1)S(1)}, bf16[96,384]{1,0:T(8,128)(2,1)S(1)}, u32[]{:S(2)}, u32[]{:S(2)}) collective-permute-start(bf16[96,384]{1,0:T(8,128)(2,1)S(1)} %get-tuple-element.42.own), channel_id=1, source_target_pairs={{0,6},{1,7},{2,4},{3,5},{4,2},{5,3},{6,0},{7,1},{8,14},{9,15},{10,... | collective-permute-start | bytes 221192 | tf_op jit(solution)/shard_map/ppermute | solution.py:171
  13.2 0.7 collective-permute-start.5
  13.9 0.8 pad_maximum_fusion
  14.7 0.6 copy-done.16
  15.3 0.5 collective-permute-done.6.far
  15.8 3.9 %collective-permute-done.5.middle = bf16[96,384]{1,0:T(8,128)(2,1)S(1)} collective-permute-done((bf16[96,384]{1,0:T(8,128)(2,1)S(1)}, bf16[96,384]{1,0:T(8,128)(2,1)S(1)}, u32[]{:S(2)}, u32[]{:S(2)}) %collective-permute-start.5) | collective-permute-done | bytes 73760 | tf_op jit(solution)/shard_map/ppermute | solution.py:171
  19.7 0.8 pad_maximum_fusion.1
  20.5 0.1 stack.65.meta
  20.6 0.1 stack.59.meta
  20.7 0.1 stack.77.meta
  20.8 0.1 stack.74.meta
  20.9 0.7 convert_element_type.3.fock
  21.6 0.7 copy-done.18
  22.3 0.7 copy-done.19
  23.0 1.4 %shard_map.73 = (bf16[192,768]{1,0:T(8,128)(2,1)S(1)}, bf16[768,768]{1,0:T(8,128)(2,1)S(1)}) custom-call(s32[5]{0:T(128)S(1)} %stack.65.meta, s32[48,48]{1,0:T(8,128)S(1)} %copy-done.18, s32[48,48]{1,0:T(8,128)S(1)} %copy-done.19), custom_call_target="tpu_custom_call" | custom-call | tf_op jit(solution)/shard_map/pallas_call | solution.py:180
  24.4 0.8 copy-done.6
  25.2 1.0 copy-done.7
  26.2 0.9 copy-done.13
  27.0 0.9 copy-done.15
  27.9 0.9 copy-done.17
  28.8 0.7 shard_map.74.w.w_far
  29.5 5.0 %shard_map.83 = (bf16[96,768]{1,0:T(8,128)(2,1)}, bf16[96,768]{1,0:T(8,128)(2,1)}) custom-call(s32[5]{0:T(128)S(1)} %stack.59.meta, f32[8,8]{1,0:T(8,128)S(1)} %convert_element_type.3.fock, bf16[2,8,96,768]{3,2,1,0:T(8,128)(2,1)S(1)} %copy-done, bf16[2,8,96,768]{3,2,1,0:T(8,128)(2,1)} %collective-permute-done.8.sib_x.sib_h, ...), custom_call_target="tpu_custom_call" | custom-call | flops 452984832 | bytes 8388608 | tf_op jit(solution)/shard_map/pallas_call | solution.py:180
  34.5 0.9 collective-permute-start.22
  35.4 2.1 %collective-permute-start.23 = (bf16[96,768]{1,0:T(8,128)(2,1)}, bf16[96,768]{1,0:T(8,128)(2,1)}, u32[]{:S(2)}, u32[]{:S(2)}) collective-permute-start(bf16[96,768]{1,0:T(8,128)(2,1)} %get-tuple-element.40), channel_id=1, source_target_pairs={{0,6},{1,7},{2,4},{3,5},{4,2},{5,3},{6,0},{7,1},{8,14},{9,15},{10,... | collective-permute-start | bytes 442376 | tf_op jit(solution)/shard_map/ppermute | solution.py:171
  37.5 4.9 %shard_map.81 = (bf16[96,768]{1,0:T(8,128)(2,1)}, bf16[96,768]{1,0:T(8,128)(2,1)}) custom-call(s32[5]{0:T(128)S(1)} %stack.77.meta, f32[8,8]{1,0:T(8,128)S(1)} %convert_element_type.3.fock, bf16[2,8,96,768]{3,2,1,0:T(8,128)(2,1)S(1)} %copy-done, bf16[2,8,96,768]{3,2,1,0:T(8,128)(2,1)} %collective-permute-done.8.sib_x.sib_h, ...), custom_call_target="tpu_custom_call" | custom-call | flops 452984832 | bytes 8388608 | tf_op jit(solution)/shard_map/pallas_call | solution.py:180
  42.4 2.9 %collective-permute-start.19 = (bf16[96,768]{1,0:T(8,128)(2,1)}, bf16[96,768]{1,0:T(8,128)(2,1)}, u32[]{:S(2)}, u32[]{:S(2)}) collective-permute-start(bf16[96,768]{1,0:T(8,128)(2,1)} %get-tuple-element.35), channel_id=1, source_target_pairs={{0,12},{1,13},{2,14},{3,15},{4,8},{5,9},{6,10},{7,11},{8,4},{9,5},... | collective-permute-start | bytes 442376 | tf_op jit(solution)/shard_map/ppermute | solution.py:171
  45.3 0.9 collective-permute-start.20
  46.2 4.9 %shard_map.79 = (bf16[96,768]{1,0:T(8,128)(2,1)}, bf16[96,768]{1,0:T(8,128)(2,1)}) custom-call(s32[5]{0:T(128)S(1)} %stack.74.meta, f32[8,8]{1,0:T(8,128)S(1)} %convert_element_type.3.fock, bf16[2,8,96,768]{3,2,1,0:T(8,128)(2,1)S(1)} %copy-done, bf16[2,8,96,768]{3,2,1,0:T(8,128)(2,1)} %collective-permute-done.8.sib_x.sib_h, ...), custom_call_target="tpu_custom_call" | custom-call | flops 452984832 | bytes 8388608 | tf_op jit(solution)/shard_map/pallas_call | solution.py:180
  51.1 1.9 %collective-permute-start.15 = (bf16[96,768]{1,0:T(8,128)(2,1)}, bf16[96,768]{1,0:T(8,128)(2,1)}, u32[]{:S(2)}, u32[]{:S(2)}) collective-permute-start(bf16[96,768]{1,0:T(8,128)(2,1)} %get-tuple-element.31), channel_id=1, source_target_pairs={{0,20},{1,21},{2,22},{3,23},{4,16},{5,17},{6,18},{7,19},{8,28},{9,... | collective-permute-start | bytes 442376 | tf_op jit(solution)/shard_map/ppermute | solution.py:171
  53.0 0.1 stack.76.meta
  53.1 0.1 stack.73.meta
  53.1 1.3 %copy-done.5 = bf16[768,768]{1,0:T(8,128)(2,1)S(1)} copy-done((bf16[768,768]{1,0:T(8,128)(2,1)S(1)}, bf16[768,768]{1,0:T(8,128)(2,1)}, u32[]{:S(2)}) %copy-start.5) | copy-done | bytes 1179672
  54.4 0.9 copy-done.11
  55.3 1.7 %shard_map.75.w.w_near = bf16[768,384]{1,0:T(8,128)(2,1)S(1)} custom-call(s32[5]{0:T(128)S(1)} %stack.65.meta, bf16[96,384]{1,0:T(8,128)(2,1)S(1)} %get-tuple-element.41.own, bf16[96,384]{1,0:T(8,128)(2,1)S(1)} %collective-permute-done.4.near, bf16[96,384]{1,0:T(8,128)(2,1)S(1)} %copy-done.11, bf16[96,384]{1,0:T(8,128)(2,1)S(1)} %copy-done.9, ...), custom_call_target="tpu_custom_call" | custom-call | tf_op jit(solution)/shard_map/pallas_call | solution.py:180
  57.0 4.9 %shard_map.82 = (bf16[96,768]{1,0:T(8,128)(2,1)S(1)}, bf16[96,768]{1,0:T(8,128)(2,1)}) custom-call(s32[5]{0:T(128)S(1)} %stack.65.meta, f32[8,8]{1,0:T(8,128)S(1)} %convert_element_type.3.fock, bf16[2,8,96,768]{3,2,1,0:T(8,128)(2,1)S(1)} %copy-done, bf16[2,8,96,768]{3,2,1,0:T(8,128)(2,1)} %collective-permute-done.8.sib_x.sib_h, ...), custom_call_target="tpu_custom_call" | custom-call | flops 452984832 | bytes 8388608 | tf_op jit(solution)/shard_map/pallas_call | solution.py:180
  61.9 5.0 %shard_map.80 = (bf16[96,768]{1,0:T(8,128)(2,1)}, bf16[96,768]{1,0:T(8,128)(2,1)}) custom-call(s32[5]{0:T(128)S(1)} %stack.76.meta, f32[8,8]{1,0:T(8,128)S(1)} %convert_element_type.3.fock, bf16[2,8,96,768]{3,2,1,0:T(8,128)(2,1)S(1)} %copy-done, bf16[2,8,96,768]{3,2,1,0:T(8,128)(2,1)} %collective-permute-done.8.sib_x.sib_h, ...), custom_call_target="tpu_custom_call" | custom-call | flops 452984832 | bytes 8388608 | tf_op jit(solution)/shard_map/pallas_call | solution.py:180
  66.9 5.0 %shard_map.78 = (bf16[96,768]{1,0:T(8,128)(2,1)}, bf16[96,768]{1,0:T(8,128)(2,1)}) custom-call(s32[5]{0:T(128)S(1)} %stack.73.meta, f32[8,8]{1,0:T(8,128)S(1)} %convert_element_type.3.fock, bf16[2,8,96,768]{3,2,1,0:T(8,128)(2,1)S(1)} %copy-done, bf16[2,8,96,768]{3,2,1,0:T(8,128)(2,1)} %collective-permute-done.8.sib_x.sib_h, ...), custom_call_target="tpu_custom_call" | custom-call | flops 452984832 | bytes 8388608 | tf_op jit(solution)/shard_map/pallas_call | solution.py:180
  71.9 2.0 %collective-permute-start.16 = (bf16[96,768]{1,0:T(8,128)(2,1)}, bf16[96,768]{1,0:T(8,128)(2,1)}, u32[]{:S(2)}, u32[]{:S(2)}) collective-permute-start(bf16[96,768]{1,0:T(8,128)(2,1)} %get-tuple-element.32), channel_id=1, source_target_pairs={{0,22},{1,23},{2,20},{3,21},{4,18},{5,19},{6,16},{7,17},{8,30},{9,... | collective-permute-start | bytes 442376 | tf_op jit(solution)/shard_map/ppermute | solution.py:171
  73.9 0.6 collective-permute-start.21
  74.5 1.5 %collective-permute-start.17 = (bf16[96,768]{1,0:T(8,128)(2,1)}, bf16[96,768]{1,0:T(8,128)(2,1)}, u32[]{:S(2)}, u32[]{:S(2)}) collective-permute-start(bf16[96,768]{1,0:T(8,128)(2,1)} %get-tuple-element.33), channel_id=1, source_target_pairs={{0,8},{1,9},{2,10},{3,11},{4,12},{5,13},{6,14},{7,15},{8,0},{9,1},... | collective-permute-start | bytes 442376 | tf_op jit(solution)/shard_map/ppermute | solution.py:171
  76.0 1.4 %collective-permute-start.18 = (bf16[96,768]{1,0:T(8,128)(2,1)}, bf16[96,768]{1,0:T(8,128)(2,1)}, u32[]{:S(2)}, u32[]{:S(2)}) collective-permute-start(bf16[96,768]{1,0:T(8,128)(2,1)} %get-tuple-element.34), channel_id=1, source_target_pairs={{0,10},{1,11},{2,8},{3,9},{4,14},{5,15},{6,12},{7,13},{8,2},{9,3},... | collective-permute-start | bytes 442376 | tf_op jit(solution)/shard_map/ppermute | solution.py:171
  77.4 1.5 %collective-permute-start.13 = (bf16[96,768]{1,0:T(8,128)(2,1)}, bf16[96,768]{1,0:T(8,128)(2,1)}, u32[]{:S(2)}, u32[]{:S(2)}) collective-permute-start(bf16[96,768]{1,0:T(8,128)(2,1)} %get-tuple-element.29), channel_id=1, source_target_pairs={{0,16},{1,17},{2,18},{3,19},{4,20},{5,21},{6,22},{7,23},{8,24},{9,... | collective-permute-start | bytes 442376 | tf_op jit(solution)/shard_map/ppermute | solution.py:171
  78.9 0.1 stack.57.meta
  79.0 0.1 stack.71.meta
  79.1 4.9 %shard_map.77 = (bf16[96,768]{1,0:T(8,128)(2,1)}, bf16[96,768]{1,0:T(8,128)(2,1)}) custom-call(s32[5]{0:T(128)S(1)} %stack.71.meta, f32[8,8]{1,0:T(8,128)S(1)} %convert_element_type.3.fock, bf16[2,8,96,768]{3,2,1,0:T(8,128)(2,1)S(1)} %copy-done, bf16[2,8,96,768]{3,2,1,0:T(8,128)(2,1)} %collective-permute-done.8.sib_x.sib_h, ...), custom_call_target="tpu_custom_call" | custom-call | flops 452984832 | bytes 8388608 | tf_op jit(solution)/shard_map/pallas_call | solution.py:180
  84.0 5.1 %shard_map.76 = (bf16[96,768]{1,0:T(8,128)(2,1)}, bf16[96,768]{1,0:T(8,128)(2,1)}) custom-call(s32[5]{0:T(128)S(1)} %stack.57.meta, f32[8,8]{1,0:T(8,128)S(1)} %convert_element_type.3.fock, bf16[2,8,96,768]{3,2,1,0:T(8,128)(2,1)S(1)} %copy-done, bf16[2,8,96,768]{3,2,1,0:T(8,128)(2,1)} %collective-permute-done.8.sib_x.sib_h, ...), custom_call_target="tpu_custom_call" | custom-call | flops 452984832 | bytes 8388608 | tf_op jit(solution)/shard_map/pallas_call | solution.py:180
  89.1 2.8 %collective-permute-start.11 = (bf16[96,768]{1,0:T(8,128)(2,1)}, bf16[96,768]{1,0:T(8,128)(2,1)}, u32[]{:S(2)}, u32[]{:S(2)}) collective-permute-start(bf16[96,768]{1,0:T(8,128)(2,1)} %get-tuple-element.27), channel_id=1, source_target_pairs={{0,28},{1,29},{2,30},{3,31},{4,24},{5,25},{6,26},{7,27},{8,20},{9,... | collective-permute-start | bytes 442376 | tf_op jit(solution)/shard_map/ppermute | solution.py:171
  92.0 1.8 %collective-permute-start.12 = (bf16[96,768]{1,0:T(8,128)(2,1)}, bf16[96,768]{1,0:T(8,128)(2,1)}, u32[]{:S(2)}, u32[]{:S(2)}) collective-permute-start(bf16[96,768]{1,0:T(8,128)(2,1)} %get-tuple-element.28), channel_id=1, source_target_pairs={{0,30},{1,31},{2,28},{3,29},{4,26},{5,27},{6,24},{7,25},{8,22},{9,... | collective-permute-start | bytes 442376 | tf_op jit(solution)/shard_map/ppermute | solution.py:171
  93.8 0.6 collective-permute-start.14
  94.4 2.4 %collective-permute-start.9 = (bf16[96,768]{1,0:T(8,128)(2,1)}, bf16[96,768]{1,0:T(8,128)(2,1)}, u32[]{:S(2)}, u32[]{:S(2)}) collective-permute-start(bf16[96,768]{1,0:T(8,128)(2,1)} %get-tuple-element.25), channel_id=1, source_target_pairs={{0,24},{1,25},{2,26},{3,27},{4,28},{5,29},{6,30},{7,31},{8,16},{9,... | collective-permute-start | bytes 442376 | tf_op jit(solution)/shard_map/ppermute | solution.py:171
  96.8 1.4 %collective-permute-start.10 = (bf16[96,768]{1,0:T(8,128)(2,1)}, bf16[96,768]{1,0:T(8,128)(2,1)}, u32[]{:S(2)}, u32[]{:S(2)}) collective-permute-start(bf16[96,768]{1,0:T(8,128)(2,1)} %get-tuple-element.26), channel_id=1, source_target_pairs={{0,26},{1,27},{2,24},{3,25},{4,30},{5,31},{6,28},{7,29},{8,18},{9,... | collective-permute-start | bytes 442376 | tf_op jit(solution)/shard_map/ppermute | solution.py:171
  98.3 0.1 dynamic-slice_bitcast_fusion
  98.4 0.1 copy.14.row_energy
  98.5 1.1 copy-done.3
  99.5 4.8 %shard_map.84.rest_0_ = f32[2,8,96,768]{3,2,1,0:T(8,128)} custom-call(s32[5]{0:T(128)S(1)} %stack.65.meta, f32[8,8]{1,0:T(8,128)S(1)} %convert_element_type.3.fock, f32[8]{0:T(128)S(1)} %copy-done.20, bf16[2,8,96,768]{3,2,1,0:T(8,128)(2,1)S(1)} %copy-done, bf16[2,8,96,768]{3,2,1,0:T(8,128)(2,1)S(1)} %copy-done, bf16[768,384]{1,0:T(8,128)(2,1)S(1)} %shard_map.74.w.w_far, ...), custom_call_target="tpu_custom_call" | custom-call | flops 452984832 | bytes 8388608 | tf_op jit(solution)/shard_map/pallas_call | solution.py:180
  104.3 4.9 %shard_map.85.rest_0_ = f32[2,8,96,768]{3,2,1,0:T(8,128)} custom-call(s32[5]{0:T(128)S(1)} %stack.76.meta, f32[8,8]{1,0:T(8,128)S(1)} %convert_element_type.3.fock, f32[8]{0:T(128)S(1)} %copy-done.20, bf16[2,8,96,768]{3,2,1,0:T(8,128)(2,1)S(1)} %copy-done, bf16[2,8,96,768]{3,2,1,0:T(8,128)(2,1)S(1)} %copy-done, ...), custom_call_target="tpu_custom_call", output_to_operand_aliasing={{}: (14, {})} | custom-call | flops 452984832 | bytes 8388608 | tf_op jit(solution)/shard_map/pallas_call | solution.py:180
  109.2 4.9 %shard_map.86.rest_0_ = f32[2,8,96,768]{3,2,1,0:T(8,128)} custom-call(s32[5]{0:T(128)S(1)} %stack.73.meta, f32[8,8]{1,0:T(8,128)S(1)} %convert_element_type.3.fock, f32[8]{0:T(128)S(1)} %copy-done.20, bf16[2,8,96,768]{3,2,1,0:T(8,128)(2,1)S(1)} %copy-done, bf16[2,8,96,768]{3,2,1,0:T(8,128)(2,1)S(1)} %copy-done, ...), custom_call_target="tpu_custom_call", output_to_operand_aliasing={{}: (14, {})} | custom-call | flops 452984832 | bytes 8388608 | tf_op jit(solution)/shard_map/pallas_call | solution.py:180
  114.1 4.9 %shard_map.87 = f32[2,8,96,768]{3,2,1,0:T(8,128)} custom-call(s32[5]{0:T(128)S(1)} %stack.57.meta, f32[8,8]{1,0:T(8,128)S(1)} %convert_element_type.3.fock, f32[8]{0:T(128)S(1)} %copy-done.20, bf16[2,8,96,768]{3,2,1,0:T(8,128)(2,1)S(1)} %copy-done, bf16[2,8,96,768]{3,2,1,0:T(8,128)(2,1)S(1)} %copy-done, ...), custom_call_target="tpu_custom_call", output_to_operand_aliasing={{}: (14, {})} | custom-call | flops 452984832 | bytes 8388608 | tf_op jit(solution)/shard_map/pallas_call | solution.py:180
  (58 shorter events, 0.1 us)
Async XLA Ops:
  0.0 29.5 %copy-start = (bf16[2,8,96,768]{3,2,1,0:T(8,128)(2,1)S(1)}, bf16[2,8,96,768]{3,2,1,0:T(8,128)(2,1)}, u32[]{:S(2)}) copy-start(bf16[2,8,96,768]{3,2,1,0:T(8,128)(2,1)} %own_h.23) | copy-start | bytes 7077892
  0.0 29.5 %collective-permute-start.8 = (bf16[2,8,96,768]{3,2,1,0:T(8,128)(2,1)}, bf16[2,8,96,768]{3,2,1,0:T(8,128)(2,1)}, u32[]{:S(2)}, u32[]{:S(2)}) collective-permute-start(bf16[2,8,96,768]{3,2,1,0:T(8,128)(2,1)} %own_h.23), channel_id=1, source_target_pairs={{0,1},{1,0},{2,3},{3,2},{4,5},{5,4},{6,7},{7,6},{8,9},{9,8},{10,11... | collective-permute-start | bytes 7077896 | tf_op jit(solution)/shard_map/ppermute | solution.py:171
  1.6 7.8 %collective-permute-start.2 = (bf16[96,384]{1,0:T(8,128)(2,1)S(1)}, bf16[96,384]{1,0:T(8,128)(2,1)S(1)}, u32[]{:S(2)}, u32[]{:S(2)}) collective-permute-start(bf16[96,384]{1,0:T(8,128)(2,1)S(1)} %get-tuple-element.41.own), channel_id=1, source_target_pairs={{0,6},{1,7},{2,4},{3,5},{4,2},{5,3},{6,0},{7,1},{8,14},{9,15},{10,... | collective-permute-start | bytes 221192 | tf_op jit(solution)/shard_map/ppermute | solution.py:171
  6.2 7.0 %collective-permute-start.1 = (bf16[96,384]{1,0:T(8,128)(2,1)S(1)}, bf16[96,384]{1,0:T(8,128)(2,1)S(1)}, u32[]{:S(2)}, u32[]{:S(2)}) collective-permute-start(bf16[96,384]{1,0:T(8,128)(2,1)S(1)} %get-tuple-element.41.own), channel_id=1, source_target_pairs={{0,4},{1,5},{2,6},{3,7},{4,0},{5,1},{6,2},{7,3},{8,12},{9,13},{10,... | collective-permute-start | bytes 221192 | tf_op jit(solution)/shard_map/ppermute | solution.py:171
  6.2 7.7 %collective-permute-start = (bf16[96,384]{1,0:T(8,128)(2,1)S(1)}, bf16[96,384]{1,0:T(8,128)(2,1)S(1)}, u32[]{:S(2)}, u32[]{:S(2)}) collective-permute-start(bf16[96,384]{1,0:T(8,128)(2,1)S(1)} %get-tuple-element.42.own), channel_id=1, source_target_pairs={{0,2},{1,3},{2,0},{3,1},{4,6},{5,7},{6,4},{7,5},{8,10},{9,11},{10,... | collective-permute-start | bytes 221192 | tf_op jit(solution)/shard_map/ppermute | solution.py:171
  6.9 8.5 %collective-permute-start.4 = (bf16[96,384]{1,0:T(8,128)(2,1)S(1)}, bf16[96,384]{1,0:T(8,128)(2,1)S(1)}, u32[]{:S(2)}, u32[]{:S(2)}) collective-permute-start(bf16[96,384]{1,0:T(8,128)(2,1)S(1)} %get-tuple-element.41.own), channel_id=1, source_target_pairs={{0,2},{1,3},{2,0},{3,1},{4,6},{5,7},{6,4},{7,5},{8,10},{9,11},{10,... | collective-permute-start | bytes 221192 | tf_op jit(solution)/shard_map/ppermute | solution.py:171
  9.4 11.4 %copy-start.12 = (bf16[96,384]{1,0:T(8,128)(2,1)}, bf16[96,384]{1,0:T(8,128)(2,1)S(1)}, u32[]{:S(2)}) copy-start(bf16[96,384]{1,0:T(8,128)(2,1)S(1)} %collective-permute-done.2.far) | copy-start | bytes 221188
  9.4 6.4 %collective-permute-start.6 = (bf16[96,384]{1,0:T(8,128)(2,1)S(1)}, bf16[96,384]{1,0:T(8,128)(2,1)S(1)}, u32[]{:S(2)}, u32[]{:S(2)}) collective-permute-start(bf16[96,384]{1,0:T(8,128)(2,1)S(1)} %get-tuple-element.42.own), channel_id=1, source_target_pairs={{0,6},{1,7},{2,4},{3,5},{4,2},{5,3},{6,0},{7,1},{8,14},{9,15},{10,... | collective-permute-start | bytes 221192 | tf_op jit(solution)/shard_map/ppermute | solution.py:171
  13.2 7.6 %copy-start.14 = (bf16[96,384]{1,0:T(8,128)(2,1)}, bf16[96,384]{1,0:T(8,128)(2,1)S(1)}, u32[]{:S(2)}) copy-start(bf16[96,384]{1,0:T(8,128)(2,1)S(1)} %collective-permute-done.1.middle) | copy-start | bytes 221188
  13.2 6.5 %collective-permute-start.5 = (bf16[96,384]{1,0:T(8,128)(2,1)S(1)}, bf16[96,384]{1,0:T(8,128)(2,1)S(1)}, u32[]{:S(2)}, u32[]{:S(2)}) collective-permute-start(bf16[96,384]{1,0:T(8,128)(2,1)S(1)} %get-tuple-element.42.own), channel_id=1, source_target_pairs={{0,4},{1,5},{2,6},{3,7},{4,0},{5,1},{6,2},{7,3},{8,12},{9,13},{10,... | collective-permute-start | bytes 221192 | tf_op jit(solution)/shard_map/ppermute | solution.py:171
  14.7 0.6 copy-start.16
  15.3 9.1 %collective-permute-start.3 = (bf16[4,96,384]{2,1,0:T(8,128)(2,1)}, bf16[4,96,384]{2,1,0:T(8,128)(2,1)S(1)}, u32[]{:S(2)}, u32[]{:S(2)}) collective-permute-start(bf16[4,96,384]{2,1,0:T(8,128)(2,1)} %pad_maximum_fusion), channel_id=1, source_target_pairs={{0,1},{1,0},{2,3},{3,2},{4,5},{5,4},{6,7},{7,6},{8,9},{9,8},{10,11... | collective-permute-start | bytes 884744 | tf_op jit(solution)/shard_map/ppermute | solution.py:171
  15.8 5.0 %copy-start.8 = (bf16[96,384]{1,0:T(8,128)(2,1)}, bf16[96,384]{1,0:T(8,128)(2,1)S(1)}, u32[]{:S(2)}) copy-start(bf16[96,384]{1,0:T(8,128)(2,1)S(1)} %collective-permute-done.6.far) | copy-start | bytes 221188
  19.7 1.1 copy-start.10
  20.5 30.6 %collective-permute-start.7 = (bf16[4,96,384]{2,1,0:T(8,128)(2,1)}, bf16[4,96,384]{2,1,0:T(8,128)(2,1)}, u32[]{:S(2)}, u32[]{:S(2)}) collective-permute-start(bf16[4,96,384]{2,1,0:T(8,128)(2,1)} %pad_maximum_fusion.1), channel_id=1, source_target_pairs={{0,1},{1,0},{2,3},{3,2},{4,5},{5,4},{6,7},{7,6},{8,9},{9,8},{10,11... | collective-permute-start | bytes 884744 | tf_op jit(solution)/shard_map/ppermute | solution.py:171
  21.5 0.7 copy-start.18
  22.3 0.7 copy-start.19
  24.4 10.1 %copy-start.4 = (bf16[768,768]{1,0:T(8,128)(2,1)}, bf16[768,768]{1,0:T(8,128)(2,1)S(1)}, u32[]{:S(2)}) copy-start(bf16[768,768]{1,0:T(8,128)(2,1)S(1)} %get-tuple-element.23.mask) | copy-start | bytes 3538948
  24.4 0.8 copy-start.6
  25.2 1.0 copy-start.7
  26.1 0.9 copy-start.13
  27.0 0.9 copy-start.15
  27.9 0.9 copy-start.17
  34.5 37.4 %collective-permute-start.22 = (bf16[96,768]{1,0:T(8,128)(2,1)}, bf16[96,768]{1,0:T(8,128)(2,1)}, u32[]{:S(2)}, u32[]{:S(2)}) collective-permute-start(bf16[96,768]{1,0:T(8,128)(2,1)} %get-tuple-element.39), channel_id=1, source_target_pairs={{0,4},{1,5},{2,6},{3,7},{4,0},{5,1},{6,2},{7,3},{8,12},{9,13},{10,... | collective-permute-start | bytes 442376 | tf_op jit(solution)/shard_map/ppermute | solution.py:171
  35.4 38.5 %collective-permute-start.23 = (bf16[96,768]{1,0:T(8,128)(2,1)}, bf16[96,768]{1,0:T(8,128)(2,1)}, u32[]{:S(2)}, u32[]{:S(2)}) collective-permute-start(bf16[96,768]{1,0:T(8,128)(2,1)} %get-tuple-element.40), channel_id=1, source_target_pairs={{0,6},{1,7},{2,4},{3,5},{4,2},{5,3},{6,0},{7,1},{8,14},{9,15},{10,... | collective-permute-start | bytes 442376 | tf_op jit(solution)/shard_map/ppermute | solution.py:171
  42.4 32.1 %collective-permute-start.19 = (bf16[96,768]{1,0:T(8,128)(2,1)}, bf16[96,768]{1,0:T(8,128)(2,1)}, u32[]{:S(2)}, u32[]{:S(2)}) collective-permute-start(bf16[96,768]{1,0:T(8,128)(2,1)} %get-tuple-element.35), channel_id=1, source_target_pairs={{0,12},{1,13},{2,14},{3,15},{4,8},{5,9},{6,10},{7,11},{8,4},{9,5},... | collective-permute-start | bytes 442376 | tf_op jit(solution)/shard_map/ppermute | solution.py:171
  45.3 7.8 %copy-start.9 = (bf16[96,384]{1,0:T(8,128)(2,1)S(1)}, bf16[96,384]{1,0:T(8,128)(2,1)}, u32[]{:S(2)}) copy-start(bf16[96,384]{1,0:T(8,128)(2,1)} %copy-done.8) | copy-start | bytes 221188
  45.3 30.7 %collective-permute-start.20 = (bf16[96,768]{1,0:T(8,128)(2,1)}, bf16[96,768]{1,0:T(8,128)(2,1)}, u32[]{:S(2)}, u32[]{:S(2)}) collective-permute-start(bf16[96,768]{1,0:T(8,128)(2,1)} %get-tuple-element.36), channel_id=1, source_target_pairs={{0,14},{1,15},{2,12},{3,13},{4,10},{5,11},{6,8},{7,9},{8,6},{9,7},... | collective-permute-start | bytes 442376 | tf_op jit(solution)/shard_map/ppermute | solution.py:171
  51.1 26.3 %collective-permute-start.15 = (bf16[96,768]{1,0:T(8,128)(2,1)}, bf16[96,768]{1,0:T(8,128)(2,1)}, u32[]{:S(2)}, u32[]{:S(2)}) collective-permute-start(bf16[96,768]{1,0:T(8,128)(2,1)} %get-tuple-element.31), channel_id=1, source_target_pairs={{0,20},{1,21},{2,22},{3,23},{4,16},{5,17},{6,18},{7,19},{8,28},{9,... | collective-permute-start | bytes 442376 | tf_op jit(solution)/shard_map/ppermute | solution.py:171
  53.1 1.3 %copy-start.5 = (bf16[768,768]{1,0:T(8,128)(2,1)S(1)}, bf16[768,768]{1,0:T(8,128)(2,1)}, u32[]{:S(2)}) copy-start(bf16[768,768]{1,0:T(8,128)(2,1)} %copy-done.4) | copy-start | bytes 3538948
  54.4 0.9 copy-start.11
  57.0 9.9 %copy-start.1 = (bf16[768,384]{1,0:T(8,128)(2,1)}, bf16[768,384]{1,0:T(8,128)(2,1)S(1)}, u32[]{:S(2)}) copy-start(bf16[768,384]{1,0:T(8,128)(2,1)S(1)} %shard_map.75.w.w_near) | copy-start | bytes 1769476
  71.9 17.3 %collective-permute-start.16 = (bf16[96,768]{1,0:T(8,128)(2,1)}, bf16[96,768]{1,0:T(8,128)(2,1)}, u32[]{:S(2)}, u32[]{:S(2)}) collective-permute-start(bf16[96,768]{1,0:T(8,128)(2,1)} %get-tuple-element.32), channel_id=1, source_target_pairs={{0,22},{1,23},{2,20},{3,21},{4,18},{5,19},{6,16},{7,17},{8,30},{9,... | collective-permute-start | bytes 442376 | tf_op jit(solution)/shard_map/ppermute | solution.py:171
  73.9 18.1 %collective-permute-start.21 = (bf16[96,768]{1,0:T(8,128)(2,1)}, bf16[96,768]{1,0:T(8,128)(2,1)}, u32[]{:S(2)}, u32[]{:S(2)}) collective-permute-start(bf16[96,768]{1,0:T(8,128)(2,1)} %get-tuple-element.38), channel_id=1, source_target_pairs={{0,2},{1,3},{2,0},{3,1},{4,6},{5,7},{6,4},{7,5},{8,10},{9,11},{10,... | collective-permute-start | bytes 442376 | tf_op jit(solution)/shard_map/ppermute | solution.py:171
  74.5 19.3 %collective-permute-start.17 = (bf16[96,768]{1,0:T(8,128)(2,1)}, bf16[96,768]{1,0:T(8,128)(2,1)}, u32[]{:S(2)}, u32[]{:S(2)}) collective-permute-start(bf16[96,768]{1,0:T(8,128)(2,1)} %get-tuple-element.33), channel_id=1, source_target_pairs={{0,8},{1,9},{2,10},{3,11},{4,12},{5,13},{6,14},{7,15},{8,0},{9,1},... | collective-permute-start | bytes 442376 | tf_op jit(solution)/shard_map/ppermute | solution.py:171
  76.0 18.4 %collective-permute-start.18 = (bf16[96,768]{1,0:T(8,128)(2,1)}, bf16[96,768]{1,0:T(8,128)(2,1)}, u32[]{:S(2)}, u32[]{:S(2)}) collective-permute-start(bf16[96,768]{1,0:T(8,128)(2,1)} %get-tuple-element.34), channel_id=1, source_target_pairs={{0,10},{1,11},{2,8},{3,9},{4,14},{5,15},{6,12},{7,13},{8,2},{9,3},... | collective-permute-start | bytes 442376 | tf_op jit(solution)/shard_map/ppermute | solution.py:171
  77.4 19.4 %collective-permute-start.13 = (bf16[96,768]{1,0:T(8,128)(2,1)}, bf16[96,768]{1,0:T(8,128)(2,1)}, u32[]{:S(2)}, u32[]{:S(2)}) collective-permute-start(bf16[96,768]{1,0:T(8,128)(2,1)} %get-tuple-element.29), channel_id=1, source_target_pairs={{0,16},{1,17},{2,18},{3,19},{4,20},{5,21},{6,22},{7,23},{8,24},{9,... | collective-permute-start | bytes 442376 | tf_op jit(solution)/shard_map/ppermute | solution.py:171
  79.1 4.9 %copy-start.2 = (bf16[768,384]{1,0:T(8,128)(2,1)S(1)}, bf16[768,384]{1,0:T(8,128)(2,1)}, u32[]{:S(2)}) copy-start(bf16[768,384]{1,0:T(8,128)(2,1)} %copy-done.1) | copy-start | bytes 1769476
  84.0 14.3 %copy-start.21 = (f32[768]{0:T(1024)S(1)}, f32[768]{0:T(1024)}, u32[]{:S(2)}) copy-start(f32[768]{0:T(1024)} %param.13) | copy-start | bytes 9220
  84.0 14.4 %copy-start.20 = (f32[8]{0:T(128)S(1)}, f32[8]{0:T(128)}, u32[]{:S(2)}) copy-start(f32[8]{0:T(128)} %occ_energy.7) | copy-start | bytes 100
  89.1 24.9 %collective-permute-start.11 = (bf16[96,768]{1,0:T(8,128)(2,1)}, bf16[96,768]{1,0:T(8,128)(2,1)}, u32[]{:S(2)}, u32[]{:S(2)}) collective-permute-start(bf16[96,768]{1,0:T(8,128)(2,1)} %get-tuple-element.27), channel_id=1, source_target_pairs={{0,28},{1,29},{2,30},{3,31},{4,24},{5,25},{6,26},{7,27},{8,20},{9,... | collective-permute-start | bytes 442376 | tf_op jit(solution)/shard_map/ppermute | solution.py:171
  92.0 22.1 %collective-permute-start.12 = (bf16[96,768]{1,0:T(8,128)(2,1)}, bf16[96,768]{1,0:T(8,128)(2,1)}, u32[]{:S(2)}, u32[]{:S(2)}) collective-permute-start(bf16[96,768]{1,0:T(8,128)(2,1)} %get-tuple-element.28), channel_id=1, source_target_pairs={{0,30},{1,31},{2,28},{3,29},{4,26},{5,27},{6,24},{7,25},{8,22},{9,... | collective-permute-start | bytes 442376 | tf_op jit(solution)/shard_map/ppermute | solution.py:171
  93.8 15.4 %collective-permute-start.14 = (bf16[96,768]{1,0:T(8,128)(2,1)}, bf16[96,768]{1,0:T(8,128)(2,1)}, u32[]{:S(2)}, u32[]{:S(2)}) collective-permute-start(bf16[96,768]{1,0:T(8,128)(2,1)} %get-tuple-element.30), channel_id=1, source_target_pairs={{0,18},{1,19},{2,16},{3,17},{4,22},{5,23},{6,20},{7,21},{8,26},{9,... | collective-permute-start | bytes 442376 | tf_op jit(solution)/shard_map/ppermute | solution.py:171
  94.4 19.6 %collective-permute-start.9 = (bf16[96,768]{1,0:T(8,128)(2,1)}, bf16[96,768]{1,0:T(8,128)(2,1)}, u32[]{:S(2)}, u32[]{:S(2)}) collective-permute-start(bf16[96,768]{1,0:T(8,128)(2,1)} %get-tuple-element.25), channel_id=1, source_target_pairs={{0,24},{1,25},{2,26},{3,27},{4,28},{5,29},{6,30},{7,31},{8,16},{9,... | collective-permute-start | bytes 442376 | tf_op jit(solution)/shard_map/ppermute | solution.py:171
  96.8 17.2 %collective-permute-start.10 = (bf16[96,768]{1,0:T(8,128)(2,1)}, bf16[96,768]{1,0:T(8,128)(2,1)}, u32[]{:S(2)}, u32[]{:S(2)}) collective-permute-start(bf16[96,768]{1,0:T(8,128)(2,1)} %get-tuple-element.26), channel_id=1, source_target_pairs={{0,26},{1,27},{2,24},{3,25},{4,30},{5,31},{6,28},{7,29},{8,18},{9,... | collective-permute-start | bytes 442376 | tf_op jit(solution)/shard_map/ppermute | solution.py:171
  98.5 1.1 copy-start.3

commit v2 on v0

--- a/solution.py
+++ b/solution.py
@@ -1,24 +1,32 @@
+import functools
+
 import jax
 import jax.numpy as jnp
 from jax import lax
+from jax.experimental import pallas as pl
+from jax.experimental.pallas import tpu as pltpu
 from jax.sharding import PartitionSpec as P
 
-VB = 16
-
-
-def expand_rows(mask, first_block, blocks):
+CORES = 2
+LIMIT = 20 * 1024 * 1024
+VMEM = pl.BlockSpec(memory_space=pltpu.VMEM)
+SMEM = pl.BlockSpec(memory_space=pltpu.SMEM)
+
+
+def expand_rows(mask, first_block, blocks, block):
     rows_here = lax.dynamic_slice_in_dim(mask, first_block, blocks, 0)
-    return jnp.repeat(jnp.repeat(rows_here, VB, axis=0), VB, axis=1).astype(jnp.bfloat16)
-
-
-def local(amplitudes, integrals, occ_fock, amp_mask, int_mask, occ_energy, vir_energy):
+    return jnp.repeat(jnp.repeat(rows_here, block, axis=0), block, axis=1).astype(jnp.bfloat16)
+
+
+def plain(amplitudes, integrals, occ_fock, amp_mask, int_mask, occ_energy, vir_energy):
     occ_rows, occ_all, vir_rows, vir_all = amplitudes.shape
+    block = vir_all // amp_mask.shape[0]
     vir_start = lax.axis_index("vir") * vir_rows
     occ_start = lax.axis_index("occ") * occ_rows
-    blocks = vir_rows // VB
-    first_block = vir_start // VB
-    masked = amplitudes * expand_rows(amp_mask, first_block, blocks)[None, None]
-    masked_w = integrals * expand_rows(int_mask, first_block, blocks)
+    blocks = vir_rows // block
+    first_block = vir_start // block
+    masked = amplitudes * expand_rows(amp_mask, first_block, blocks, block)[None, None]
+    masked_w = integrals * expand_rows(int_mask, first_block, blocks, block)
     flat_amps = masked.reshape(-1, vir_all)
     full_w = lax.all_gather(masked_w, "vir", axis=0, tiled=True)
     ladder = jnp.dot(flat_amps, full_w, preferred_element_type=jnp.float32)
@@ -40,7 +48,234 @@
     return (mixed + mirrored) / denominator
 
 
+def one_hot(shape, row_of, column_of):
+    rows = lax.broadcasted_iota(jnp.int32, shape, 0)
+    columns = lax.broadcasted_iota(jnp.int32, shape, 1)
+    return (row_of(rows) == column_of(columns)).astype(jnp.float32).astype(jnp.bfloat16)
+
+
+def mask_kernel(block, meta, amp_mask, int_mask, amp_out, int_out):
+    blocks, width = amp_mask.shape[0], int_out.shape[1]
+    chip_rows = amp_out.shape[0]
+    first = meta[1] * chip_rows
+    spread = one_hot((blocks, width), lambda r: r, lambda c: c // block)
+    mine = one_hot((chip_rows, blocks), lambda r: (r + first) // block, lambda c: c)
+    every = one_hot((width, blocks), lambda r: r // block, lambda c: c)
+
+    def wide(rows, mask):
+        tall = jnp.dot(rows, mask[...].astype(jnp.float32).astype(jnp.bfloat16), preferred_element_type=jnp.float32)
+        return jnp.dot(tall.astype(jnp.bfloat16), spread, preferred_element_type=jnp.float32).astype(jnp.bfloat16)
+
+    amp_out[...] = wide(mine, amp_mask)
+    int_out[...] = wide(every, int_mask)
+
+
+def send_kernel(partner, side, first, carried, *refs):
+    meta, fock, own, sib, amp_mask = refs[:5]
+    if first:
+        pieces, siblings, int_mask, passed = refs[5:9], refs[9:13], refs[13], refs[14 : 14 + carried]
+        outs = refs[14 + carried :]
+    else:
+        w = refs[5]
+        outs = refs[7:]
+    out0, out1, mixed_out, token = outs[:4]
+    x, h, flipped = outs[-3:]
+    occ_rows, occ_all, rows, width = own.shape
+    half, chip = width // 2, CORES * rows
+    o, z, core = meta[0], meta[1], meta[2]
+    first_j = (o ^ partner) * occ_rows
+    columns = pl.ds(pl.multiple_of(((z // 2) ^ side) * half, half), half)
+    if first:
+        w = outs[4]
+        for k in range(4):
+            for piece, at in ((pieces[k], core), (siblings[k], 1 - core)):
+                start = pl.multiple_of(((z ^ k) * CORES + at) * rows, rows)
+                w[pl.ds(start, rows), :] = piece[...] * int_mask[pl.ds(start, rows), columns]
+        for source, copy in zip(passed, outs[5 : 5 + carried], strict=True):
+            copy[...] = source[...]
+    for source, at in ((own, core), (sib, 1 - core)):
+        start = pl.multiple_of(at * rows, rows)
+        mask = amp_mask[pl.ds(start, rows), :]
+        for i in range(occ_rows):
+            for jj in range(occ_rows):
+                x[i, jj, at] = source[i, first_j + jj] * mask
+
+        def step(s, carry, source=source, at=at, start=start):
+            row = pl.multiple_of(s * 16, 16)
+            live = amp_mask[pl.ds(pl.multiple_of(start + row, 16), 16), columns].astype(jnp.float32)
+            for i in range(occ_rows):
+                amps = [source[i, k, pl.ds(row, 16), columns].astype(jnp.float32) for k in range(occ_all)]
+                for jj in range(occ_rows):
+                    total = amps[0] * fock[0, first_j + jj]
+                    for k in range(1, occ_all):
+                        total = total + amps[k] * fock[k, first_j + jj]
+                    h[i, jj, at, pl.ds(row, 16), :] = total * live
+            return carry
+
+        lax.fori_loop(0, rows // 16, step, 0)
+    pairs = occ_rows * occ_rows
+    ladder = jnp.dot(x[...].reshape(pairs * chip, width), w[...], preferred_element_type=jnp.float32)
+    for i in range(occ_rows):
+        for jj in range(occ_rows):
+            n = i * occ_rows + jj
+            mixed = ladder[n * chip : (n + 1) * chip] + h[i, jj].reshape(chip, half)
+            h[i, jj] = mixed.reshape(CORES, rows, half)
+            mixed_out[i, jj] = h[i, jj, core]
+            flipped[:, n * chip : (n + 1) * chip] = mixed.astype(jnp.bfloat16).T
+    for s, out in ((0, out0), (1, out1)):
+        start = pl.multiple_of((((z & 1) ^ s) * CORES + core) * rows, rows)
+        out[...] = flipped[pl.ds(start, rows), :]
+    token[...] = jnp.zeros(token.shape, token.dtype)
+
+
+def finish_kernel(partner, *refs):
+    meta, occ_energy, near, far, row_energy, all_energy, r0, r1, r2, r3 = refs[:10]
+    result, tile, sems = refs[-3:]
+    occ_rows, _, rows, half = near.shape
+    chip = CORES * rows
+    o, z = meta[0], meta[1]
+    odd = (z & 1) == 1
+    first_j = (o ^ partner) * occ_rows
+    copies = []
+    for i in range(occ_rows):
+        for side, mixed, same, other in ((0, near, r0, r1), (1, far, r2, r3)):
+            lanes = pl.ds(pl.multiple_of(((z // 2) ^ side) * half, half), half)
+            for jj in range(occ_rows):
+                lane = (jj * occ_rows + i) * chip
+                a, b = same[:, lane : lane + chip], other[:, lane : lane + chip]
+                mirror = jnp.concatenate([jnp.where(odd, b, a), jnp.where(odd, a, b)], axis=1)
+                below = (
+                    row_energy[...] + all_energy[:, lanes] - occ_energy[o * occ_rows + i] - occ_energy[first_j + jj]
+                )
+                tile[i, jj, :, lanes] = (mixed[i, jj] + mirror.astype(jnp.float32)) / below
+        copies.append(pltpu.make_async_copy(tile.at[i], result.at[i, pl.ds(first_j, occ_rows)], sems.at[i]))
+        copies[-1].start()
+    for copy in copies:
+        copy.wait()
+
+
+def in_vmem(a):
+    return pltpu.with_memory_space_constraint(a, pltpu.VMEM)
+
+
+def paired(occ, vir, amplitudes, integrals, occ_fock, amp_mask, int_mask, occ_energy, vir_energy):
+    occ_rows, occ_all, rows, width = amplitudes.shape
+    block = width // amp_mask.shape[0]
+    chip = CORES * rows
+    half = width // 2
+    pairs = occ_rows * occ_rows
+    axes = ("occ", "vir")
+    o, v = lax.axis_index("occ"), lax.axis_index("vir")
+    z, core = v // CORES, v % CORES
+    near_at = z // 2
+    devices = occ * vir
+    bf16, f32 = jnp.bfloat16, jnp.float32
+    params = pltpu.CompilerParams(vmem_limit_bytes=LIMIT)
+    meta = jnp.stack([o, z, core]).astype(jnp.int32)
+    fock = occ_fock.astype(f32)
+
+    def swap(a, k):
+        return lax.ppermute(a, axes, [(d, d ^ k) for d in range(devices)])
+
+    side_of = [lax.dynamic_slice_in_dim(integrals, (near_at ^ side) * half, half, 1) for side in (0, 1)]
+    first = [side_of[1]] + [swap(side_of[1 - (k >> 1)], 2 * k) for k in (1, 2, 3)]
+    sibling = swap(amplitudes, 1)
+    wide_amp, wide_int = pl.pallas_call(
+        functools.partial(mask_kernel, block),
+        in_specs=[SMEM, VMEM, VMEM],
+        out_specs=[VMEM, VMEM],
+        out_shape=[pltpu.VMEM((chip, width), bf16), pltpu.VMEM((width, width), bf16)],
+        compiler_params=params,
+    )(meta, amp_mask, int_mask)
+
+    def tiles(partner, side, w, token, pieces=None, passed=()):
+        args = [meta, fock, in_vmem(amplitudes), in_vmem(sibling), in_vmem(wide_amp)]
+        shapes = [
+            pltpu.VMEM((rows, pairs * chip), bf16),
+            pltpu.VMEM((rows, pairs * chip), bf16),
+            pltpu.VMEM((occ_rows, occ_rows, rows, half), f32),
+            pltpu.VMEM((8, 128), f32),
+        ]
+        if pieces is not None:
+            args += [in_vmem(a) for a in pieces]
+            args += [in_vmem(swap(a, 1)) for a in pieces]
+            args += [in_vmem(wide_int)] + [in_vmem(a) for a in passed]
+            shapes += [pltpu.VMEM((width, half), bf16)] + [pltpu.VMEM(a.shape, a.dtype) for a in passed]
+        else:
+            args += [in_vmem(w), in_vmem(token)]
+        return pl.pallas_call(
+            functools.partial(send_kernel, partner, side, pieces is not None, len(passed)),
+            in_specs=[SMEM, SMEM] + [VMEM] * (len(args) - 2),
+            out_specs=[VMEM] * len(shapes),
+            out_shape=shapes,
+            scratch_shapes=[
+                pltpu.VMEM((occ_rows, occ_rows, CORES, rows, width), bf16),
+                pltpu.VMEM((occ_rows, occ_rows, CORES, rows, half), f32),
+                pltpu.VMEM((half, pairs * chip), bf16),
+            ],
+            compiler_params=params,
+            cost_estimate=pl.CostEstimate(
+                flops=2 * pairs * chip * width * half, bytes_accessed=8 * 1024 * 1024, transcendentals=0
+            ),
+        )(*args)
+
+    arrived, mixed, w = {}, {}, {}
+    token, again = None, None
+    order = [(0, 1), (1, 1), (0, 0), (2, 1), (1, 0), (2, 0), (3, 1), (3, 0)] if occ == 4 else [
+        (partner, side) for side in (1, 0) for partner in range(occ)
+    ]
+    for partner, side in order:
+        if (partner, side) == (0, 1):
+            t0, t1, mixed[partner, side], token, w[side], *again = tiles(partner, side, None, None, first, side_of)
+        elif partner == 0:
+            pieces = [again[0]] + [swap(again[k >> 1], 2 * k) for k in (1, 2, 3)]
+            t0, t1, mixed[partner, side], token, w[side] = tiles(partner, side, None, None, pieces)
+        else:
+            t0, t1, mixed[partner, side], token = tiles(partner, side, w[side], token)
+        k = 2 * side
+        arrived[partner, k + 1] = swap(t1, partner * vir + 2 * (k + 1))
+        arrived[partner, k] = swap(t0, partner * vir + 2 * k) if partner or k else t0
+    row_energy = lax.dynamic_slice_in_dim(vir_energy, v * rows, rows, 0).reshape(rows, 1)
+    all_energy = vir_energy.reshape(1, width)
+    out = None
+    for partner in range(occ):
+        args = [meta, occ_energy, in_vmem(mixed[partner, 0]), in_vmem(mixed[partner, 1]), row_energy, all_energy]
+        args += [in_vmem(arrived[partner, k]) for k in range(4)]
+        specs = [SMEM, SMEM] + [VMEM] * 8
+        aliases = {}
+        if out is not None:
+            aliases = {len(args): 0}
+            args.append(out)
+            specs.append(pl.BlockSpec(memory_space=pl.ANY))
+        out = pl.pallas_call(
+            functools.partial(finish_kernel, partner),
+            in_specs=specs,
+            out_specs=pl.BlockSpec(memory_space=pl.ANY),
+            out_shape=jax.ShapeDtypeStruct(amplitudes.shape, f32),
+            scratch_shapes=[pltpu.VMEM((occ_rows, occ_rows, rows, width), f32), pltpu.SemaphoreType.DMA((occ_rows,))],
+            input_output_aliases=aliases,
+            compiler_params=params,
+            cost_estimate=pl.CostEstimate(flops=0, bytes_accessed=4 * 1024 * 1024, transcendentals=0),
+        )(*args)
+    return out
+
+
 def solution(mesh):
+    occ, vir = mesh.shape["occ"], mesh.shape["vir"]
+
+    def local(amplitudes, *others):
+        occ_rows, _, rows, width = amplitudes.shape
+        fits = (
+            occ & (occ - 1) == 0
+            and vir == 4 * CORES
+            and rows % 16 == 0
+            and width % 256 == 0
+            and (occ_rows * occ_rows * CORES * rows) % 128 == 0
+        )
+        if fits:
+            return paired(occ, vir, amplitudes, *others)
+        return plain(amplitudes, *others)
+
     in_specs = (P("occ", None, "vir", None), P("vir", None), P(), P(), P(), P(), P())
     out_specs = P("occ", None, "vir", None)
     return jax.shard_map(local, mesh=mesh, in_specs=in_specs, out_specs=out_specs, check_vma=False)

time: 175 us -> 100 us (0.57)
  blocking collectives: 74.8 us -> 0 us
  waiting for transfers between devices: 46.8 us -> 10.6 us
  Pallas kernels: 0 us -> 35.3 us
  starting transfers between devices: 3.77 us -> 35.9 us
  between operations: 13.5 us -> 0.62 us
  matrix products: 12.2 us -> 0 us
  other arithmetic: 8.05 us -> 0.76 us
    all_to_all x1 -> x0, blocking collectives: 74.8 us -> none  [local(): lax.all_to_all(outgoing, 'vir', split_axis=3, concat_axis=2, tiled=True)]
    ppermute x0 -> x30, starting transfers between devices: none -> 35.9 us  [swap(): return lax.ppermute(a, axes, [(d, d ^ k) for d in range(devices)])]
    pallas_call x0 -> x13, Pallas kernels: none -> 35.3 us  [the longest x8 26.6 us: tiles(): pl.pallas_call(functools.partial(send_kernel, partner, side, pieces is no...]
    all_to_all x1 -> x0, waiting for transfers between devices: 27.2 us -> none  [local(): lax.all_to_all(halfway, 'occ', split_axis=1, concat_axis=0, tiled=True)]
    all_gather x1 -> x0, waiting for transfers between devices: 19.6 us -> none  [local(): full_w = lax.all_gather(masked_w, 'vir', axis=0, tiled=True)]
    unnamed x10 -> x80, local copies, waits for them, and re-layouts: 1.49 us -> 15.6 us
    dot_general x2 -> x0, matrix products: 12.2 us -> none  [the longest x1 8.47 us: local(): ladder = jnp.dot(flat_amps, full_w, preferred_element_type=jnp.float32)]
    ppermute x0 -> x30, waiting for transfers between devices: none -> 10.6 us  [swap(): return lax.ppermute(a, axes, [(d, d ^ k) for d in range(devices)])]
  transfers between devices with their start and end apart: 2 -> 30, of which waited for: 2 -> 4; matrix products, arithmetic and copies ran while one was open for 4% -> 2% of each run, Pallas kernels for 0% -> 30%
where the time goes in v2:
time: 100 us; the launch traced here: 99.8 us
  starting transfers between devices  35.9 us (36%)
  Pallas kernels  35.3 us (35%)
  local copies, waits for them, and re-layouts  16.7 us (17%)
  waiting for transfers between devices  10.6 us (11%)
    ppermute x30, starting transfers between devices, swap(): return lax.ppermute(a, axes, [(d, d ^ k) for d in range(devices)])  35.9 us
    pallas_call x8, Pallas kernels, tiles(): pl.pallas_call(functools.partial(send_kernel, partner, side, pieces is no...  26.6 us
    unnamed x80, local copies, waits for them, and re-layouts  15.6 us
    ppermute x30, waiting for transfers between devices, swap(): return lax.ppermute(a, axes, [(d, d ^ k) for d in range(devices)])  10.6 us
    pallas_call x4, Pallas kernels, paired(): pl.pallas_call(functools.partial(finish_kernel, partner), in_specs=specs,...  7.31 us
  transfers between devices with their start and end apart: 30, of which 4 were waited for; matrix products, arithmetic and copies ran while one was open for 2% of the time, Pallas kernels for 30%

profile of v2, /device:TPU:0, one launch (start us, length us, event | category | flops | bytes accessed | tf_op | source)
XLA Modules:
  0.0 99.8 jit_solution(12027745280053005261)
XLA Ops:
  0.0 0.5 collective-permute-start
  0.5 0.9 constant_dynamic-slice_fusion
  1.4 4.7 %collective-permute-start.3 = (bf16[96,384]{1,0:T(8,128)(2,1)S(1)}, bf16[96,384]{1,0:T(8,128)(2,1)S(1)}, u32[]{:S(2)}, u32[]{:S(2)}) collective-permute-start(bf16[96,384]{1,0:T(8,128)(2,1)S(1)} %get-tuple-element.77.refs_14_), channel_id=1, source_target_pairs={{0,6},{1,7},{2,4},{3,5},{4,2},{5,3},{6,0},{7,1},{8,14},{9,15},{10,... | collective-permute-start | bytes 221192 | tf_op jit(solution)/shard_map/ppermute | solution.py:178
  6.1 0.6 collective-permute-start.1
  6.7 0.7 convert_element_type.3.refs_1_
  7.4 1.9 %collective-permute-done.3.refs_8_ = bf16[96,384]{1,0:T(8,128)(2,1)S(1)} collective-permute-done((bf16[96,384]{1,0:T(8,128)(2,1)S(1)}, bf16[96,384]{1,0:T(8,128)(2,1)S(1)}, u32[]{:S(2)}, u32[]{:S(2)}) %collective-permute-start.3) | collective-permute-done | bytes 73760 | tf_op jit(solution)/shard_map/ppermute | solution.py:178
  9.3 3.6 %collective-permute-done.2.refs_7_ = bf16[96,384]{1,0:T(8,128)(2,1)S(1)} collective-permute-done((bf16[96,384]{1,0:T(8,128)(2,1)S(1)}, bf16[96,384]{1,0:T(8,128)(2,1)S(1)}, u32[]{:S(2)}, u32[]{:S(2)}) %collective-permute-start.2) | collective-permute-done | bytes 73760 | tf_op jit(solution)/shard_map/ppermute | solution.py:178
  12.9 0.5 collective-permute-start.5
  13.4 0.1 pad_add_fusion.meta.refs_0_
  13.5 0.7 copy-done.36
  14.2 0.7 copy-done.37
  15.0 1.4 %shard_map.73 = (bf16[192,768]{1,0:T(8,128)(2,1)S(1)}, bf16[768,768]{1,0:T(8,128)(2,1)S(1)}) custom-call(s32[3]{0:T(128)S(1)} %pad_add_fusion.meta.refs_0_, s32[48,48]{1,0:T(8,128)S(1)} %copy-done.36, s32[48,48]{1,0:T(8,128)S(1)} %copy-done.37), custom_call_target="tpu_custom_call" | custom-call | tf_op jit(solution)/shard_map/pallas_call | solution.py:183
  16.4 0.0 copy-start
  16.4 1.7 %copy-done = bf16[2,8,96,768]{3,2,1,0:T(8,128)(2,1)S(1)} copy-done((bf16[2,8,96,768]{3,2,1,0:T(8,128)(2,1)S(1)}, bf16[2,8,96,768]{3,2,1,0:T(8,128)(2,1)}, u32[]{:S(2)}) %copy-start) | copy-done | bytes 2359320
  18.1 3.1 %shard_map.74 = (bf16[96,768]{1,0:T(8,128)(2,1)S(1)}, bf16[96,768]{1,0:T(8,128)(2,1)S(1)}, f32[2,2,96,384]{3,2,1,0:T(8,128)S(1)}, f32[8,128]{1,0:T(8,128)S(1)}, ...) custom-call(s32[3]{0:T(128)S(1)} %pad_add_fusion.meta.refs_0_, ...), custom_call_target="tpu_custom_call" | custom-call | flops 452984832 | bytes 8388608 | tf_op jit(solution)/shard_map/pallas_call | solution.py:206
  21.2 2.5 %collective-permute-start.10 = (bf16[96,384]{1,0:T(8,128)(2,1)S(1)}, bf16[96,384]{1,0:T(8,128)(2,1)S(1)}, u32[]{:S(2)}, u32[]{:S(2)}) collective-permute-start(bf16[96,384]{1,0:T(8,128)(2,1)S(1)} %get-tuple-element.44), channel_id=1, source_target_pairs={{0,6},{1,7},{2,4},{3,5},{4,2},{5,3},{6,0},{7,1},{8,14},{9,15},{10,... | collective-permute-start | bytes 221192 | tf_op jit(solution)/shard_map/ppermute | solution.py:178
  23.7 1.9 %collective-permute-start.8 = (bf16[96,384]{1,0:T(8,128)(2,1)S(1)}, bf16[96,384]{1,0:T(8,128)(2,1)S(1)}, u32[]{:S(2)}, u32[]{:S(2)}) collective-permute-start(bf16[96,384]{1,0:T(8,128)(2,1)S(1)} %get-tuple-element.43.refs_5_), channel_id=1, source_target_pairs={{0,2},{1,3},{2,0},{3,1},{4,6},{5,7},{6,4},{7,5},{8,10},{9,11},{10,... | collective-permute-start | bytes 221192 | tf_op jit(solution)/shard_map/ppermute | solution.py:178
  25.6 2.5 %collective-permute-done.10.refs_8_ = bf16[96,384]{1,0:T(8,128)(2,1)S(1)} collective-permute-done((bf16[96,384]{1,0:T(8,128)(2,1)S(1)}, bf16[96,384]{1,0:T(8,128)(2,1)S(1)}, u32[]{:S(2)}, u32[]{:S(2)}) %collective-permute-start.10) | collective-permute-done | bytes 73760 | tf_op jit(solution)/shard_map/ppermute | solution.py:178
  28.1 2.5 %collective-permute-done.9.refs_7_ = bf16[96,384]{1,0:T(8,128)(2,1)S(1)} collective-permute-done((bf16[96,384]{1,0:T(8,128)(2,1)S(1)}, bf16[96,384]{1,0:T(8,128)(2,1)S(1)}, u32[]{:S(2)}, u32[]{:S(2)}) %collective-permute-start.9) | collective-permute-done | bytes 73760 | tf_op jit(solution)/shard_map/ppermute | solution.py:178
  30.6 0.0 collective-permute-start.13
  30.7 0.5 collective-permute-start.12
  31.2 0.6 collective-permute-start.28
  31.7 3.4 %shard_map.81 = (bf16[96,768]{1,0:T(8,128)(2,1)S(1)}, bf16[96,768]{1,0:T(8,128)(2,1)S(1)}, f32[2,2,96,384]{3,2,1,0:T(8,128)S(1)}, f32[8,128]{1,0:T(8,128)}) custom-call(s32[3]{0:T(128)S(1)} %pad_add_fusion.meta.refs_0_, f32[8,8]{1,0:T(8,128)S(1)} %convert_element_type.3.refs_1_, bf16[2,8,96,768]{3,2,1,0:T(8,128)(2,1)S(1)} %copy-done.1, ...), custom_call_target="tpu_custom_call" | custom-call | flops 452984832 | bytes 8388608 | tf_op jit(solution)/shard_map/pallas_call | solution.py:206
  35.1 1.7 %collective-permute-start.29 = (bf16[96,768]{1,0:T(8,128)(2,1)S(1)}, bf16[96,768]{1,0:T(8,128)(2,1)S(1)}, u32[]{:S(2)}, u32[]{:S(2)}) collective-permute-start(bf16[96,768]{1,0:T(8,128)(2,1)S(1)} %get-tuple-element.76), channel_id=1, source_target_pairs={{0,6},{1,7},{2,4},{3,5},{4,2},{5,3},{6,0},{7,1},{8,14},{9,15},{10,... | collective-permute-start | bytes 442376 | tf_op jit(solution)/shard_map/ppermute | solution.py:178
  36.9 2.9 %collective-permute-start.25 = (bf16[96,768]{1,0:T(8,128)(2,1)S(1)}, bf16[96,768]{1,0:T(8,128)(2,1)S(1)}, u32[]{:S(2)}, u32[]{:S(2)}) collective-permute-start(bf16[96,768]{1,0:T(8,128)(2,1)S(1)} %get-tuple-element.69), channel_id=1, source_target_pairs={{0,12},{1,13},{2,14},{3,15},{4,8},{5,9},{6,10},{7,11},{8,4},{9,5},... | collective-permute-start | bytes 442376 | tf_op jit(solution)/shard_map/ppermute | solution.py:178
  39.8 1.6 %collective-permute-start.26 = (bf16[96,768]{1,0:T(8,128)(2,1)S(1)}, bf16[96,768]{1,0:T(8,128)(2,1)S(1)}, u32[]{:S(2)}, u32[]{:S(2)}) collective-permute-start(bf16[96,768]{1,0:T(8,128)(2,1)S(1)} %get-tuple-element.70), channel_id=1, source_target_pairs={{0,14},{1,15},{2,12},{3,13},{4,10},{5,11},{6,8},{7,9},{8,6},{9,7},... | collective-permute-start | bytes 442376 | tf_op jit(solution)/shard_map/ppermute | solution.py:178
  41.3 3.1 %shard_map.75 = (bf16[96,768]{1,0:T(8,128)(2,1)S(1)}, bf16[96,768]{1,0:T(8,128)(2,1)S(1)}, f32[2,2,96,384]{3,2,1,0:T(8,128)S(1)}, f32[8,128]{1,0:T(8,128)S(1)}, bf16[768,384]{1,0:T(8,128)(2,1)S(1)}) custom-call(s32[3]{0:T(128)S(1)} %pad_add_fusion.meta.refs_0_, f32[8,8]{1,0:T(8,128)S(1)} %convert_element_type.3.refs_1_, ...), custom_call_target="tpu_custom_call" | custom-call | flops 452984832 | bytes 8388608 | tf_op jit(solution)/shard_map/pallas_call | solution.py:206
  44.5 0.0 copy-start.12
  44.5 0.1 collective-permute-start.27
  44.6 2.9 %shard_map.76 = (bf16[96,768]{1,0:T(8,128)(2,1)S(1)}, bf16[96,768]{1,0:T(8,128)(2,1)S(1)}, f32[2,2,96,384]{3,2,1,0:T(8,128)S(1)}, f32[8,128]{1,0:T(8,128)S(1)}) custom-call(s32[3]{0:T(128)S(1)} %pad_add_fusion.meta.refs_0_, f32[8,8]{1,0:T(8,128)S(1)} %convert_element_type.3.refs_1_, bf16[2,8,96,768]{3,2,1,0:T(8,128)(2,1)S(1)} %copy-done.1, ...), custom_call_target="tpu_custom_call" | custom-call | flops 452984832 | bytes 8388608 | tf_op jit(solution)/shard_map/pallas_call | solution.py:206
  47.5 3.0 %shard_map.77 = (bf16[96,768]{1,0:T(8,128)(2,1)S(1)}, bf16[96,768]{1,0:T(8,128)(2,1)S(1)}, f32[2,2,96,384]{3,2,1,0:T(8,128)S(1)}, f32[8,128]{1,0:T(8,128)S(1)}) custom-call(s32[3]{0:T(128)S(1)} %pad_add_fusion.meta.refs_0_, f32[8,8]{1,0:T(8,128)S(1)} %convert_element_type.3.refs_1_, bf16[2,8,96,768]{3,2,1,0:T(8,128)(2,1)S(1)} %copy-done.1, ...), custom_call_target="tpu_custom_call" | custom-call | flops 452984832 | bytes 8388608 | tf_op jit(solution)/shard_map/pallas_call | solution.py:206
  50.5 0.8 copy-done.4
  51.3 3.6 %shard_map.78 = (bf16[96,768]{1,0:T(8,128)(2,1)S(1)}, bf16[96,768]{1,0:T(8,128)(2,1)}, f32[2,2,96,384]{3,2,1,0:T(8,128)S(1)}, f32[8,128]{1,0:T(8,128)S(1)}) custom-call(s32[3]{0:T(128)S(1)} %pad_add_fusion.meta.refs_0_, f32[8,8]{1,0:T(8,128)S(1)} %convert_element_type.3.refs_1_, bf16[2,8,96,768]{3,2,1,0:T(8,128)(2,1)S(1)} %copy-done.1, ...), custom_call_target="tpu_custom_call" | custom-call | flops 452984832 | bytes 8388608 | tf_op jit(solution)/shard_map/pallas_call | solution.py:206
  54.9 0.8 copy-done.2
  55.7 3.7 %collective-permute-start.21 = (bf16[96,768]{1,0:T(8,128)(2,1)S(1)}, bf16[96,768]{1,0:T(8,128)(2,1)S(1)}, u32[]{:S(2)}, u32[]{:S(2)}) collective-permute-start(bf16[96,768]{1,0:T(8,128)(2,1)S(1)} %get-tuple-element.62), channel_id=1, source_target_pairs={{0,20},{1,21},{2,22},{3,23},{4,16},{5,17},{6,18},{7,19},{8,28},{9,... | collective-permute-start | bytes 442376 | tf_op jit(solution)/shard_map/ppermute | solution.py:178
  59.5 1.6 %collective-permute-start.22 = (bf16[96,768]{1,0:T(8,128)(2,1)S(1)}, bf16[96,768]{1,0:T(8,128)(2,1)S(1)}, u32[]{:S(2)}, u32[]{:S(2)}) collective-permute-start(bf16[96,768]{1,0:T(8,128)(2,1)S(1)} %get-tuple-element.63), channel_id=1, source_target_pairs={{0,22},{1,23},{2,20},{3,21},{4,18},{5,19},{6,16},{7,17},{8,30},{9,... | collective-permute-start | bytes 442376 | tf_op jit(solution)/shard_map/ppermute | solution.py:178
  61.0 1.5 %collective-permute-start.23 = (bf16[96,768]{1,0:T(8,128)(2,1)S(1)}, bf16[96,768]{1,0:T(8,128)(2,1)S(1)}, u32[]{:S(2)}, u32[]{:S(2)}) collective-permute-start(bf16[96,768]{1,0:T(8,128)(2,1)S(1)} %get-tuple-element.67), channel_id=1, source_target_pairs={{0,8},{1,9},{2,10},{3,11},{4,12},{5,13},{6,14},{7,15},{8,0},{9,1},... | collective-permute-start | bytes 442376 | tf_op jit(solution)/shard_map/ppermute | solution.py:178
  62.5 2.0 %collective-permute-start.19 = (bf16[96,768]{1,0:T(8,128)(2,1)S(1)}, bf16[96,768]{1,0:T(8,128)(2,1)S(1)}, u32[]{:S(2)}, u32[]{:S(2)}) collective-permute-start(bf16[96,768]{1,0:T(8,128)(2,1)S(1)} %get-tuple-element.60), channel_id=1, source_target_pairs={{0,16},{1,17},{2,18},{3,19},{4,20},{5,21},{6,22},{7,23},{8,24},{9,... | collective-permute-start | bytes 442376 | tf_op jit(solution)/shard_map/ppermute | solution.py:178
  64.5 3.7 %shard_map.79 = (bf16[96,768]{1,0:T(8,128)(2,1)}, bf16[96,768]{1,0:T(8,128)(2,1)}, f32[2,2,96,384]{3,2,1,0:T(8,128)S(1)}, f32[8,128]{1,0:T(8,128)S(1)}) custom-call(s32[3]{0:T(128)S(1)} %pad_add_fusion.meta.refs_0_, f32[8,8]{1,0:T(8,128)S(1)} %convert_element_type.3.refs_1_, bf16[2,8,96,768]{3,2,1,0:T(8,128)(2,1)S(1)} %copy-done.1, ...), custom_call_target="tpu_custom_call" | custom-call | flops 452984832 | bytes 8388608 | tf_op jit(solution)/shard_map/pallas_call | solution.py:206
  68.2 0.8 copy-done.6
  69.0 3.8 %shard_map.80 = (bf16[96,768]{1,0:T(8,128)(2,1)}, bf16[96,768]{1,0:T(8,128)(2,1)}, f32[2,2,96,384]{3,2,1,0:T(8,128)S(1)}, f32[8,128]{1,0:T(8,128)}) custom-call(s32[3]{0:T(128)S(1)} %pad_add_fusion.meta.refs_0_, f32[8,8]{1,0:T(8,128)S(1)} %convert_element_type.3.refs_1_, bf16[2,8,96,768]{3,2,1,0:T(8,128)(2,1)S(1)} %copy-done.1, ...), custom_call_target="tpu_custom_call" | custom-call | flops 452984832 | bytes 8388608 | tf_op jit(solution)/shard_map/pallas_call | solution.py:206
  72.9 0.8 copy-done.8
  73.7 0.7 copy-done.26
  74.4 1.4 %collective-permute-start.20 = (bf16[96,768]{1,0:T(8,128)(2,1)}, bf16[96,768]{1,0:T(8,128)(2,1)S(1)}, u32[]{:S(2)}, u32[]{:S(2)}) collective-permute-start(bf16[96,768]{1,0:T(8,128)(2,1)} %get-tuple-element.61), channel_id=1, source_target_pairs={{0,18},{1,19},{2,16},{3,17},{4,22},{5,23},{6,20},{7,21},{8,26},{9,... | collective-permute-start | bytes 442376 | tf_op jit(solution)/shard_map/ppermute | solution.py:178
  75.9 0.7 copy-done.28
  76.5 1.8 %collective-permute-start.17 = (bf16[96,768]{1,0:T(8,128)(2,1)}, bf16[96,768]{1,0:T(8,128)(2,1)S(1)}, u32[]{:S(2)}, u32[]{:S(2)}) collective-permute-start(bf16[96,768]{1,0:T(8,128)(2,1)} %get-tuple-element.56), channel_id=1, source_target_pairs={{0,28},{1,29},{2,30},{3,31},{4,24},{5,25},{6,26},{7,27},{8,20},{9,... | collective-permute-start | bytes 442376 | tf_op jit(solution)/shard_map/ppermute | solution.py:178
  78.3 0.7 copy-done.30
  79.0 2.5 %collective-permute-start.18 = (bf16[96,768]{1,0:T(8,128)(2,1)}, bf16[96,768]{1,0:T(8,128)(2,1)S(1)}, u32[]{:S(2)}, u32[]{:S(2)}) collective-permute-start(bf16[96,768]{1,0:T(8,128)(2,1)} %get-tuple-element.57), channel_id=1, source_target_pairs={{0,30},{1,31},{2,28},{3,29},{4,26},{5,27},{6,24},{7,25},{8,22},{9,... | collective-permute-start | bytes 442376 | tf_op jit(solution)/shard_map/ppermute | solution.py:178
  81.5 0.7 copy-done.34
  82.1 2.8 %collective-permute-start.15 = (bf16[96,768]{1,0:T(8,128)(2,1)}, bf16[96,768]{1,0:T(8,128)(2,1)S(1)}, u32[]{:S(2)}, u32[]{:S(2)}) collective-permute-start(bf16[96,768]{1,0:T(8,128)(2,1)} %get-tuple-element.54), channel_id=1, source_target_pairs={{0,24},{1,25},{2,26},{3,27},{4,28},{5,29},{6,30},{7,31},{8,16},{9,... | collective-permute-start | bytes 442376 | tf_op jit(solution)/shard_map/ppermute | solution.py:178
  85.0 0.6 copy-done.32
  85.6 0.5 collective-permute-start.16
  86.2 0.1 dynamic-slice_bitcast_fusion
  86.2 0.1 copy.14.refs_4_
  86.3 1.1 %copy-done.11 = f32[2,2,96,384]{3,2,1,0:T(8,128)S(1)} copy-done((f32[2,2,96,384]{3,2,1,0:T(8,128)S(1)}, f32[2,2,96,384]{3,2,1,0:T(8,128)}, u32[]{:S(2)}) %copy-start.11) | copy-done | bytes 589848
  87.4 1.1 %copy-done.13 = f32[2,2,96,384]{3,2,1,0:T(8,128)S(1)} copy-done((f32[2,2,96,384]{3,2,1,0:T(8,128)S(1)}, f32[2,2,96,384]{3,2,1,0:T(8,128)}, u32[]{:S(2)}) %copy-start.13) | copy-done | bytes 589848
  88.5 0.9 copy-done.15
  89.4 0.9 copy-done.17
  90.3 0.9 copy-done.19
  91.2 0.9 copy-done.21
  92.1 1.8 %shard_map.82.refs_10_ = f32[2,8,96,768]{3,2,1,0:T(8,128)} custom-call(s32[3]{0:T(128)S(1)} %pad_add_fusion.meta.refs_0_, f32[8]{0:T(128)S(1)} %copy-done.38, f32[2,2,96,384]{3,2,1,0:T(8,128)S(1)} %copy-done.13, f32[2,2,96,384]{3,2,1,0:T(8,128)S(1)} %copy-done.11, f32[96,1]{1,0:T(8,128)S(1)} %copy.14.refs_4_, f32[1,768]{1,0:T(1,128)S(1)} %reshape.7.refs_5_, ...), custom_call_target="tpu_custom_call" | custom-call | bytes 4194304 | tf_op jit(solution)/shard_map/pallas_call | solution.py:250
  94.1 1.8 %shard_map.83.refs_10_ = f32[2,8,96,768]{3,2,1,0:T(8,128)} custom-call(s32[3]{0:T(128)S(1)} %pad_add_fusion.meta.refs_0_, f32[8]{0:T(128)S(1)} %copy-done.38, f32[2,2,96,384]{3,2,1,0:T(8,128)S(1)} %copy-done.5, f32[2,2,96,384]{3,2,1,0:T(8,128)S(1)} %get-tuple-element.66.refs_3_, f32[96,1]{1,0:T(8,128)S(1)} %copy.14.refs_4_, ...), custom_call_target="tpu_custom_call", output_to_operand_aliasing={{}: (10, {})} | custom-call | bytes 4194304 | tf_op jit(solution)/shard_map/pallas_call | solution.py:250
  96.0 1.8 %shard_map.84.refs_10_ = f32[2,8,96,768]{3,2,1,0:T(8,128)} custom-call(s32[3]{0:T(128)S(1)} %pad_add_fusion.meta.refs_0_, f32[8]{0:T(128)S(1)} %copy-done.38, f32[2,2,96,384]{3,2,1,0:T(8,128)S(1)} %copy-done.3, f32[2,2,96,384]{3,2,1,0:T(8,128)S(1)} %get-tuple-element.59.refs_3_, f32[96,1]{1,0:T(8,128)S(1)} %copy.14.refs_4_, ...), custom_call_target="tpu_custom_call", output_to_operand_aliasing={{}: (10, {})} | custom-call | bytes 4194304 | tf_op jit(solution)/shard_map/pallas_call | solution.py:250
  97.9 1.8 %shard_map.85 = f32[2,8,96,768]{3,2,1,0:T(8,128)} custom-call(s32[3]{0:T(128)S(1)} %pad_add_fusion.meta.refs_0_, f32[8]{0:T(128)S(1)} %copy-done.38, f32[2,2,96,384]{3,2,1,0:T(8,128)S(1)} %copy-done.9, f32[2,2,96,384]{3,2,1,0:T(8,128)S(1)} %copy-done.7, f32[96,1]{1,0:T(8,128)S(1)} %copy.14.refs_4_, ...), custom_call_target="tpu_custom_call", output_to_operand_aliasing={{}: (10, {})} | custom-call | bytes 4194304 | tf_op jit(solution)/shard_map/pallas_call | solution.py:250
  (95 shorter events, 0.2 us)
Async XLA Ops:
  0.0 16.4 %collective-permute-start = (bf16[2,8,96,768]{3,2,1,0:T(8,128)(2,1)}, bf16[2,8,96,768]{3,2,1,0:T(8,128)(2,1)S(1)}, u32[]{:S(2)}, u32[]{:S(2)}) collective-permute-start(bf16[2,8,96,768]{3,2,1,0:T(8,128)(2,1)} %refs_2_.15), channel_id=1, source_target_pairs={{0,1},{1,0},{2,3},{3,2},{4,5},{5,4},{6,7},{7,6},{8,9},{9,8},{10,11... | collective-permute-start | bytes 7077896 | tf_op jit(solution)/shard_map/ppermute | solution.py:178
  1.4 7.9 %collective-permute-start.3 = (bf16[96,384]{1,0:T(8,128)(2,1)S(1)}, bf16[96,384]{1,0:T(8,128)(2,1)S(1)}, u32[]{:S(2)}, u32[]{:S(2)}) collective-permute-start(bf16[96,384]{1,0:T(8,128)(2,1)S(1)} %get-tuple-element.77.refs_14_), channel_id=1, source_target_pairs={{0,6},{1,7},{2,4},{3,5},{4,2},{5,3},{6,0},{7,1},{8,14},{9,15},{10,... | collective-permute-start | bytes 221192 | tf_op jit(solution)/shard_map/ppermute | solution.py:178
  6.1 6.8 %collective-permute-start.2 = (bf16[96,384]{1,0:T(8,128)(2,1)S(1)}, bf16[96,384]{1,0:T(8,128)(2,1)S(1)}, u32[]{:S(2)}, u32[]{:S(2)}) collective-permute-start(bf16[96,384]{1,0:T(8,128)(2,1)S(1)} %get-tuple-element.77.refs_14_), channel_id=1, source_target_pairs={{0,4},{1,5},{2,6},{3,7},{4,0},{5,1},{6,2},{7,3},{8,12},{9,13},{10,... | collective-permute-start | bytes 221192 | tf_op jit(solution)/shard_map/ppermute | solution.py:178
  6.1 6.8 %collective-permute-start.1 = (bf16[96,384]{1,0:T(8,128)(2,1)S(1)}, bf16[96,384]{1,0:T(8,128)(2,1)S(1)}, u32[]{:S(2)}, u32[]{:S(2)}) collective-permute-start(bf16[96,384]{1,0:T(8,128)(2,1)S(1)} %get-tuple-element.78.refs_5_.refs_15_), channel_id=1, source_target_pairs={{0,2},{1,3},{2,0},{3,1},{4,6},{5,7},{6,4},{7,5},{8,10},{9,11},{10,... | collective-permute-start | bytes 221192 | tf_op jit(solution)/shard_map/ppermute | solution.py:178
  6.7 9.6 %collective-permute-start.4 = (bf16[96,384]{1,0:T(8,128)(2,1)S(1)}, bf16[96,384]{1,0:T(8,128)(2,1)S(1)}, u32[]{:S(2)}, u32[]{:S(2)}) collective-permute-start(bf16[96,384]{1,0:T(8,128)(2,1)S(1)} %get-tuple-element.78.refs_5_.refs_15_), channel_id=1, source_target_pairs={{0,1},{1,0},{2,3},{3,2},{4,5},{5,4},{6,7},{7,6},{8,9},{9,8},{10,11... | collective-permute-start | bytes 221192 | tf_op jit(solution)/shard_map/ppermute | solution.py:178
  9.3 7.1 %collective-permute-start.7 = (bf16[96,384]{1,0:T(8,128)(2,1)S(1)}, bf16[96,384]{1,0:T(8,128)(2,1)S(1)}, u32[]{:S(2)}, u32[]{:S(2)}) collective-permute-start(bf16[96,384]{1,0:T(8,128)(2,1)S(1)} %collective-permute-done.3.refs_8_), channel_id=1, source_target_pairs={{0,1},{1,0},{2,3},{3,2},{4,5},{5,4},{6,7},{7,6},{8,9},{9,8},{10,11... | collective-permute-start | bytes 221192 | tf_op jit(solution)/shard_map/ppermute | solution.py:178
  12.9 3.5 %collective-permute-start.6 = (bf16[96,384]{1,0:T(8,128)(2,1)S(1)}, bf16[96,384]{1,0:T(8,128)(2,1)S(1)}, u32[]{:S(2)}, u32[]{:S(2)}) collective-permute-start(bf16[96,384]{1,0:T(8,128)(2,1)S(1)} %collective-permute-done.2.refs_7_), channel_id=1, source_target_pairs={{0,1},{1,0},{2,3},{3,2},{4,5},{5,4},{6,7},{7,6},{8,9},{9,8},{10,11... | collective-permute-start | bytes 221192 | tf_op jit(solution)/shard_map/ppermute | solution.py:178
  12.9 3.5 %collective-permute-start.5 = (bf16[96,384]{1,0:T(8,128)(2,1)S(1)}, bf16[96,384]{1,0:T(8,128)(2,1)S(1)}, u32[]{:S(2)}, u32[]{:S(2)}) collective-permute-start(bf16[96,384]{1,0:T(8,128)(2,1)S(1)} %collective-permute-done.1.refs_6_), channel_id=1, source_target_pairs={{0,1},{1,0},{2,3},{3,2},{4,5},{5,4},{6,7},{7,6},{8,9},{9,8},{10,11... | collective-permute-start | bytes 221192 | tf_op jit(solution)/shard_map/ppermute | solution.py:178
  13.5 0.7 copy-start.36
  16.4 1.7 %copy-start = (bf16[2,8,96,768]{3,2,1,0:T(8,128)(2,1)S(1)}, bf16[2,8,96,768]{3,2,1,0:T(8,128)(2,1)}, u32[]{:S(2)}) copy-start(bf16[2,8,96,768]{3,2,1,0:T(8,128)(2,1)} %refs_2_.15) | copy-start | bytes 7077892
  18.1 13.7 %copy-start.1 = (bf16[2,8,96,768]{3,2,1,0:T(8,128)(2,1)S(1)}, bf16[2,8,96,768]{3,2,1,0:T(8,128)(2,1)}, u32[]{:S(2)}) copy-start(bf16[2,8,96,768]{3,2,1,0:T(8,128)(2,1)} %refs_2_.15) | copy-start | bytes 7077892
  21.2 20.2 %copy-start.10 = (f32[2,2,96,384]{3,2,1,0:T(8,128)}, f32[2,2,96,384]{3,2,1,0:T(8,128)S(1)}, u32[]{:S(2)}) copy-start(f32[2,2,96,384]{3,2,1,0:T(8,128)S(1)} %get-tuple-element.72.refs_3_) | copy-start | bytes 1769476
  21.2 6.9 %collective-permute-start.10 = (bf16[96,384]{1,0:T(8,128)(2,1)S(1)}, bf16[96,384]{1,0:T(8,128)(2,1)S(1)}, u32[]{:S(2)}, u32[]{:S(2)}) collective-permute-start(bf16[96,384]{1,0:T(8,128)(2,1)S(1)} %get-tuple-element.44), channel_id=1, source_target_pairs={{0,6},{1,7},{2,4},{3,5},{4,2},{5,3},{6,0},{7,1},{8,14},{9,15},{10,... | collective-permute-start | bytes 221192 | tf_op jit(solution)/shard_map/ppermute | solution.py:178
  23.7 6.9 %collective-permute-start.9 = (bf16[96,384]{1,0:T(8,128)(2,1)S(1)}, bf16[96,384]{1,0:T(8,128)(2,1)S(1)}, u32[]{:S(2)}, u32[]{:S(2)}) collective-permute-start(bf16[96,384]{1,0:T(8,128)(2,1)S(1)} %get-tuple-element.44), channel_id=1, source_target_pairs={{0,4},{1,5},{2,6},{3,7},{4,0},{5,1},{6,2},{7,3},{8,12},{9,13},{10,... | collective-permute-start | bytes 221192 | tf_op jit(solution)/shard_map/ppermute | solution.py:178
  23.7 6.9 %collective-permute-start.8 = (bf16[96,384]{1,0:T(8,128)(2,1)S(1)}, bf16[96,384]{1,0:T(8,128)(2,1)S(1)}, u32[]{:S(2)}, u32[]{:S(2)}) collective-permute-start(bf16[96,384]{1,0:T(8,128)(2,1)S(1)} %get-tuple-element.43.refs_5_), channel_id=1, source_target_pairs={{0,2},{1,3},{2,0},{3,1},{4,6},{5,7},{6,4},{7,5},{8,10},{9,11},{10,... | collective-permute-start | bytes 221192 | tf_op jit(solution)/shard_map/ppermute | solution.py:178
  25.6 9.5 %collective-permute-start.11 = (bf16[96,384]{1,0:T(8,128)(2,1)S(1)}, bf16[96,384]{1,0:T(8,128)(2,1)S(1)}, u32[]{:S(2)}, u32[]{:S(2)}) collective-permute-start(bf16[96,384]{1,0:T(8,128)(2,1)S(1)} %get-tuple-element.43.refs_5_), channel_id=1, source_target_pairs={{0,1},{1,0},{2,3},{3,2},{4,5},{5,4},{6,7},{7,6},{8,9},{9,8},{10,11... | collective-permute-start | bytes 221192 | tf_op jit(solution)/shard_map/ppermute | solution.py:178
  28.1 8.8 %collective-permute-start.14 = (bf16[96,384]{1,0:T(8,128)(2,1)S(1)}, bf16[96,384]{1,0:T(8,128)(2,1)S(1)}, u32[]{:S(2)}, u32[]{:S(2)}) collective-permute-start(bf16[96,384]{1,0:T(8,128)(2,1)S(1)} %collective-permute-done.10.refs_8_), channel_id=1, source_target_pairs={{0,1},{1,0},{2,3},{3,2},{4,5},{5,4},{6,7},{7,6},{8,9},{9,8},{10,11... | collective-permute-start | bytes 221192 | tf_op jit(solution)/shard_map/ppermute | solution.py:178
  30.6 9.1 %collective-permute-start.13 = (bf16[96,384]{1,0:T(8,128)(2,1)S(1)}, bf16[96,384]{1,0:T(8,128)(2,1)S(1)}, u32[]{:S(2)}, u32[]{:S(2)}) collective-permute-start(bf16[96,384]{1,0:T(8,128)(2,1)S(1)} %collective-permute-done.9.refs_7_), channel_id=1, source_target_pairs={{0,1},{1,0},{2,3},{3,2},{4,5},{5,4},{6,7},{7,6},{8,9},{9,8},{10,11... | collective-permute-start | bytes 221192 | tf_op jit(solution)/shard_map/ppermute | solution.py:178
  30.7 10.7 %collective-permute-start.12 = (bf16[96,384]{1,0:T(8,128)(2,1)S(1)}, bf16[96,384]{1,0:T(8,128)(2,1)S(1)}, u32[]{:S(2)}, u32[]{:S(2)}) collective-permute-start(bf16[96,384]{1,0:T(8,128)(2,1)S(1)} %collective-permute-done.8.refs_6_), channel_id=1, source_target_pairs={{0,1},{1,0},{2,3},{3,2},{4,5},{5,4},{6,7},{7,6},{8,9},{9,8},{10,11... | collective-permute-start | bytes 221192 | tf_op jit(solution)/shard_map/ppermute | solution.py:178
  31.2 24.6 %collective-permute-start.28 = (bf16[96,768]{1,0:T(8,128)(2,1)S(1)}, bf16[96,768]{1,0:T(8,128)(2,1)S(1)}, u32[]{:S(2)}, u32[]{:S(2)}) collective-permute-start(bf16[96,768]{1,0:T(8,128)(2,1)S(1)} %get-tuple-element.75), channel_id=1, source_target_pairs={{0,4},{1,5},{2,6},{3,7},{4,0},{5,1},{6,2},{7,3},{8,12},{9,13},{10,... | collective-permute-start | bytes 442376 | tf_op jit(solution)/shard_map/ppermute | solution.py:178
  35.1 24.3 %collective-permute-start.29 = (bf16[96,768]{1,0:T(8,128)(2,1)S(1)}, bf16[96,768]{1,0:T(8,128)(2,1)S(1)}, u32[]{:S(2)}, u32[]{:S(2)}) collective-permute-start(bf16[96,768]{1,0:T(8,128)(2,1)S(1)} %get-tuple-element.76), channel_id=1, source_target_pairs={{0,6},{1,7},{2,4},{3,5},{4,2},{5,3},{6,0},{7,1},{8,14},{9,15},{10,... | collective-permute-start | bytes 442376 | tf_op jit(solution)/shard_map/ppermute | solution.py:178
  36.9 24.1 %collective-permute-start.25 = (bf16[96,768]{1,0:T(8,128)(2,1)S(1)}, bf16[96,768]{1,0:T(8,128)(2,1)S(1)}, u32[]{:S(2)}, u32[]{:S(2)}) collective-permute-start(bf16[96,768]{1,0:T(8,128)(2,1)S(1)} %get-tuple-element.69), channel_id=1, source_target_pairs={{0,12},{1,13},{2,14},{3,15},{4,8},{5,9},{6,10},{7,11},{8,4},{9,5},... | collective-permute-start | bytes 442376 | tf_op jit(solution)/shard_map/ppermute | solution.py:178
  39.8 22.8 %collective-permute-start.26 = (bf16[96,768]{1,0:T(8,128)(2,1)S(1)}, bf16[96,768]{1,0:T(8,128)(2,1)S(1)}, u32[]{:S(2)}, u32[]{:S(2)}) collective-permute-start(bf16[96,768]{1,0:T(8,128)(2,1)S(1)} %get-tuple-element.70), channel_id=1, source_target_pairs={{0,14},{1,15},{2,12},{3,13},{4,10},{5,11},{6,8},{7,9},{8,6},{9,7},... | collective-permute-start | bytes 442376 | tf_op jit(solution)/shard_map/ppermute | solution.py:178
  44.5 6.0 %copy-start.12 = (f32[2,2,96,384]{3,2,1,0:T(8,128)}, f32[2,2,96,384]{3,2,1,0:T(8,128)S(1)}, u32[]{:S(2)}) copy-start(f32[2,2,96,384]{3,2,1,0:T(8,128)S(1)} %get-tuple-element.71.refs_2_) | copy-start | bytes 1769476
  44.5 6.0 %copy-start.18 = (bf16[96,768]{1,0:T(8,128)(2,1)}, bf16[96,768]{1,0:T(8,128)(2,1)S(1)}, u32[]{:S(2)}) copy-start(bf16[96,768]{1,0:T(8,128)(2,1)S(1)} %get-tuple-element.73.refs_6_) | copy-start | bytes 442372
  44.5 18.0 %collective-permute-start.27 = (bf16[96,768]{1,0:T(8,128)(2,1)S(1)}, bf16[96,768]{1,0:T(8,128)(2,1)S(1)}, u32[]{:S(2)}, u32[]{:S(2)}) collective-permute-start(bf16[96,768]{1,0:T(8,128)(2,1)S(1)} %get-tuple-element.74), channel_id=1, source_target_pairs={{0,2},{1,3},{2,0},{3,1},{4,6},{5,7},{6,4},{7,5},{8,10},{9,11},{10,... | collective-permute-start | bytes 442376 | tf_op jit(solution)/shard_map/ppermute | solution.py:178
  50.5 0.8 copy-start.4
  54.9 0.8 copy-start.2
  55.7 17.1 %copy-start.14 = (bf16[96,768]{1,0:T(8,128)(2,1)}, bf16[96,768]{1,0:T(8,128)(2,1)S(1)}, u32[]{:S(2)}) copy-start(bf16[96,768]{1,0:T(8,128)(2,1)S(1)} %collective-permute-done.28.refs_8_) | copy-start | bytes 442372
  55.7 18.0 %collective-permute-start.21 = (bf16[96,768]{1,0:T(8,128)(2,1)S(1)}, bf16[96,768]{1,0:T(8,128)(2,1)S(1)}, u32[]{:S(2)}, u32[]{:S(2)}) collective-permute-start(bf16[96,768]{1,0:T(8,128)(2,1)S(1)} %get-tuple-element.62), channel_id=1, source_target_pairs={{0,20},{1,21},{2,22},{3,23},{4,16},{5,17},{6,18},{7,19},{8,28},{9,... | collective-permute-start | bytes 442376 | tf_op jit(solution)/shard_map/ppermute | solution.py:178
  59.5 13.4 %copy-start.16 = (bf16[96,768]{1,0:T(8,128)(2,1)}, bf16[96,768]{1,0:T(8,128)(2,1)S(1)}, u32[]{:S(2)}) copy-start(bf16[96,768]{1,0:T(8,128)(2,1)S(1)} %collective-permute-done.29.refs_9_) | copy-start | bytes 442372
  59.5 16.4 %collective-permute-start.22 = (bf16[96,768]{1,0:T(8,128)(2,1)S(1)}, bf16[96,768]{1,0:T(8,128)(2,1)S(1)}, u32[]{:S(2)}, u32[]{:S(2)}) collective-permute-start(bf16[96,768]{1,0:T(8,128)(2,1)S(1)} %get-tuple-element.63), channel_id=1, source_target_pairs={{0,22},{1,23},{2,20},{3,21},{4,18},{5,19},{6,16},{7,17},{8,30},{9,... | collective-permute-start | bytes 442376 | tf_op jit(solution)/shard_map/ppermute | solution.py:178
  61.0 11.9 %copy-start.22 = (bf16[96,768]{1,0:T(8,128)(2,1)}, bf16[96,768]{1,0:T(8,128)(2,1)S(1)}, u32[]{:S(2)}) copy-start(bf16[96,768]{1,0:T(8,128)(2,1)S(1)} %collective-permute-done.25.refs_8_) | copy-start | bytes 442372
  61.0 17.3 %collective-permute-start.23 = (bf16[96,768]{1,0:T(8,128)(2,1)S(1)}, bf16[96,768]{1,0:T(8,128)(2,1)S(1)}, u32[]{:S(2)}, u32[]{:S(2)}) collective-permute-start(bf16[96,768]{1,0:T(8,128)(2,1)S(1)} %get-tuple-element.67), channel_id=1, source_target_pairs={{0,8},{1,9},{2,10},{3,11},{4,12},{5,13},{6,14},{7,15},{8,0},{9,1},... | collective-permute-start | bytes 442376 | tf_op jit(solution)/shard_map/ppermute | solution.py:178
  62.5 10.4 %copy-start.24 = (bf16[96,768]{1,0:T(8,128)(2,1)}, bf16[96,768]{1,0:T(8,128)(2,1)S(1)}, u32[]{:S(2)}) copy-start(bf16[96,768]{1,0:T(8,128)(2,1)S(1)} %collective-permute-done.26.refs_9_) | copy-start | bytes 442372
  62.5 18.9 %collective-permute-start.24 = (bf16[96,768]{1,0:T(8,128)(2,1)S(1)}, bf16[96,768]{1,0:T(8,128)(2,1)S(1)}, u32[]{:S(2)}, u32[]{:S(2)}) collective-permute-start(bf16[96,768]{1,0:T(8,128)(2,1)S(1)} %get-tuple-element.68), channel_id=1, source_target_pairs={{0,10},{1,11},{2,8},{3,9},{4,14},{5,15},{6,12},{7,13},{8,2},{9,3},... | collective-permute-start | bytes 442376 | tf_op jit(solution)/shard_map/ppermute | solution.py:178
  62.5 10.4 %copy-start.20 = (bf16[96,768]{1,0:T(8,128)(2,1)}, bf16[96,768]{1,0:T(8,128)(2,1)S(1)}, u32[]{:S(2)}) copy-start(bf16[96,768]{1,0:T(8,128)(2,1)S(1)} %collective-permute-done.27.refs_7_) | copy-start | bytes 442372
  62.5 22.4 %collective-permute-start.19 = (bf16[96,768]{1,0:T(8,128)(2,1)S(1)}, bf16[96,768]{1,0:T(8,128)(2,1)S(1)}, u32[]{:S(2)}, u32[]{:S(2)}) collective-permute-start(bf16[96,768]{1,0:T(8,128)(2,1)S(1)} %get-tuple-element.60), channel_id=1, source_target_pairs={{0,16},{1,17},{2,18},{3,19},{4,20},{5,21},{6,22},{7,23},{8,24},{9,... | collective-permute-start | bytes 442376 | tf_op jit(solution)/shard_map/ppermute | solution.py:178
  64.5 21.6 %copy-start.39 = (f32[768]{0:T(1024)S(1)}, f32[768]{0:T(1024)}, u32[]{:S(2)}) copy-start(f32[768]{0:T(1024)} %param.13) | copy-start | bytes 9220
  64.5 21.8 %copy-start.38 = (f32[8]{0:T(128)S(1)}, f32[8]{0:T(128)}, u32[]{:S(2)}) copy-start(f32[8]{0:T(128)} %refs_1_.7) | copy-start | bytes 100
  68.2 0.8 copy-start.6
  72.9 0.8 copy-start.8
  73.7 20.2 %copy-start.5 = (f32[2,2,96,384]{3,2,1,0:T(8,128)S(1)}, f32[2,2,96,384]{3,2,1,0:T(8,128)}, u32[]{:S(2)}) copy-start(f32[2,2,96,384]{3,2,1,0:T(8,128)} %copy-done.4) | copy-start | bytes 1769476
  74.4 21.5 %collective-permute-start.20 = (bf16[96,768]{1,0:T(8,128)(2,1)}, bf16[96,768]{1,0:T(8,128)(2,1)S(1)}, u32[]{:S(2)}, u32[]{:S(2)}) collective-permute-start(bf16[96,768]{1,0:T(8,128)(2,1)} %get-tuple-element.61), channel_id=1, source_target_pairs={{0,18},{1,19},{2,16},{3,17},{4,22},{5,23},{6,20},{7,21},{8,26},{9,... | collective-permute-start | bytes 442376 | tf_op jit(solution)/shard_map/ppermute | solution.py:178
  76.5 21.3 %collective-permute-start.17 = (bf16[96,768]{1,0:T(8,128)(2,1)}, bf16[96,768]{1,0:T(8,128)(2,1)S(1)}, u32[]{:S(2)}, u32[]{:S(2)}) collective-permute-start(bf16[96,768]{1,0:T(8,128)(2,1)} %get-tuple-element.56), channel_id=1, source_target_pairs={{0,28},{1,29},{2,30},{3,31},{4,24},{5,25},{6,26},{7,27},{8,20},{9,... | collective-permute-start | bytes 442376 | tf_op jit(solution)/shard_map/ppermute | solution.py:178
  79.0 18.8 %collective-permute-start.18 = (bf16[96,768]{1,0:T(8,128)(2,1)}, bf16[96,768]{1,0:T(8,128)(2,1)S(1)}, u32[]{:S(2)}, u32[]{:S(2)}) collective-permute-start(bf16[96,768]{1,0:T(8,128)(2,1)} %get-tuple-element.57), channel_id=1, source_target_pairs={{0,30},{1,31},{2,28},{3,29},{4,26},{5,27},{6,24},{7,25},{8,22},{9,... | collective-permute-start | bytes 442376 | tf_op jit(solution)/shard_map/ppermute | solution.py:178
  82.1 15.7 %collective-permute-start.15 = (bf16[96,768]{1,0:T(8,128)(2,1)}, bf16[96,768]{1,0:T(8,128)(2,1)S(1)}, u32[]{:S(2)}, u32[]{:S(2)}) collective-permute-start(bf16[96,768]{1,0:T(8,128)(2,1)} %get-tuple-element.54), channel_id=1, source_target_pairs={{0,24},{1,25},{2,26},{3,27},{4,28},{5,29},{6,30},{7,31},{8,16},{9,... | collective-permute-start | bytes 442376 | tf_op jit(solution)/shard_map/ppermute | solution.py:178
  85.6 12.2 %collective-permute-start.16 = (bf16[96,768]{1,0:T(8,128)(2,1)}, bf16[96,768]{1,0:T(8,128)(2,1)S(1)}, u32[]{:S(2)}, u32[]{:S(2)}) collective-permute-start(bf16[96,768]{1,0:T(8,128)(2,1)} %get-tuple-element.55), channel_id=1, source_target_pairs={{0,26},{1,27},{2,24},{3,25},{4,30},{5,31},{6,28},{7,29},{8,18},{9,... | collective-permute-start | bytes 442376 | tf_op jit(solution)/shard_map/ppermute | solution.py:178
  86.3 1.1 %copy-start.11 = (f32[2,2,96,384]{3,2,1,0:T(8,128)S(1)}, f32[2,2,96,384]{3,2,1,0:T(8,128)}, u32[]{:S(2)}) copy-start(f32[2,2,96,384]{3,2,1,0:T(8,128)} %copy-done.10) | copy-start | bytes 1769476
  87.4 1.1 %copy-start.13 = (f32[2,2,96,384]{3,2,1,0:T(8,128)S(1)}, f32[2,2,96,384]{3,2,1,0:T(8,128)}, u32[]{:S(2)}) copy-start(f32[2,2,96,384]{3,2,1,0:T(8,128)} %copy-done.12) | copy-start | bytes 1769476
  88.5 0.9 copy-start.15
  89.4 0.9 copy-start.17
  90.3 0.9 copy-start.19
  91.2 0.9 copy-start.21
  92.1 1.9 %copy-start.23 = (bf16[96,768]{1,0:T(8,128)(2,1)S(1)}, bf16[96,768]{1,0:T(8,128)(2,1)}, u32[]{:S(2)}) copy-start(bf16[96,768]{1,0:T(8,128)(2,1)} %copy-done.22) | copy-start | bytes 442372
  92.1 1.9 %copy-start.25 = (bf16[96,768]{1,0:T(8,128)(2,1)S(1)}, bf16[96,768]{1,0:T(8,128)(2,1)}, u32[]{:S(2)}) copy-start(bf16[96,768]{1,0:T(8,128)(2,1)} %copy-done.24) | copy-start | bytes 442372
  92.1 1.9 %copy-start.31 = (bf16[96,768]{1,0:T(8,128)(2,1)S(1)}, bf16[96,768]{1,0:T(8,128)(2,1)}, u32[]{:S(2)}) copy-start(bf16[96,768]{1,0:T(8,128)(2,1)} %copy-done.30) | copy-start | bytes 442372
  92.1 1.9 %copy-start.35 = (bf16[96,768]{1,0:T(8,128)(2,1)S(1)}, bf16[96,768]{1,0:T(8,128)(2,1)}, u32[]{:S(2)}) copy-start(bf16[96,768]{1,0:T(8,128)(2,1)} %copy-done.34) | copy-start | bytes 442372
  94.0 1.9 %copy-start.3 = (f32[2,2,96,384]{3,2,1,0:T(8,128)S(1)}, f32[2,2,96,384]{3,2,1,0:T(8,128)}, u32[]{:S(2)}) copy-start(f32[2,2,96,384]{3,2,1,0:T(8,128)} %copy-done.2) | copy-start | bytes 1769476
  94.0 1.9 %copy-start.27 = (bf16[96,768]{1,0:T(8,128)(2,1)S(1)}, bf16[96,768]{1,0:T(8,128)(2,1)}, u32[]{:S(2)}) copy-start(bf16[96,768]{1,0:T(8,128)(2,1)} %copy-done.26) | copy-start | bytes 442372
  94.0 1.9 %copy-start.29 = (bf16[96,768]{1,0:T(8,128)(2,1)S(1)}, bf16[96,768]{1,0:T(8,128)(2,1)}, u32[]{:S(2)}) copy-start(bf16[96,768]{1,0:T(8,128)(2,1)} %copy-done.28) | copy-start | bytes 442372
  94.1 1.9 %copy-start.33 = (bf16[96,768]{1,0:T(8,128)(2,1)S(1)}, bf16[96,768]{1,0:T(8,128)(2,1)}, u32[]{:S(2)}) copy-start(bf16[96,768]{1,0:T(8,128)(2,1)} %copy-done.32) | copy-start | bytes 442372
  95.9 1.9 %copy-start.7 = (f32[2,2,96,384]{3,2,1,0:T(8,128)S(1)}, f32[2,2,96,384]{3,2,1,0:T(8,128)}, u32[]{:S(2)}) copy-start(f32[2,2,96,384]{3,2,1,0:T(8,128)} %copy-done.6) | copy-start | bytes 1769476
  95.9 1.9 %copy-start.9 = (f32[2,2,96,384]{3,2,1,0:T(8,128)S(1)}, f32[2,2,96,384]{3,2,1,0:T(8,128)}, u32[]{:S(2)}) copy-start(f32[2,2,96,384]{3,2,1,0:T(8,128)} %copy-done.8) | copy-start | bytes 1769476
  (6 other events, 4.0 us)

commit v3 on v0

v3 whole, which is shorter than its diff:
```python
import functools

import jax
import jax.numpy as jnp
from jax import lax
from jax.experimental import pallas as pl
from jax.experimental.pallas import tpu as pltpu
from jax.sharding import PartitionSpec as P

CORES = 2
LIMIT = 12 * 1024 * 1024
VMEM = pl.BlockSpec(memory_space=pltpu.VMEM)
SMEM = pl.BlockSpec(memory_space=pltpu.SMEM)
ANY = pl.BlockSpec(memory_space=pl.ANY)
HBM = pl.BlockSpec(memory_space=pltpu.HBM)


def expand_rows(mask, first_block, blocks, block):
    rows_here = lax.dynamic_slice_in_dim(mask, first_block, blocks, 0)
    return jnp.repeat(jnp.repeat(rows_here, block, axis=0), block, axis=1).astype(jnp.bfloat16)


def plain(amplitudes, integrals, occ_fock, amp_mask, int_mask, occ_energy, vir_energy):
    occ_rows, occ_all, vir_rows, vir_all = amplitudes.shape
    block = vir_all // amp_mask.shape[0]
    vir_start = lax.axis_index("vir") * vir_rows
    occ_start = lax.axis_index("occ") * occ_rows
    blocks = vir_rows // block
    first_block = vir_start // block
    masked = amplitudes * expand_rows(amp_mask, first_block, blocks, block)[None, None]
    masked_w = integrals * expand_rows(int_mask, first_block, blocks, block)
    flat_amps = masked.reshape(-1, vir_all)
    full_w = lax.all_gather(masked_w, "vir", axis=0, tiled=True)
    ladder = jnp.dot(flat_amps, full_w, preferred_element_type=jnp.float32)
    ladder = ladder.reshape(occ_rows, occ_all, vir_rows, vir_all)
    holes = jnp.einsum("ikab,kj->ijab", masked, occ_fock, preferred_element_type=jnp.float32)
    mixed = ladder + holes
    outgoing = mixed.astype(jnp.bfloat16)
    halfway = lax.all_to_all(outgoing, "vir", split_axis=3, concat_axis=2, tiled=True)
    arrived = lax.all_to_all(halfway, "occ", split_axis=1, concat_axis=0, tiled=True)
    mirrored = arrived.transpose(1, 0, 3, 2).astype(jnp.float32)
    vir_here = lax.dynamic_slice_in_dim(vir_energy, vir_start, vir_rows, 0)
    occ_here = lax.dynamic_slice_in_dim(occ_energy, occ_start, occ_rows, 0)
    denominator = (
        vir_here[None, None, :, None]
        + vir_energy[None, None, None, :]
        - occ_here[:, None, None, None]
        - occ_energy[None, :, None, None]
    )
    return (mixed + mirrored) / denominator


def one_hot(shape, row_of, column_of):
    rows = lax.broadcasted_iota(jnp.int32, shape, 0)
    columns = lax.broadcasted_iota(jnp.int32, shape, 1)
    return (row_of(rows) == column_of(columns)).astype(jnp.float32).astype(jnp.bfloat16)


def prepare_kernel(block, meta, fock, own, sib, amp_flags, int_flags, x, h, wide_int, amp_mask, int_mask, sems):
    occ_rows, occ_all, _, rows, width = x.shape
    blocks = amp_mask.shape[0]
    z, core = meta[1], meta[2]
    sources = ((own, core), (sib, 1 - core))
    loads = [pltpu.make_async_copy(source, x.at[:, :, at], sems.at[n]) for n, (source, at) in enumerate(sources)]
    flags = [pltpu.make_async_copy(amp_flags, amp_mask, sems.at[2]), pltpu.make_async_copy(int_flags, int_mask, sems.at[3])]
    for load in flags + loads:
        load.start()
    for load in flags:
        load.wait()
    spread = one_hot((blocks, width), lambda r: r, lambda c: c // block)

    def wide(mask, first):
        rows_of = one_hot((rows, blocks), lambda r: (r + first) // block, lambda c: c)
        tall = jnp.dot(rows_of, mask[...].astype(jnp.float32).astype(jnp.bfloat16), preferred_element_type=jnp.float32)
        return jnp.dot(tall.astype(jnp.bfloat16), spread, preferred_element_type=jnp.float32).astype(jnp.bfloat16)

    for k in range(4):
        wide_int[k] = wide(int_mask, ((z ^ k) * CORES + core) * rows)
    part = width // 2
    for n, (_, at) in enumerate(sources):
        live = wide(amp_mask, (z * CORES + at) * rows)
        loads[n].wait()
        for i in range(occ_rows):
            for j in range(occ_all):
                x[i, j, at] = x[i, j, at] * live

        def step(s, carry, at=at):
            row = pl.multiple_of((s // 2) * 16, 16)
            columns = pl.ds(pl.multiple_of((s % 2) * part, part), part)
            for i in range(occ_rows):
                amps = [x[i, k, at, pl.ds(row, 16), columns].astype(jnp.float32) for k in range(occ_all)]
                for j in range(occ_all):
                    total = amps[0] * fock[0, j]
                    for k in range(1, occ_all):
                        total = total + amps[k] * fock[k, j]
                    h[i, j, at, pl.ds(row, 16), columns] = total
            return carry

        lax.fori_loop(0, 2 * rows // 16, step, 0)


def relay_kernel(own, near, middle, far, mask, out):
    for k, piece in enumerate((own, near, middle, far)):
        out[k] = piece[...] * mask[k]


def tile_kernel(tasks, first, *refs):
    meta, x, h = refs[:3]
    _, occ_all, _, rows, width = x.shape
    half, chip = width // 2, CORES * rows
    o, z, core = meta[0], meta[1], meta[2]
    flipped, own, sems = refs[-3:]
    if first:
        mine, theirs = refs[3:5]
        outs, w = refs[5:-4], refs[-4]
        for k in range(4):
            for piece, at in ((mine, core), (theirs, 1 - core)):
                w[pl.ds(pl.multiple_of(((z ^ k) * CORES + at) * rows, rows), rows), :] = piece[k]
    else:
        w, outs, token = refs[3], refs[5:-4], refs[-4]
        token[...] = jnp.zeros(token.shape, token.dtype)
    occ_rows = own.shape[1]
    pairs = occ_rows * occ_rows
    outs = iter(outs)
    copies = []
    for n, (partner, side) in enumerate(tasks):
        mixed_out = next(outs)
        first_j = (o ^ partner) * occ_rows
        columns = pl.ds(pl.multiple_of(((z // 2) ^ side) * half, half), half)
        ladder = jnp.dot(
            x[:, pl.ds(first_j, occ_rows)].reshape(pairs * chip, width), w[:, columns], preferred_element_type=jnp.float32
        )
        for i in range(occ_rows):
            for jj in range(occ_rows):
                m = i * occ_rows + jj
                mixed = ladder[m * chip : (m + 1) * chip] + h[i, first_j + jj, :, :, columns].reshape(chip, half)
                own[n, i, jj] = mixed.reshape(CORES, rows, half)
                flipped[:, m * chip : (m + 1) * chip] = mixed.astype(jnp.bfloat16).T
        copies.append(pltpu.make_async_copy(own.at[n, :, :, core], mixed_out, sems.at[n]))
        copies[-1].start()
        for s in (0, 1):
            start = pl.multiple_of((((z & 1) ^ s) * CORES + core) * rows, rows)
            next(outs)[...] = flipped[pl.ds(start, rows), :]
    for copy in copies:
        copy.wait()


def finish_kernel(tasks, held, *refs):
    meta, occ_energy, energy = refs[:3]
    count = len(tasks)
    per = [refs[4 + 3 * n : 7 + 3 * n] for n in range(count)]
    result, token = refs[-4:-2] if held else refs[-7:-5]
    if held:
        done, out_sems = refs[-2:]
    else:
        done, out_sems, mixed, tiles, in_sems = refs[-5:]
        loads = []
        for n in range(count):
            targets = [mixed.at[n], tiles.at[n, 0], tiles.at[n, 1]]
            loads.append([pltpu.make_async_copy(per[n][c], targets[c], in_sems.at[n, c]) for c in range(3)])
            for copy in loads[-1]:
                copy.start()
    _, occ_rows, _, rows, half = done.shape
    width, chip = energy.shape[1], CORES * rows
    o, z, core = meta[0], meta[1], meta[2]
    odd = (z & 1) == 1
    place = (z * CORES + core) * rows
    mine = lax.broadcasted_iota(jnp.int32, (rows, width), 1) == lax.broadcasted_iota(jnp.int32, (rows, width), 0) + place
    row_energy = jnp.sum(jnp.where(mine, energy[...], 0.0), axis=1, keepdims=True)
    stores = []
    for n, (partner, side) in enumerate(tasks):
        first_j = (o ^ partner) * occ_rows
        lanes = pl.ds(pl.multiple_of(((z // 2) ^ side) * half, half), half)
        if held:
            own, one, two = per[n]
        else:
            own, one, two = mixed.at[n], tiles.at[n, 0], tiles.at[n, 1]
            for copy in loads[n]:
                copy.wait()
        for i in range(occ_rows):
            for jj in range(occ_rows):
                lane = (jj * occ_rows + i) * chip
                a, b = one[:, lane : lane + chip], two[:, lane : lane + chip]
                mirror = jnp.concatenate([jnp.where(odd, b, a), jnp.where(odd, a, b)], axis=1)
                below = row_energy + energy[:, lanes] - occ_energy[o * occ_rows + i] - occ_energy[first_j + jj]
                done[n, i, jj] = (own[i, jj] + mirror.astype(jnp.float32)) / below
            target = result.at[i, pl.ds(first_j, occ_rows), :, lanes]
            stores.append(pltpu.make_async_copy(done.at[n, i], target, out_sems.at[n, i]))
            stores[-1].start()
    token[...] = jnp.zeros(token.shape, token.dtype)
    for copy in stores:
        copy.wait()


def in_hbm(a):
    return pltpu.with_memory_space_constraint(a, pltpu.HBM)


def in_vmem(a):
    return pltpu.with_memory_space_constraint(a, pltpu.VMEM)


def paired(occ, vir, amplitudes, integrals, occ_fock, amp_mask, int_mask, occ_energy, vir_energy):
    occ_rows, occ_all, rows, width = amplitudes.shape
    block = width // amp_mask.shape[0]
    chip, half, pairs = CORES * rows, width // 2, occ_rows * occ_rows
    axes = ("occ", "vir")
    o, v = lax.axis_index("occ"), lax.axis_index("vir")
    devices = occ * vir
    bf16, f32 = jnp.bfloat16, jnp.float32
    params = pltpu.CompilerParams(vmem_limit_bytes=LIMIT)
    meta = jnp.stack([o, v // CORES, v % CORES]).astype(jnp.int32)
    token_shape = pltpu.VMEM((8, 128), f32)

    def swap(a, k):
        return lax.ppermute(a, axes, [(d, d ^ k) for d in range(devices)])

    def cost(moved):
        return pl.CostEstimate(flops=0, bytes_accessed=moved, transcendentals=0)

    pieces = [integrals] + [swap(integrals, 2 * k) for k in (1, 2, 3)]
    sibling = swap(amplitudes, 1)
    both = (occ_rows, occ_all, CORES, rows, width)
    x, h, wide_int = pl.pallas_call(
        functools.partial(prepare_kernel, block),
        in_specs=[SMEM, SMEM] + [HBM] * 4,
        out_specs=[VMEM] * 3,
        out_shape=[pltpu.VMEM(both, bf16), pltpu.VMEM(both, f32), pltpu.VMEM((4, rows, width), bf16)],
        scratch_shapes=[pltpu.VMEM(a.shape, a.dtype) for a in (amp_mask, int_mask)] + [pltpu.SemaphoreType.DMA((4,))],
        compiler_params=params,
        cost_estimate=cost(1024),
    )(meta, occ_fock.astype(f32), *[in_hbm(a) for a in (amplitudes, sibling, amp_mask, int_mask)])
    relayed = pl.pallas_call(
        relay_kernel,
        in_specs=[VMEM] * 5,
        out_specs=VMEM,
        out_shape=pltpu.VMEM((4, rows, width), bf16),
        compiler_params=params,
        cost_estimate=cost(1024),
    )(*[in_vmem(a) for a in pieces], in_vmem(wide_int))

    tile = (rows, pairs * chip)

    def tiles(tasks, w, token):
        args, specs = [meta, in_vmem(x), in_vmem(h)], [SMEM, VMEM, VMEM]
        shapes, outs = [], []
        for _ in tasks:
            shapes += [jax.ShapeDtypeStruct((occ_rows, occ_rows, rows, half), f32)]
            shapes += [pltpu.VMEM(tile, bf16)] * 2
            outs += [ANY, VMEM, VMEM]
        if w is None:
            args += [in_vmem(relayed), in_vmem(swap(relayed, 1))]
            shapes += [pltpu.VMEM((width, width), bf16)]
        else:
            args += [in_vmem(w), in_vmem(token)]
            shapes += [token_shape]
        made = pl.pallas_call(
            functools.partial(tile_kernel, tasks, w is None),
            in_specs=specs + [VMEM] * (len(args) - 3),
            out_specs=outs + [VMEM],
            out_shape=shapes,
            scratch_shapes=[
                pltpu.VMEM((half, pairs * chip), bf16),
                pltpu.VMEM((len(tasks), occ_rows, occ_rows, CORES, rows, half), f32),
                pltpu.SemaphoreType.DMA((len(tasks),)),
            ],
            compiler_params=params,
            cost_estimate=cost(1024),
        )(*args)
        for n, (partner, side) in enumerate(tasks):
            mixed[partner, side], sends[partner, 2 * side], sends[partner, 2 * side + 1] = made[3 * n : 3 * n + 3]
        arrived.update({(0, 0): sends[0, 0]} if (0, 0) in tasks else {})
        return made[-1]

    def start(which):
        for partner, k in which:
            arrived[partner, k] = swap(sends[partner, k], partner * vir + CORES * k)

    def finish(tasks, passed, out, token, held=False):
        args = [meta, occ_energy, vir_energy.reshape(1, width), in_vmem(token)]
        specs = [SMEM, SMEM, VMEM, VMEM]
        for partner, side in tasks:
            three = (mixed[partner, side], arrived[partner, 2 * side], arrived[partner, 2 * side + 1])
            args += [in_vmem(a) for a in three] if held else three
            specs += [VMEM if held else ANY] * 3
        shapes, outs = [], []
        aliases = {}
        for n, s in enumerate(passed):
            aliases[len(args)] = n
            args.append(in_vmem(sends[s]))
            specs.append(VMEM)
            shapes.append(pltpu.VMEM(sends[s].shape, bf16))
        if out is not None:
            aliases[len(args)] = len(passed)
            args.append(out)
            specs.append(ANY)
        shapes += [jax.ShapeDtypeStruct(amplitudes.shape, f32), token_shape]
        count = len(tasks)
        scratch = [
            pltpu.VMEM((count, occ_rows, occ_rows, rows, half), f32),
            pltpu.SemaphoreType.DMA((count, occ_rows)),
        ]
        if not held:
            scratch += [
                pltpu.VMEM((count, occ_rows, occ_rows, rows, half), f32),
                pltpu.VMEM((count, 2) + tile, bf16),
                pltpu.SemaphoreType.DMA((count, 3)),
            ]
        made = pl.pallas_call(
            functools.partial(finish_kernel, tasks, held),
            in_specs=specs,
            out_specs=[VMEM] * len(passed) + [ANY, VMEM],
            out_shape=shapes,
            scratch_shapes=scratch,
            input_output_aliases=aliases,
            compiler_params=params,
            cost_estimate=cost(1024),
        )(*args)
        for s, a in zip(passed, made):
            sends[s] = a
        return made[len(passed) :]

    arrived, mixed, sends = {}, {}, {}
    w = tiles(((0, 1),), None, None)
    start([(0, 3), (0, 2)])
    token = tiles(((1, 1), (1, 0), (0, 0), (2, 0), (3, 0), (2, 1), (3, 1)), w, sends[0, 2])
    start([(1, 3), (1, 2), (0, 1), (1, 0), (1, 1), (2, 0), (2, 1), (3, 0), (3, 1)])
    out, token = finish(((0, 1),), [(2, 3), (2, 2)], None, token)
    start([(2, 3), (2, 2)])
    out, token = finish(((1, 1), (0, 0), (1, 0)), [(3, 3), (3, 2)], out, token)
    start([(3, 3), (3, 2)])
    out, token = finish(((2, 1), (2, 0), (3, 0)), [], out, token)
    out, token = finish(((3, 1),), [], out, token, True)
    return out


def solution(mesh):
    occ, vir = mesh.shape["occ"], mesh.shape["vir"]

    def local(amplitudes, *others):
        occ_rows, _, rows, width = amplitudes.shape
        fits = (
            occ == 4
            and vir == 4 * CORES
            and rows % 16 == 0
            and width % 256 == 0
            and (occ_rows * occ_rows * CORES * rows) % 128 == 0
        )
        if fits:
            return paired(occ, vir, amplitudes, *others)
        return plain(amplitudes, *others)

    in_specs = (P("occ", None, "vir", None), P("vir", None), P(), P(), P(), P(), P())
    out_specs = P("occ", None, "vir", None)
    return jax.shard_map(local, mesh=mesh, in_specs=in_specs, out_specs=out_specs, check_vma=False)
```

time: 175 us -> 84.9 us (0.49)
  blocking collectives: 74.8 us -> 0 us
  Pallas kernels: 0 us -> 30.8 us
  starting transfers between devices: 3.77 us -> 32 us
  waiting for transfers between devices: 46.8 us -> 19.6 us
  local copies, waits for them, and re-layouts: 15.6 us -> 1.42 us
  between operations: 13.5 us -> 0.13 us
  matrix products: 12.2 us -> 0 us
  other arithmetic: 8.05 us -> 0.76 us
    all_to_all x1 -> x0, blocking collectives: 74.8 us -> none  [local(): lax.all_to_all(outgoing, 'vir', split_axis=3, concat_axis=2, tiled=True)]
    ppermute x0 -> x20, starting transfers between devices: none -> 32 us  [swap(): return lax.ppermute(a, axes, [(d, d ^ k) for d in range(devices)])]
    pallas_call x0 -> x8, Pallas kernels: none -> 30.8 us  [the longest x4 11.5 us: finish(): pl.pallas_call(functools.partial(finish_kernel, tasks, held), in_specs=sp...]
    all_to_all x1 -> x0, waiting for transfers between devices: 27.2 us -> none  [local(): lax.all_to_all(halfway, 'occ', split_axis=1, concat_axis=0, tiled=True)]
    all_gather x1 -> x0, waiting for transfers between devices: 19.6 us -> none  [local(): full_w = lax.all_gather(masked_w, 'vir', axis=0, tiled=True)]
    ppermute x0 -> x20, waiting for transfers between devices: none -> 19.6 us  [swap(): return lax.ppermute(a, axes, [(d, d ^ k) for d in range(devices)])]
    dot_general x2 -> x0, matrix products: 12.2 us -> none  [the longest x1 8.47 us: local(): ladder = jnp.dot(flat_amps, full_w, preferred_element_type=jnp.float32)]
    all_to_all x4 -> x0, local copies, waits for them, and re-layouts: 9.05 us -> none  [the longest x3 8.89 us: local(): lax.all_to_all(outgoing, 'vir', split_axis=3, concat_axis=2, tiled=True)]
  transfers between devices with their start and end apart: 2 -> 20, of which waited for: 2 -> 6; matrix products, arithmetic and copies ran while one was open for 4% -> 1% of each run, Pallas kernels for 0% -> 32%
where the time goes in v3:
time: 84.9 us; the launch traced here: 84.7 us
  starting transfers between devices  32 us (38%)
  Pallas kernels  30.8 us (36%)
  waiting for transfers between devices  19.6 us (23%)
  local copies, waits for them, and re-layouts  1.42 us (2%)
    ppermute x20, starting transfers between devices, swap(): return lax.ppermute(a, axes, [(d, d ^ k) for d in range(devices)])  32 us
    ppermute x20, waiting for transfers between devices, swap(): return lax.ppermute(a, axes, [(d, d ^ k) for d in range(devices)])  19.6 us
    pallas_call x4, Pallas kernels, finish(): pl.pallas_call(functools.partial(finish_kernel, tasks, held), in_specs=sp...  11.5 us
    pallas_call x2, Pallas kernels, tiles(): pl.pallas_call(functools.partial(tile_kernel, tasks, w is None), in_specs...  10.6 us
    pallas_call x1, Pallas kernels, paired(): pl.pallas_call(functools.partial(prepare_kernel, block), in_specs=[SMEM,...  8.6 us
  transfers between devices with their start and end apart: 20, of which 6 were waited for; matrix products, arithmetic and copies ran while one was open for 1% of the time, Pallas kernels for 32%

profile of v3, /device:TPU:0, one launch (start us, length us, event | category | flops | bytes accessed | tf_op | source)
XLA Modules:
  0.0 84.7 jit_solution(11207577416074011838)
XLA Ops:
  0.0 0.0 copy-start
  0.0 0.5 collective-permute-start
  0.5 2.6 %collective-permute-start.1 = (bf16[96,768]{1,0:T(8,128)(2,1)}, bf16[96,768]{1,0:T(8,128)(2,1)S(1)}, u32[]{:S(2)}, u32[]{:S(2)}) collective-permute-start(bf16[96,768]{1,0:T(8,128)(2,1)} %own.3), channel_id=1, source_target_pairs={{0,2},{1,3},{2,0},{3,1},{4,6},{5,7},{6,4},{7,5},{8,10},{9,11},{10,... | collective-permute-start | bytes 442376 | tf_op jit(solution)/shard_map/ppermute | solution.py:216
  3.1 2.6 %collective-permute-start.2 = (bf16[96,768]{1,0:T(8,128)(2,1)}, bf16[96,768]{1,0:T(8,128)(2,1)S(1)}, u32[]{:S(2)}, u32[]{:S(2)}) collective-permute-start(bf16[96,768]{1,0:T(8,128)(2,1)} %own.3), channel_id=1, source_target_pairs={{0,4},{1,5},{2,6},{3,7},{4,0},{5,1},{6,2},{7,3},{8,12},{9,13},{10,... | collective-permute-start | bytes 442376 | tf_op jit(solution)/shard_map/ppermute | solution.py:216
  5.7 0.0 collective-permute-start.3
  5.7 0.7 convert_element_type.3.fock
  6.4 0.1 pad_add_fusion.meta.refs_0_
  6.4 0.0 collective-permute-done.sib
  6.4 0.0 copy-start.2
  6.4 1.4 %copy-done.2 = bf16[2,8,96,768]{3,2,1,0:T(8,128)(2,1)} copy-done((bf16[2,8,96,768]{3,2,1,0:T(8,128)(2,1)}, bf16[2,8,96,768]{3,2,1,0:T(8,128)(2,1)S(1)}, u32[]{:S(2)}) %copy-start.2) | copy-done | bytes 2359320
  7.9 8.6 %shard_map.73 = (bf16[2,8,2,96,768]{4,3,2,1,0:T(8,128)(2,1)S(1)}, f32[2,8,2,96,768]{4,3,2,1,0:T(8,128)S(1)}, bf16[4,96,768]{2,1,0:T(8,128)(2,1)S(1)}) custom-call(s32[3]{0:T(128)S(1)} %pad_add_fusion.meta.refs_0_, f32[8,8]{1,0:T(8,128)S(1)} %convert_element_type.3.fock, bf16[2,8,96,768]{3,2,1,0:T(8,128)(2,1)} %own.2, bf16[2,8,96,768]{3,2,1,0:T(8,128)(2,1)} %copy-done.2, ...), custom_call_target="tpu_custom_call" | custom-call | bytes 1024 | tf_op jit(solution)/shard_map/pallas_call | solution.py:224
  16.5 0.0 collective-permute-done.1.near
  16.5 0.8 collective-permute-done.2.middle
  17.3 0.0 collective-permute-done.3.far
  17.3 0.0 copy-done
  17.3 0.1 shard_map.74.refs_3_
  17.3 0.1 collective-permute-start.4
  17.4 2.0 %collective-permute-done.4.refs_4_ = bf16[4,96,768]{2,1,0:T(8,128)(2,1)S(1)} collective-permute-done((bf16[4,96,768]{2,1,0:T(8,128)(2,1)S(1)}, bf16[4,96,768]{2,1,0:T(8,128)(2,1)S(1)}, u32[]{:S(2)}, u32[]{:S(2)}) %collective-permute-start.4) | collective-permute-done | bytes 589856 | tf_op jit(solution)/shard_map/ppermute | solution.py:216
  19.4 1.8 %shard_map.75 = (f32[2,2,96,384]{3,2,1,0:T(8,128)S(1)}, bf16[96,768]{1,0:T(8,128)(2,1)S(1)}, bf16[96,768]{1,0:T(8,128)(2,1)S(1)}, bf16[768,768]{1,0:T(8,128)(2,1)S(1)}) custom-call(s32[3]{0:T(128)S(1)} %pad_add_fusion.meta.refs_0_, bf16[2,8,2,96,768]{4,3,2,1,0:T(8,128)(2,1)S(1)} %get-tuple-element.45.refs_1_, ...), custom_call_target="tpu_custom_call" | custom-call | bytes 1024 | tf_op jit(solution)/shard_map/pallas_call | solution.py:257
  21.2 4.0 %collective-permute-start.5 = (bf16[96,768]{1,0:T(8,128)(2,1)S(1)}, bf16[96,768]{1,0:T(8,128)(2,1)S(1)}, u32[]{:S(2)}, u32[]{:S(2)}) collective-permute-start(bf16[96,768]{1,0:T(8,128)(2,1)S(1)} %get-tuple-element.49.refs_4_), channel_id=1, source_target_pairs={{0,4},{1,5},{2,6},{3,7},{4,0},{5,1},{6,2},{7,3},{8,12},{9,13},{10,... | collective-permute-start | bytes 442376 | tf_op jit(solution)/shard_map/ppermute | solution.py:216
  25.2 1.4 %collective-permute-start.6 = (bf16[96,768]{1,0:T(8,128)(2,1)S(1)}, bf16[96,768]{1,0:T(8,128)(2,1)S(1)}, u32[]{:S(2)}, u32[]{:S(2)}) collective-permute-start(bf16[96,768]{1,0:T(8,128)(2,1)S(1)} %get-tuple-element.52), channel_id=1, source_target_pairs={{0,6},{1,7},{2,4},{3,5},{4,2},{5,3},{6,0},{7,1},{8,14},{9,15},{10,... | collective-permute-start | bytes 442376 | tf_op jit(solution)/shard_map/ppermute | solution.py:216
  26.6 0.0 copy-start.3
  26.6 0.0 copy-start.1
  26.6 8.8 %shard_map.76 = (f32[2,2,96,384]{3,2,1,0:T(8,128)S(1)}, bf16[96,768]{1,0:T(8,128)(2,1)S(1)}, bf16[96,768]{1,0:T(8,128)(2,1)S(1)}, f32[2,2,96,384]{3,2,1,0:T(8,12...) custom-call(s32[3]{0:T(128)S(1)} %pad_add_fusion.meta.refs_0_, ...), custom_call_target="tpu_custom_call" | custom-call | bytes 1024 | tf_op jit(solution)/shard_map/pallas_call | solution.py:257
  35.4 1.6 %collective-permute-start.10 = (bf16[96,768]{1,0:T(8,128)(2,1)S(1)}, bf16[96,768]{1,0:T(8,128)(2,1)S(1)}, u32[]{:S(2)}, u32[]{:S(2)}) collective-permute-start(bf16[96,768]{1,0:T(8,128)(2,1)S(1)} %get-tuple-element.63), channel_id=1, source_target_pairs={{0,8},{1,9},{2,10},{3,11},{4,12},{5,13},{6,14},{7,15},{8,0},{9,1},... | collective-permute-start | bytes 442376 | tf_op jit(solution)/shard_map/ppermute | solution.py:216
  37.0 0.0 collective-permute-start.11
  37.0 3.9 %collective-permute-start.7 = (bf16[96,768]{1,0:T(8,128)(2,1)S(1)}, bf16[96,768]{1,0:T(8,128)(2,1)S(1)}, u32[]{:S(2)}, u32[]{:S(2)}) collective-permute-start(bf16[96,768]{1,0:T(8,128)(2,1)S(1)} %get-tuple-element.57), channel_id=1, source_target_pairs={{0,12},{1,13},{2,14},{3,15},{4,8},{5,9},{6,10},{7,11},{8,4},{9,5},... | collective-permute-start | bytes 442376 | tf_op jit(solution)/shard_map/ppermute | solution.py:216
  40.9 0.0 collective-permute-done.5.refs_5_
  40.9 1.3 %collective-permute-start.8 = (bf16[96,768]{1,0:T(8,128)(2,1)S(1)}, bf16[96,768]{1,0:T(8,128)(2,1)S(1)}, u32[]{:S(2)}, u32[]{:S(2)}) collective-permute-start(bf16[96,768]{1,0:T(8,128)(2,1)S(1)} %get-tuple-element.58), channel_id=1, source_target_pairs={{0,14},{1,15},{2,12},{3,13},{4,10},{5,11},{6,8},{7,9},{8,6},{9,7},... | collective-permute-start | bytes 442376 | tf_op jit(solution)/shard_map/ppermute | solution.py:216
  42.3 0.0 collective-permute-done.6.refs_6_
  42.3 0.0 collective-permute-start.9
  42.3 5.7 %collective-permute-done.10.refs_11_ = bf16[96,768]{1,0:T(8,128)(2,1)S(1)} collective-permute-done((bf16[96,768]{1,0:T(8,128)(2,1)S(1)}, bf16[96,768]{1,0:T(8,128)(2,1)S(1)}, u32[]{:S(2)}, u32[]{:S(2)}) %collective-permute-start.10) | collective-permute-done | bytes 147488 | tf_op jit(solution)/shard_map/ppermute | solution.py:216
  48.0 1.5 %collective-permute-start.14 = (bf16[96,768]{1,0:T(8,128)(2,1)S(1)}, bf16[96,768]{1,0:T(8,128)(2,1)S(1)}, u32[]{:S(2)}, u32[]{:S(2)}) collective-permute-start(bf16[96,768]{1,0:T(8,128)(2,1)S(1)} %get-tuple-element.73), channel_id=1, source_target_pairs={{0,16},{1,17},{2,18},{3,19},{4,20},{5,21},{6,22},{7,23},{8,24},{9,... | collective-permute-start | bytes 442376 | tf_op jit(solution)/shard_map/ppermute | solution.py:216
  49.5 0.0 collective-permute-done.11.refs_12_
  49.5 0.0 collective-permute-start.15
  49.5 2.2 %collective-permute-done.7.refs_5_ = bf16[96,768]{1,0:T(8,128)(2,1)S(1)} collective-permute-done((bf16[96,768]{1,0:T(8,128)(2,1)S(1)}, bf16[96,768]{1,0:T(8,128)(2,1)S(1)}, u32[]{:S(2)}, u32[]{:S(2)}) %collective-permute-start.7) | collective-permute-done | bytes 147488 | tf_op jit(solution)/shard_map/ppermute | solution.py:216
  51.7 1.6 %collective-permute-start.16 = (bf16[96,768]{1,0:T(8,128)(2,1)S(1)}, bf16[96,768]{1,0:T(8,128)(2,1)S(1)}, u32[]{:S(2)}, u32[]{:S(2)}) collective-permute-start(bf16[96,768]{1,0:T(8,128)(2,1)S(1)} %get-tuple-element.76), channel_id=1, source_target_pairs={{0,24},{1,25},{2,26},{3,27},{4,28},{5,29},{6,30},{7,31},{8,16},{9,... | collective-permute-start | bytes 442376 | tf_op jit(solution)/shard_map/ppermute | solution.py:216
  53.3 0.0 copy-done.3
  53.3 0.0 copy-done.1
  53.3 2.1 %shard_map.77 = (bf16[96,768]{1,0:T(8,128)(2,1)S(1)}, bf16[96,768]{1,0:T(8,128)(2,1)S(1)}, f32[2,8,96,768]{3,2,1,0:T(8,128)}, f32[8,128]{1,0:T(8,128)S(1)}) custom-call(s32[3]{0:T(128)S(1)} %pad_add_fusion.meta.refs_0_, f32[8]{0:T(128)S(1)} %copy-done.1, f32[1,768]{1,0:T(1,128)S(1)} %reshape.2.refs_2_, ...), custom_call_target="tpu_custom_call", output_to_operand_aliasing={{0}: (7, {}), {1}: (8, {})} | custom-call | bytes 1024 | tf_op jit(solution)/shard_map/pallas_call | solution.py:309
  55.4 0.0 collective-permute-done.8.refs_6_
  55.4 2.2 %collective-permute-start.17 = (bf16[96,768]{1,0:T(8,128)(2,1)S(1)}, bf16[96,768]{1,0:T(8,128)(2,1)S(1)}, u32[]{:S(2)}, u32[]{:S(2)}) collective-permute-start(bf16[96,768]{1,0:T(8,128)(2,1)S(1)} %get-tuple-element.77), channel_id=1, source_target_pairs={{0,26},{1,27},{2,24},{3,25},{4,30},{5,31},{6,28},{7,29},{8,18},{9,... | collective-permute-start | bytes 442376 | tf_op jit(solution)/shard_map/ppermute | solution.py:216
  57.6 0.0 collective-permute-done.9.refs_9_
  57.6 2.5 %collective-permute-start.12 = (bf16[96,768]{1,0:T(8,128)(2,1)S(1)}, bf16[96,768]{1,0:T(8,128)(2,1)S(1)}, u32[]{:S(2)}, u32[]{:S(2)}) collective-permute-start(bf16[96,768]{1,0:T(8,128)(2,1)S(1)} %get-tuple-element.70), channel_id=1, source_target_pairs={{0,20},{1,21},{2,22},{3,23},{4,16},{5,17},{6,18},{7,19},{8,28},{9,... | collective-permute-start | bytes 442376 | tf_op jit(solution)/shard_map/ppermute | solution.py:216
  60.1 5.0 %collective-permute-done.14.refs_8_ = bf16[96,768]{1,0:T(8,128)(2,1)S(1)} collective-permute-done((bf16[96,768]{1,0:T(8,128)(2,1)S(1)}, bf16[96,768]{1,0:T(8,128)(2,1)S(1)}, u32[]{:S(2)}, u32[]{:S(2)}) %collective-permute-start.14) | collective-permute-done | bytes 147488 | tf_op jit(solution)/shard_map/ppermute | solution.py:216
  65.1 4.1 %collective-permute-start.13 = (bf16[96,768]{1,0:T(8,128)(2,1)S(1)}, bf16[96,768]{1,0:T(8,128)(2,1)S(1)}, u32[]{:S(2)}, u32[]{:S(2)}) collective-permute-start(bf16[96,768]{1,0:T(8,128)(2,1)S(1)} %get-tuple-element.71), channel_id=1, source_target_pairs={{0,22},{1,23},{2,20},{3,21},{4,18},{5,19},{6,16},{7,17},{8,30},{9,... | collective-permute-start | bytes 442376 | tf_op jit(solution)/shard_map/ppermute | solution.py:216
  69.3 3.6 %shard_map.78 = (bf16[96,768]{1,0:T(8,128)(2,1)S(1)}, bf16[96,768]{1,0:T(8,128)(2,1)S(1)}, f32[2,8,96,768]{3,2,1,0:T(8,128)}, f32[8,128]{1,0:T(8,128)S(1)}) custom-call(s32[3]{0:T(128)S(1)} %pad_add_fusion.meta.refs_0_, f32[8]{0:T(128)S(1)} %copy-done.1, f32[1,768]{1,0:T(1,128)S(1)} %reshape.2.refs_2_, ...), custom_call_target="tpu_custom_call", output_to_operand_aliasing={{0}: (13, {}), {1}: (14, {}), {2}: (15, {})} | custom-call | bytes 1024 | tf_op jit(solution)/shard_map/pallas_call | solution.py:309
  72.9 0.0 collective-permute-done.15.refs_9_
  72.9 0.1 collective-permute-start.18
  73.0 0.0 collective-permute-done.16.refs_11_
  73.0 2.1 %collective-permute-start.19 = (bf16[96,768]{1,0:T(8,128)(2,1)S(1)}, bf16[96,768]{1,0:T(8,128)(2,1)S(1)}, u32[]{:S(2)}, u32[]{:S(2)}) collective-permute-start(bf16[96,768]{1,0:T(8,128)(2,1)S(1)} %get-tuple-element.82), channel_id=1, source_target_pairs={{0,30},{1,31},{2,28},{3,29},{4,26},{5,27},{6,24},{7,25},{8,22},{9,... | collective-permute-start | bytes 442376 | tf_op jit(solution)/shard_map/ppermute | solution.py:216
  75.0 0.0 collective-permute-done.17.refs_12_
  75.1 0.0 collective-permute-done.12.refs_5_
  75.1 0.0 collective-permute-done.13.refs_6_
  75.1 3.6 %shard_map.79 = (f32[2,8,96,768]{3,2,1,0:T(8,128)}, f32[8,128]{1,0:T(8,128)S(1)}) custom-call(s32[3]{0:T(128)S(1)} %pad_add_fusion.meta.refs_0_, f32[8]{0:T(128)S(1)} %copy-done.1, f32[1,768]{1,0:T(1,128)S(1)} %reshape.2.refs_2_, f32[8,128]{1,0:T(8,128)S(1)} %get-tuple-element.68.refs_3_, ...), custom_call_target="tpu_custom_call", output_to_operand_aliasing={{0}: (13, {})} | custom-call | bytes 1024 | tf_op jit(solution)/shard_map/pallas_call | solution.py:309
  78.7 3.9 %collective-permute-done.18.refs_5_ = bf16[96,768]{1,0:T(8,128)(2,1)S(1)} collective-permute-done((bf16[96,768]{1,0:T(8,128)(2,1)S(1)}, bf16[96,768]{1,0:T(8,128)(2,1)S(1)}, u32[]{:S(2)}, u32[]{:S(2)}) %collective-permute-start.18) | collective-permute-done | bytes 147488 | tf_op jit(solution)/shard_map/ppermute | solution.py:216
  82.6 0.0 collective-permute-done.19.refs_6_
  82.6 2.1 %shard_map.80 = (f32[2,8,96,768]{3,2,1,0:T(8,128)}, f32[8,128]{1,0:T(8,128)}) custom-call(s32[3]{0:T(128)S(1)} %pad_add_fusion.meta.refs_0_, f32[8]{0:T(128)S(1)} %copy-done.1, f32[1,768]{1,0:T(1,128)S(1)} %reshape.2.refs_2_, f32[8,128]{1,0:T(8,128)S(1)} %get-tuple-element.79.refs_3_, ...), custom_call_target="tpu_custom_call", output_to_operand_aliasing={{0}: (7, {})} | custom-call | bytes 1024 | tf_op jit(solution)/shard_map/pallas_call | solution.py:309
  (1 shorter events, 0.0 us)
Async XLA Ops:
  0.0 17.3 %copy-start = (bf16[96,768]{1,0:T(8,128)(2,1)S(1)}, bf16[96,768]{1,0:T(8,128)(2,1)}, u32[]{:S(2)}) copy-start(bf16[96,768]{1,0:T(8,128)(2,1)} %own.3) | copy-start | bytes 442372
  0.0 6.4 %collective-permute-start = (bf16[2,8,96,768]{3,2,1,0:T(8,128)(2,1)}, bf16[2,8,96,768]{3,2,1,0:T(8,128)(2,1)S(1)}, u32[]{:S(2)}, u32[]{:S(2)}) collective-permute-start(bf16[2,8,96,768]{3,2,1,0:T(8,128)(2,1)} %own.2), channel_id=1, source_target_pairs={{0,1},{1,0},{2,3},{3,2},{4,5},{5,4},{6,7},{7,6},{8,9},{9,8},{10,11... | collective-permute-start | bytes 7077896 | tf_op jit(solution)/shard_map/ppermute | solution.py:216
  0.5 16.0 %collective-permute-start.1 = (bf16[96,768]{1,0:T(8,128)(2,1)}, bf16[96,768]{1,0:T(8,128)(2,1)S(1)}, u32[]{:S(2)}, u32[]{:S(2)}) collective-permute-start(bf16[96,768]{1,0:T(8,128)(2,1)} %own.3), channel_id=1, source_target_pairs={{0,2},{1,3},{2,0},{3,1},{4,6},{5,7},{6,4},{7,5},{8,10},{9,11},{10,... | collective-permute-start | bytes 442376 | tf_op jit(solution)/shard_map/ppermute | solution.py:216
  3.1 14.2 %collective-permute-start.2 = (bf16[96,768]{1,0:T(8,128)(2,1)}, bf16[96,768]{1,0:T(8,128)(2,1)S(1)}, u32[]{:S(2)}, u32[]{:S(2)}) collective-permute-start(bf16[96,768]{1,0:T(8,128)(2,1)} %own.3), channel_id=1, source_target_pairs={{0,4},{1,5},{2,6},{3,7},{4,0},{5,1},{6,2},{7,3},{8,12},{9,13},{10,... | collective-permute-start | bytes 442376 | tf_op jit(solution)/shard_map/ppermute | solution.py:216
  5.7 11.6 %collective-permute-start.3 = (bf16[96,768]{1,0:T(8,128)(2,1)}, bf16[96,768]{1,0:T(8,128)(2,1)S(1)}, u32[]{:S(2)}, u32[]{:S(2)}) collective-permute-start(bf16[96,768]{1,0:T(8,128)(2,1)} %own.3), channel_id=1, source_target_pairs={{0,6},{1,7},{2,4},{3,5},{4,2},{5,3},{6,0},{7,1},{8,14},{9,15},{10,... | collective-permute-start | bytes 442376 | tf_op jit(solution)/shard_map/ppermute | solution.py:216
  6.4 1.4 %copy-start.2 = (bf16[2,8,96,768]{3,2,1,0:T(8,128)(2,1)}, bf16[2,8,96,768]{3,2,1,0:T(8,128)(2,1)S(1)}, u32[]{:S(2)}) copy-start(bf16[2,8,96,768]{3,2,1,0:T(8,128)(2,1)S(1)} %collective-permute-done.sib) | copy-start | bytes 7077892
  17.3 2.1 %collective-permute-start.4 = (bf16[4,96,768]{2,1,0:T(8,128)(2,1)S(1)}, bf16[4,96,768]{2,1,0:T(8,128)(2,1)S(1)}, u32[]{:S(2)}, u32[]{:S(2)}) collective-permute-start(bf16[4,96,768]{2,1,0:T(8,128)(2,1)S(1)} %shard_map.74.refs_3_), channel_id=1, source_target_pairs={{0,1},{1,0},{2,3},{3,2},{4,5},{5,4},{6,7},{7,6},{8,9},{9,8},{10,11... | collective-permute-start | bytes 1769480 | tf_op jit(solution)/shard_map/ppermute | solution.py:216
  21.2 19.7 %collective-permute-start.5 = (bf16[96,768]{1,0:T(8,128)(2,1)S(1)}, bf16[96,768]{1,0:T(8,128)(2,1)S(1)}, u32[]{:S(2)}, u32[]{:S(2)}) collective-permute-start(bf16[96,768]{1,0:T(8,128)(2,1)S(1)} %get-tuple-element.49.refs_4_), channel_id=1, source_target_pairs={{0,4},{1,5},{2,6},{3,7},{4,0},{5,1},{6,2},{7,3},{8,12},{9,13},{10,... | collective-permute-start | bytes 442376 | tf_op jit(solution)/shard_map/ppermute | solution.py:216
  25.2 17.0 %collective-permute-start.6 = (bf16[96,768]{1,0:T(8,128)(2,1)S(1)}, bf16[96,768]{1,0:T(8,128)(2,1)S(1)}, u32[]{:S(2)}, u32[]{:S(2)}) collective-permute-start(bf16[96,768]{1,0:T(8,128)(2,1)S(1)} %get-tuple-element.52), channel_id=1, source_target_pairs={{0,6},{1,7},{2,4},{3,5},{4,2},{5,3},{6,0},{7,1},{8,14},{9,15},{10,... | collective-permute-start | bytes 442376 | tf_op jit(solution)/shard_map/ppermute | solution.py:216
  26.6 26.7 %copy-start.3 = (f32[768]{0:T(1024)S(1)}, f32[768]{0:T(1024)}, u32[]{:S(2)}) copy-start(f32[768]{0:T(1024)} %param.13) | copy-start | bytes 9220
  26.6 26.7 %copy-start.1 = (f32[8]{0:T(128)S(1)}, f32[8]{0:T(128)}, u32[]{:S(2)}) copy-start(f32[8]{0:T(128)} %refs_1_.7) | copy-start | bytes 100
  35.4 12.6 %collective-permute-start.10 = (bf16[96,768]{1,0:T(8,128)(2,1)S(1)}, bf16[96,768]{1,0:T(8,128)(2,1)S(1)}, u32[]{:S(2)}, u32[]{:S(2)}) collective-permute-start(bf16[96,768]{1,0:T(8,128)(2,1)S(1)} %get-tuple-element.63), channel_id=1, source_target_pairs={{0,8},{1,9},{2,10},{3,11},{4,12},{5,13},{6,14},{7,15},{8,0},{9,1},... | collective-permute-start | bytes 442376 | tf_op jit(solution)/shard_map/ppermute | solution.py:216
  37.0 12.5 %collective-permute-start.11 = (bf16[96,768]{1,0:T(8,128)(2,1)S(1)}, bf16[96,768]{1,0:T(8,128)(2,1)S(1)}, u32[]{:S(2)}, u32[]{:S(2)}) collective-permute-start(bf16[96,768]{1,0:T(8,128)(2,1)S(1)} %get-tuple-element.64), channel_id=1, source_target_pairs={{0,10},{1,11},{2,8},{3,9},{4,14},{5,15},{6,12},{7,13},{8,2},{9,3},... | collective-permute-start | bytes 442376 | tf_op jit(solution)/shard_map/ppermute | solution.py:216
  37.0 14.7 %collective-permute-start.7 = (bf16[96,768]{1,0:T(8,128)(2,1)S(1)}, bf16[96,768]{1,0:T(8,128)(2,1)S(1)}, u32[]{:S(2)}, u32[]{:S(2)}) collective-permute-start(bf16[96,768]{1,0:T(8,128)(2,1)S(1)} %get-tuple-element.57), channel_id=1, source_target_pairs={{0,12},{1,13},{2,14},{3,15},{4,8},{5,9},{6,10},{7,11},{8,4},{9,5},... | collective-permute-start | bytes 442376 | tf_op jit(solution)/shard_map/ppermute | solution.py:216
  40.9 14.5 %collective-permute-start.8 = (bf16[96,768]{1,0:T(8,128)(2,1)S(1)}, bf16[96,768]{1,0:T(8,128)(2,1)S(1)}, u32[]{:S(2)}, u32[]{:S(2)}) collective-permute-start(bf16[96,768]{1,0:T(8,128)(2,1)S(1)} %get-tuple-element.58), channel_id=1, source_target_pairs={{0,14},{1,15},{2,12},{3,13},{4,10},{5,11},{6,8},{7,9},{8,6},{9,7},... | collective-permute-start | bytes 442376 | tf_op jit(solution)/shard_map/ppermute | solution.py:216
  42.3 15.3 %collective-permute-start.9 = (bf16[96,768]{1,0:T(8,128)(2,1)S(1)}, bf16[96,768]{1,0:T(8,128)(2,1)S(1)}, u32[]{:S(2)}, u32[]{:S(2)}) collective-permute-start(bf16[96,768]{1,0:T(8,128)(2,1)S(1)} %get-tuple-element.61), channel_id=1, source_target_pairs={{0,2},{1,3},{2,0},{3,1},{4,6},{5,7},{6,4},{7,5},{8,10},{9,11},{10,... | collective-permute-start | bytes 442376 | tf_op jit(solution)/shard_map/ppermute | solution.py:216
  48.0 17.1 %collective-permute-start.14 = (bf16[96,768]{1,0:T(8,128)(2,1)S(1)}, bf16[96,768]{1,0:T(8,128)(2,1)S(1)}, u32[]{:S(2)}, u32[]{:S(2)}) collective-permute-start(bf16[96,768]{1,0:T(8,128)(2,1)S(1)} %get-tuple-element.73), channel_id=1, source_target_pairs={{0,16},{1,17},{2,18},{3,19},{4,20},{5,21},{6,22},{7,23},{8,24},{9,... | collective-permute-start | bytes 442376 | tf_op jit(solution)/shard_map/ppermute | solution.py:216
  49.5 23.4 %collective-permute-start.15 = (bf16[96,768]{1,0:T(8,128)(2,1)S(1)}, bf16[96,768]{1,0:T(8,128)(2,1)S(1)}, u32[]{:S(2)}, u32[]{:S(2)}) collective-permute-start(bf16[96,768]{1,0:T(8,128)(2,1)S(1)} %get-tuple-element.74), channel_id=1, source_target_pairs={{0,18},{1,19},{2,16},{3,17},{4,22},{5,23},{6,20},{7,21},{8,26},{9,... | collective-permute-start | bytes 442376 | tf_op jit(solution)/shard_map/ppermute | solution.py:216
  51.7 21.3 %collective-permute-start.16 = (bf16[96,768]{1,0:T(8,128)(2,1)S(1)}, bf16[96,768]{1,0:T(8,128)(2,1)S(1)}, u32[]{:S(2)}, u32[]{:S(2)}) collective-permute-start(bf16[96,768]{1,0:T(8,128)(2,1)S(1)} %get-tuple-element.76), channel_id=1, source_target_pairs={{0,24},{1,25},{2,26},{3,27},{4,28},{5,29},{6,30},{7,31},{8,16},{9,... | collective-permute-start | bytes 442376 | tf_op jit(solution)/shard_map/ppermute | solution.py:216
  55.4 19.6 %collective-permute-start.17 = (bf16[96,768]{1,0:T(8,128)(2,1)S(1)}, bf16[96,768]{1,0:T(8,128)(2,1)S(1)}, u32[]{:S(2)}, u32[]{:S(2)}) collective-permute-start(bf16[96,768]{1,0:T(8,128)(2,1)S(1)} %get-tuple-element.77), channel_id=1, source_target_pairs={{0,26},{1,27},{2,24},{3,25},{4,30},{5,31},{6,28},{7,29},{8,18},{9,... | collective-permute-start | bytes 442376 | tf_op jit(solution)/shard_map/ppermute | solution.py:216
  57.6 17.5 %collective-permute-start.12 = (bf16[96,768]{1,0:T(8,128)(2,1)S(1)}, bf16[96,768]{1,0:T(8,128)(2,1)S(1)}, u32[]{:S(2)}, u32[]{:S(2)}) collective-permute-start(bf16[96,768]{1,0:T(8,128)(2,1)S(1)} %get-tuple-element.70), channel_id=1, source_target_pairs={{0,20},{1,21},{2,22},{3,23},{4,16},{5,17},{6,18},{7,19},{8,28},{9,... | collective-permute-start | bytes 442376 | tf_op jit(solution)/shard_map/ppermute | solution.py:216
  65.1 9.9 %collective-permute-start.13 = (bf16[96,768]{1,0:T(8,128)(2,1)S(1)}, bf16[96,768]{1,0:T(8,128)(2,1)S(1)}, u32[]{:S(2)}, u32[]{:S(2)}) collective-permute-start(bf16[96,768]{1,0:T(8,128)(2,1)S(1)} %get-tuple-element.71), channel_id=1, source_target_pairs={{0,22},{1,23},{2,20},{3,21},{4,18},{5,19},{6,16},{7,17},{8,30},{9,... | collective-permute-start | bytes 442376 | tf_op jit(solution)/shard_map/ppermute | solution.py:216
  72.9 9.7 %collective-permute-start.18 = (bf16[96,768]{1,0:T(8,128)(2,1)S(1)}, bf16[96,768]{1,0:T(8,128)(2,1)S(1)}, u32[]{:S(2)}, u32[]{:S(2)}) collective-permute-start(bf16[96,768]{1,0:T(8,128)(2,1)S(1)} %get-tuple-element.81), channel_id=1, source_target_pairs={{0,28},{1,29},{2,30},{3,31},{4,24},{5,25},{6,26},{7,27},{8,20},{9,... | collective-permute-start | bytes 442376 | tf_op jit(solution)/shard_map/ppermute | solution.py:216
  73.0 9.6 %collective-permute-start.19 = (bf16[96,768]{1,0:T(8,128)(2,1)S(1)}, bf16[96,768]{1,0:T(8,128)(2,1)S(1)}, u32[]{:S(2)}, u32[]{:S(2)}) collective-permute-start(bf16[96,768]{1,0:T(8,128)(2,1)S(1)} %get-tuple-element.82), channel_id=1, source_target_pairs={{0,30},{1,31},{2,28},{3,29},{4,26},{5,27},{6,24},{7,25},{8,22},{9,... | collective-permute-start | bytes 442376 | tf_op jit(solution)/shard_map/ppermute | solution.py:216

commit v4 on v3

v4 whole, which is shorter than its diff:
```python
import functools

import jax
import jax.numpy as jnp
from jax import lax
from jax.experimental import pallas as pl
from jax.experimental.pallas import tpu as pltpu
from jax.sharding import PartitionSpec as P

CORES = 2
LIMIT = 12 * 1024 * 1024
VMEM = pl.BlockSpec(memory_space=pltpu.VMEM)
SMEM = pl.BlockSpec(memory_space=pltpu.SMEM)
ANY = pl.BlockSpec(memory_space=pl.ANY)
HBM = pl.BlockSpec(memory_space=pltpu.HBM)


def expand_rows(mask, first_block, blocks, block):
    rows_here = lax.dynamic_slice_in_dim(mask, first_block, blocks, 0)
    return jnp.repeat(jnp.repeat(rows_here, block, axis=0), block, axis=1).astype(jnp.bfloat16)


def plain(amplitudes, integrals, occ_fock, amp_mask, int_mask, occ_energy, vir_energy):
    occ_rows, occ_all, vir_rows, vir_all = amplitudes.shape
    block = vir_all // amp_mask.shape[0]
    vir_start = lax.axis_index("vir") * vir_rows
    occ_start = lax.axis_index("occ") * occ_rows
    blocks = vir_rows // block
    first_block = vir_start // block
    masked = amplitudes * expand_rows(amp_mask, first_block, blocks, block)[None, None]
    masked_w = integrals * expand_rows(int_mask, first_block, blocks, block)
    flat_amps = masked.reshape(-1, vir_all)
    full_w = lax.all_gather(masked_w, "vir", axis=0, tiled=True)
    ladder = jnp.dot(flat_amps, full_w, preferred_element_type=jnp.float32)
    ladder = ladder.reshape(occ_rows, occ_all, vir_rows, vir_all)
    holes = jnp.einsum("ikab,kj->ijab", masked, occ_fock, preferred_element_type=jnp.float32)
    mixed = ladder + holes
    outgoing = mixed.astype(jnp.bfloat16)
    halfway = lax.all_to_all(outgoing, "vir", split_axis=3, concat_axis=2, tiled=True)
    arrived = lax.all_to_all(halfway, "occ", split_axis=1, concat_axis=0, tiled=True)
    mirrored = arrived.transpose(1, 0, 3, 2).astype(jnp.float32)
    vir_here = lax.dynamic_slice_in_dim(vir_energy, vir_start, vir_rows, 0)
    occ_here = lax.dynamic_slice_in_dim(occ_energy, occ_start, occ_rows, 0)
    denominator = (
        vir_here[None, None, :, None]
        + vir_energy[None, None, None, :]
        - occ_here[:, None, None, None]
        - occ_energy[None, :, None, None]
    )
    return (mixed + mirrored) / denominator


def one_hot(shape, row_of, column_of):
    rows = lax.broadcasted_iota(jnp.int32, shape, 0)
    columns = lax.broadcasted_iota(jnp.int32, shape, 1)
    return (row_of(rows) == column_of(columns)).astype(jnp.float32).astype(jnp.bfloat16)


def prepare_kernel(block, meta, fock, own, sib, amp_flags, int_flags, x, h, wide_int, amp_mask, int_mask, sems):
    occ_rows, occ_all, _, rows, width = x.shape
    blocks = amp_mask.shape[0]
    z, core = meta[1], meta[2]
    sources = ((own, core), (sib, 1 - core))
    loads = [pltpu.make_async_copy(source, x.at[:, :, at], sems.at[n]) for n, (source, at) in enumerate(sources)]
    flags = [pltpu.make_async_copy(amp_flags, amp_mask, sems.at[2]), pltpu.make_async_copy(int_flags, int_mask, sems.at[3])]
    for load in flags + loads:
        load.start()
    for load in flags:
        load.wait()
    spread = one_hot((blocks, width), lambda r: r, lambda c: c // block)

    def wide(mask, first):
        rows_of = one_hot((rows, blocks), lambda r: (r + first) // block, lambda c: c)
        tall = jnp.dot(rows_of, mask[...].astype(jnp.float32).astype(jnp.bfloat16), preferred_element_type=jnp.float32)
        return jnp.dot(tall.astype(jnp.bfloat16), spread, preferred_element_type=jnp.float32).astype(jnp.bfloat16)

    for k in range(4):
        wide_int[k] = wide(int_mask, ((z ^ k) * CORES + core) * rows)
    part = width // 2
    for n, (_, at) in enumerate(sources):
        live = wide(amp_mask, (z * CORES + at) * rows)
        loads[n].wait()
        for i in range(occ_rows):
            for j in range(occ_all):
                x[i, j, at] = x[i, j, at] * live

        def step(s, carry, at=at):
            row = pl.multiple_of((s // 2) * 16, 16)
            columns = pl.ds(pl.multiple_of((s % 2) * part, part), part)
            for i in range(occ_rows):
                amps = [x[i, k, at, pl.ds(row, 16), columns].astype(jnp.float32) for k in range(occ_all)]
                for j in range(occ_all):
                    total = amps[0] * fock[0, j]
                    for k in range(1, occ_all):
                        total = total + amps[k] * fock[k, j]
                    h[i, j, at, pl.ds(row, 16), columns] = total
            return carry

        lax.fori_loop(0, 2 * rows // 16, step, 0)


def relay_kernel(own, near, middle, far, mask, out):
    for k, piece in enumerate((own, near, middle, far)):
        out[k] = piece[...] * mask[k]


def make_tiles(makes, r):
    meta, x, h, w, flipped, own, sems = (r[name] for name in ("meta", "x", "h", "w", "flipped", "own", "own_sems"))
    _, occ_rows, _, _, rows, half = own.shape
    width, chip, pairs = x.shape[-1], CORES * rows, occ_rows * occ_rows
    o, z, core = meta[0], meta[1], meta[2]
    copies = []
    for n, (partner, side) in enumerate(makes):
        first_j = (o ^ partner) * occ_rows
        columns = pl.ds(pl.multiple_of(((z // 2) ^ side) * half, half), half)
        ladder = jnp.dot(
            x[:, pl.ds(first_j, occ_rows)].reshape(pairs * chip, width), w[:, columns], preferred_element_type=jnp.float32
        )
        for i in range(occ_rows):
            for jj in range(occ_rows):
                m = i * occ_rows + jj
                mixed = ladder[m * chip : (m + 1) * chip] + h[i, first_j + jj, :, :, columns].reshape(chip, half)
                own[n, i, jj] = mixed.reshape(CORES, rows, half)
                flipped[:, m * chip : (m + 1) * chip] = mixed.astype(jnp.bfloat16).T
        copies.append(pltpu.make_async_copy(own.at[n, :, :, core], r["mixed", partner, side], sems.at[n]))
        copies[-1].start()
        for s in (0, 1):
            start = pl.multiple_of((((z & 1) ^ s) * CORES + core) * rows, rows)
            r["tile", partner, 2 * side + s][...] = flipped[pl.ds(start, rows), :]
    return copies


def finish_tiles(ends, r):
    meta, occ_energy, energy, done, sems = (r[name] for name in ("meta", "occ_energy", "energy", "done", "done_sems"))
    _, occ_rows, _, rows, half = done.shape
    width, chip = energy.shape[1], CORES * rows
    o, z, core = meta[0], meta[1], meta[2]
    odd = (z & 1) == 1
    place = (z * CORES + core) * rows
    mine = lax.broadcasted_iota(jnp.int32, (rows, width), 1) == lax.broadcasted_iota(jnp.int32, (rows, width), 0) + place
    row_energy = jnp.sum(jnp.where(mine, energy[...], 0.0), axis=1, keepdims=True)
    stores = []
    for n, (partner, side) in enumerate(ends):
        first_j = (o ^ partner) * occ_rows
        lanes = pl.ds(pl.multiple_of(((z // 2) ^ side) * half, half), half)
        own, one, two = (r["got", partner, side, c] for c in range(3))
        for i in range(occ_rows):
            for jj in range(occ_rows):
                lane = (jj * occ_rows + i) * chip
                a, b = one[:, lane : lane + chip], two[:, lane : lane + chip]
                mirror = jnp.concatenate([jnp.where(odd, b, a), jnp.where(odd, a, b)], axis=1)
                below = row_energy + energy[:, lanes] - occ_energy[o * occ_rows + i] - occ_energy[first_j + jj]
                done[n, i, jj] = (own[i, jj] + mirror.astype(jnp.float32)) / below
            target = r["result"].at[i, pl.ds(first_j, occ_rows), :, lanes]
            stores.append(pltpu.make_async_copy(done.at[n, i], target, sems.at[n, i]))
            stores[-1].start()
    return stores


def step_kernel(names, makes, ends, *refs):
    r = dict(zip(names, refs, strict=True))
    if "mine" in r:
        z, core = r["meta"][1], r["meta"][2]
        rows = r["mine"].shape[1]
        for k in range(4):
            for piece, at in ((r["mine"], core), (r["theirs"], 1 - core)):
                r["w"][pl.ds(pl.multiple_of(((z ^ k) * CORES + at) * rows, rows), rows), :] = piece[k]
    copies = make_tiles(makes, r) if makes else []
    copies += finish_tiles(ends, r) if ends else []
    r["token"][...] = jnp.zeros(r["token"].shape, r["token"].dtype)
    for copy in copies:
        copy.wait()


def in_hbm(a):
    return pltpu.with_memory_space_constraint(a, pltpu.HBM)


def in_vmem(a):
    return pltpu.with_memory_space_constraint(a, pltpu.VMEM)


def paired(occ, vir, amplitudes, integrals, occ_fock, amp_mask, int_mask, occ_energy, vir_energy):
    occ_rows, occ_all, rows, width = amplitudes.shape
    block = width // amp_mask.shape[0]
    chip, half, pairs = CORES * rows, width // 2, occ_rows * occ_rows
    axes = ("occ", "vir")
    o, v = lax.axis_index("occ"), lax.axis_index("vir")
    devices = occ * vir
    bf16, f32 = jnp.bfloat16, jnp.float32
    params = pltpu.CompilerParams(vmem_limit_bytes=LIMIT)
    meta = jnp.stack([o, v // CORES, v % CORES]).astype(jnp.int32)
    energy = vir_energy.reshape(1, width)
    tile = (rows, pairs * chip)

    def swap(a, k):
        return lax.ppermute(a, axes, [(d, d ^ k) for d in range(devices)])

    pieces = [integrals] + [swap(integrals, CORES * k) for k in (1, 2, 3)]
    sibling = swap(amplitudes, 1)
    both = (occ_rows, occ_all, CORES, rows, width)
    x, h, wide_int = pl.pallas_call(
        functools.partial(prepare_kernel, block),
        in_specs=[SMEM, SMEM] + [HBM] * 4,
        out_specs=[VMEM] * 3,
        out_shape=[pltpu.VMEM(both, bf16), pltpu.VMEM(both, f32), pltpu.VMEM((4, rows, width), bf16)],
        scratch_shapes=[pltpu.VMEM(a.shape, a.dtype) for a in (amp_mask, int_mask)] + [pltpu.SemaphoreType.DMA((4,))],
        compiler_params=params,
    )(meta, occ_fock.astype(f32), *[in_hbm(a) for a in (amplitudes, sibling, amp_mask, int_mask)])
    relayed = pl.pallas_call(
        relay_kernel,
        in_specs=[VMEM] * 5,
        out_specs=VMEM,
        out_shape=pltpu.VMEM((4, rows, width), bf16),
        compiler_params=params,
    )(*[in_vmem(a) for a in pieces], in_vmem(wide_int))

    sends, arrived, mixed, kept = {}, {}, {}, {}

    def step(makes=(), ends=(), passed=()):
        ins, outs, scratch, aliases = [("meta", meta, SMEM)], [], [], {}
        if makes:
            ins += [("x", in_vmem(x), VMEM), ("h", in_vmem(h), VMEM)]
            if "w" in kept:
                ins.append(("w", in_vmem(kept["w"]), VMEM))
            else:
                ins += [("mine", in_vmem(relayed), VMEM), ("theirs", in_vmem(swap(relayed, 1)), VMEM)]
                outs.append(("w", pltpu.VMEM((width, width), bf16), VMEM))
            for partner, side in makes:
                outs.append((("mixed", partner, side), jax.ShapeDtypeStruct((occ_rows, occ_rows, rows, half), f32), ANY))
                outs += [(("tile", partner, 2 * side + s), pltpu.VMEM(tile, bf16), VMEM) for s in (0, 1)]
            scratch += [
                ("flipped", pltpu.VMEM((half, pairs * chip), bf16)),
                ("own", pltpu.VMEM((len(makes), occ_rows, occ_rows, CORES, rows, half), f32)),
                ("own_sems", pltpu.SemaphoreType.DMA((len(makes),))),
            ]
        if ends:
            count = len(ends)
            ins += [("occ_energy", occ_energy, SMEM), ("energy", energy, VMEM)]
            for partner, side in ends:
                got = (mixed[partner, side], arrived[partner, 2 * side], arrived[partner, 2 * side + 1])
                for c, a in enumerate(got):
                    ins.append((("got", partner, side, c), in_vmem(a), VMEM))
            if "result" in kept:
                aliases["partial"] = "result"
                ins.append(("partial", kept["result"], ANY))
            outs.append(("result", jax.ShapeDtypeStruct(amplitudes.shape, f32), ANY))
            scratch += [
                ("done", pltpu.VMEM((count, occ_rows, occ_rows, rows, half), f32)),
                ("done_sems", pltpu.SemaphoreType.DMA((count, occ_rows))),
            ]
        for s in passed:
            aliases["pass", s] = ("passed", s)
            ins.append((("pass", s), in_vmem(sends[s]), VMEM))
            outs.append((("passed", s), pltpu.VMEM(sends[s].shape, bf16), VMEM))
        if "token" in kept:
            ins.append(("before", in_vmem(kept["token"]), VMEM))
        outs.append(("token", pltpu.VMEM((8, 128), f32), VMEM))
        in_names, out_names = [name for name, _, _ in ins], [name for name, _, _ in outs]
        made = pl.pallas_call(
            functools.partial(
                step_kernel, in_names + out_names + [name for name, _ in scratch], tuple(makes), tuple(ends)
            ),
            in_specs=[spec for _, _, spec in ins],
            out_specs=[spec for _, _, spec in outs],
            out_shape=[shape for _, shape, _ in outs],
            scratch_shapes=[shape for _, shape in scratch],
            input_output_aliases={in_names.index(a): out_names.index(b) for a, b in aliases.items()},
            compiler_params=params,
        )(*[a for _, a, _ in ins])
        for name, a in zip(out_names, made, strict=True):
            if name[0] == "mixed":
                mixed[name[1:]] = a
            elif name[0] == "tile":
                sends[name[1:]] = a
            elif name[0] == "passed":
                sends[name[1]] = a
            else:
                kept[name] = a

    def start(which):
        for partner, k in which:
            arrived[partner, k] = swap(sends[partner, k], partner * vir + CORES * k) if partner or k else sends[0, 0]

    step(makes=[(0, 1)])
    start([(0, 3), (0, 2)])
    step(makes=[(1, 1), (0, 0), (1, 0), (2, 0)])
    start([(1, 3), (1, 2), (0, 0), (0, 1), (1, 0), (1, 1), (2, 0)])
    step(makes=[(2, 1), (3, 1), (3, 0)], ends=[(1, 0), (0, 1)], passed=[(2, 1)])
    start([(2, 3), (2, 2), (2, 1), (3, 0)])
    step(ends=[(0, 0), (1, 1)], passed=[(3, 2), (3, 1)])
    start([(3, 2), (3, 1)])
    step(ends=[(2, 1), (2, 0)], passed=[(3, 3)])
    start([(3, 3)])
    step(ends=[(3, 1), (3, 0)])
    return kept["result"]


def solution(mesh):
    occ, vir = mesh.shape["occ"], mesh.shape["vir"]

    def local(amplitudes, *others):
        occ_rows, _, rows, width = amplitudes.shape
        fits = (
            occ == 4
            and vir == 4 * CORES
            and rows % 16 == 0
            and width % 256 == 0
            and (occ_rows * occ_rows * CORES * rows) % 128 == 0
        )
        if fits:
            return paired(occ, vir, amplitudes, *others)
        return plain(amplitudes, *others)

    in_specs = (P("occ", None, "vir", None), P("vir", None), P(), P(), P(), P(), P())
    out_specs = P("occ", None, "vir", None)
    return jax.shard_map(local, mesh=mesh, in_specs=in_specs, out_specs=out_specs, check_vma=False)
```

time: 84.9 us -> 79.3 us (0.934)
  waiting for transfers between devices: 19.6 us -> 10.8 us
  starting transfers between devices: 32 us -> 39.1 us
  Pallas kernels: 30.8 us -> 26.9 us
    ppermute x20, waiting for transfers between devices: 19.6 us -> 10.8 us  [swap(): return lax.ppermute(a, axes, [(d, d ^ k) for d in range(devices)])]
    ppermute x20, starting transfers between devices: 32 us -> 39.1 us  [swap(): return lax.ppermute(a, axes, [(d, d ^ k) for d in range(devices)])]
    pallas_call x6, Pallas kernels: 22.1 us -> 18.2 us  [step(): pl.pallas_call(functools.partial(step_kernel, in_names + out_names + [nam...]
  transfers between devices with their start and end apart: 20 -> 20, of which waited for: 6 -> 8; matrix products, arithmetic and copies ran while one was open for 1% -> 1% of each run, Pallas kernels for 32% -> 29%
where the time goes in v4:
time: 79.3 us; the launch traced here: 79.1 us
  starting transfers between devices  39.1 us (49%)
  Pallas kernels  26.9 us (34%)
  waiting for transfers between devices  10.8 us (14%)
  local copies, waits for them, and re-layouts  1.42 us (2%)
    ppermute x20, starting transfers between devices, swap(): return lax.ppermute(a, axes, [(d, d ^ k) for d in range(devices)])  39.1 us
    pallas_call x6, Pallas kernels, step(): pl.pallas_call(functools.partial(step_kernel, in_names + out_names + [nam...  18.2 us
    ppermute x20, waiting for transfers between devices, swap(): return lax.ppermute(a, axes, [(d, d ^ k) for d in range(devices)])  10.8 us
    pallas_call x1, Pallas kernels, paired(): pl.pallas_call(functools.partial(prepare_kernel, block), in_specs=[SMEM,...  8.6 us
  transfers between devices with their start and end apart: 20, of which 8 were waited for; matrix products, arithmetic and copies ran while one was open for 1% of the time, Pallas kernels for 29%

profile of v4, /device:TPU:0, one launch (start us, length us, event | category | flops | bytes accessed | tf_op | source)
XLA Modules:
  0.0 79.1 jit_solution(5866936858459802736)
XLA Ops:
  0.0 0.0 copy-start
  0.0 0.5 collective-permute-start
  0.5 3.6 %collective-permute-start.2 = (bf16[96,768]{1,0:T(8,128)(2,1)}, bf16[96,768]{1,0:T(8,128)(2,1)S(1)}, u32[]{:S(2)}, u32[]{:S(2)}) collective-permute-start(bf16[96,768]{1,0:T(8,128)(2,1)} %own.3), channel_id=1, source_target_pairs={{0,4},{1,5},{2,6},{3,7},{4,0},{5,1},{6,2},{7,3},{8,12},{9,13},{10,... | collective-permute-start | bytes 442376 | tf_op jit(solution)/shard_map/ppermute | solution.py:197
  4.1 1.6 %collective-permute-start.1 = (bf16[96,768]{1,0:T(8,128)(2,1)}, bf16[96,768]{1,0:T(8,128)(2,1)S(1)}, u32[]{:S(2)}, u32[]{:S(2)}) collective-permute-start(bf16[96,768]{1,0:T(8,128)(2,1)} %own.3), channel_id=1, source_target_pairs={{0,2},{1,3},{2,0},{3,1},{4,6},{5,7},{6,4},{7,5},{8,10},{9,11},{10,... | collective-permute-start | bytes 442376 | tf_op jit(solution)/shard_map/ppermute | solution.py:197
  5.7 0.0 collective-permute-start.3
  5.7 0.7 convert_element_type.3.fock
  6.4 0.1 pad_add_fusion.meta.refs_0_
  6.4 0.0 collective-permute-done.sib
  6.4 0.0 copy-start.2
  6.4 1.4 %copy-done.2 = bf16[2,8,96,768]{3,2,1,0:T(8,128)(2,1)} copy-done((bf16[2,8,96,768]{3,2,1,0:T(8,128)(2,1)}, bf16[2,8,96,768]{3,2,1,0:T(8,128)(2,1)S(1)}, u32[]{:S(2)}) %copy-start.2) | copy-done | bytes 2359320
  7.9 8.6 %shard_map.73 = (bf16[2,8,2,96,768]{4,3,2,1,0:T(8,128)(2,1)S(1)}, f32[2,8,2,96,768]{4,3,2,1,0:T(8,128)S(1)}, bf16[4,96,768]{2,1,0:T(8,128)(2,1)S(1)}) custom-call(s32[3]{0:T(128)S(1)} %pad_add_fusion.meta.refs_0_, f32[8,8]{1,0:T(8,128)S(1)} %convert_element_type.3.fock, bf16[2,8,96,768]{3,2,1,0:T(8,128)(2,1)} %own.2, bf16[2,8,96,768]{3,2,1,0:T(8,128)(2,1)} %copy-done.2, ...), custom_call_target="tpu_custom_call" | custom-call | tf_op jit(solution)/shard_map/pallas_call | solution.py:202
  16.5 0.0 collective-permute-done.2.middle
  16.5 0.0 collective-permute-done.1.near
  16.5 0.0 collective-permute-done.3.far
  16.5 0.0 copy-done
  16.5 0.1 shard_map.74.refs_3_
  16.6 0.1 collective-permute-start.4
  16.7 2.0 %collective-permute-done.4.refs_4_ = bf16[4,96,768]{2,1,0:T(8,128)(2,1)S(1)} collective-permute-done((bf16[4,96,768]{2,1,0:T(8,128)(2,1)S(1)}, bf16[4,96,768]{2,1,0:T(8,128)(2,1)S(1)}, u32[]{:S(2)}, u32[]{:S(2)}) %collective-permute-start.4) | collective-permute-done | bytes 589856 | tf_op jit(solution)/shard_map/ppermute | solution.py:197
  18.6 1.8 %shard_map.75 = (bf16[768,768]{1,0:T(8,128)(2,1)S(1)}, f32[2,2,96,384]{3,2,1,0:T(8,128)S(1)}, bf16[96,768]{1,0:T(8,128)(2,1)S(1)}, bf16[96,768]{1,0:T(8,128)(2,1)S(1)}, f32[8,128]{1,0:T(8,128)S(1)}) custom-call(s32[3]{0:T(128)S(1)} %pad_add_fusion.meta.refs_0_, bf16[2,8,2,96,768]{4,3,2,1,0:T(8,128)(2,1)S(1)} %get-tuple-element.46.refs_1_, ...), custom_call_target="tpu_custom_call" | custom-call | tf_op jit(solution)/shard_map/pallas_call | solution.py:260
  20.5 4.4 %collective-permute-start.7 = (bf16[96,768]{1,0:T(8,128)(2,1)S(1)}, bf16[96,768]{1,0:T(8,128)(2,1)S(1)}, u32[]{:S(2)}, u32[]{:S(2)}) collective-permute-start(bf16[96,768]{1,0:T(8,128)(2,1)S(1)} %get-tuple-element.55), channel_id=1, source_target_pairs={{0,4},{1,5},{2,6},{3,7},{4,0},{5,1},{6,2},{7,3},{8,12},{9,13},{10,... | collective-permute-start | bytes 442376 | tf_op jit(solution)/shard_map/ppermute | solution.py:197
  24.9 0.6 collective-permute-start.8
  25.5 0.0 copy-start.3
  25.5 0.0 copy-start.1
  25.5 5.3 %shard_map.76 = (f32[2,2,96,384]{3,2,1,0:T(8,128)S(1)}, bf16[96,768]{1,0:T(8,128)(2,1)S(1)}, bf16[96,768]{1,0:T(8,128)(2,1)S(1)}, f32[2,2,96,384]{3,2,1,0:T(8,12...) custom-call(s32[3]{0:T(128)S(1)} %pad_add_fusion.meta.refs_0_, ...), custom_call_target="tpu_custom_call" | custom-call | tf_op jit(solution)/shard_map/pallas_call | solution.py:260
  30.7 1.6 %collective-permute-start.5 = (bf16[96,768]{1,0:T(8,128)(2,1)S(1)}, bf16[96,768]{1,0:T(8,128)(2,1)S(1)}, u32[]{:S(2)}, u32[]{:S(2)}) collective-permute-start(bf16[96,768]{1,0:T(8,128)(2,1)S(1)} %get-tuple-element.52), channel_id=1, source_target_pairs={{0,8},{1,9},{2,10},{3,11},{4,12},{5,13},{6,14},{7,15},{8,0},{9,1},... | collective-permute-start | bytes 442376 | tf_op jit(solution)/shard_map/ppermute | solution.py:197
  32.3 0.1 collective-permute-start.6
  32.4 1.9 %collective-permute-start.9 = (bf16[96,768]{1,0:T(8,128)(2,1)S(1)}, bf16[96,768]{1,0:T(8,128)(2,1)S(1)}, u32[]{:S(2)}, u32[]{:S(2)}) collective-permute-start(bf16[96,768]{1,0:T(8,128)(2,1)S(1)} %get-tuple-element.62), channel_id=1, source_target_pairs={{0,2},{1,3},{2,0},{3,1},{4,6},{5,7},{6,4},{7,5},{8,10},{9,11},{10,... | collective-permute-start | bytes 442376 | tf_op jit(solution)/shard_map/ppermute | solution.py:197
  34.3 1.4 %collective-permute-done.7.refs_10_ = bf16[96,768]{1,0:T(8,128)(2,1)S(1)} collective-permute-done((bf16[96,768]{1,0:T(8,128)(2,1)S(1)}, bf16[96,768]{1,0:T(8,128)(2,1)S(1)}, u32[]{:S(2)}, u32[]{:S(2)}) %collective-permute-start.7) | collective-permute-done | bytes 147488 | tf_op jit(solution)/shard_map/ppermute | solution.py:197
  35.7 1.3 %collective-permute-start.10 = (bf16[96,768]{1,0:T(8,128)(2,1)S(1)}, bf16[96,768]{1,0:T(8,128)(2,1)S(1)}, u32[]{:S(2)}, u32[]{:S(2)}) collective-permute-start(bf16[96,768]{1,0:T(8,128)(2,1)S(1)} %get-tuple-element.64), channel_id=1, source_target_pairs={{0,12},{1,13},{2,14},{3,15},{4,8},{5,9},{6,10},{7,11},{8,4},{9,5},... | collective-permute-start | bytes 442376 | tf_op jit(solution)/shard_map/ppermute | solution.py:197
  37.0 0.0 copy-done.3
  37.0 0.0 collective-permute-done.8.refs_11_
  37.0 2.2 %collective-permute-start.11 = (bf16[96,768]{1,0:T(8,128)(2,1)S(1)}, bf16[96,768]{1,0:T(8,128)(2,1)S(1)}, u32[]{:S(2)}, u32[]{:S(2)}) collective-permute-start(bf16[96,768]{1,0:T(8,128)(2,1)S(1)} %get-tuple-element.65), channel_id=1, source_target_pairs={{0,14},{1,15},{2,12},{3,13},{4,10},{5,11},{6,8},{7,9},{8,6},{9,7},... | collective-permute-start | bytes 442376 | tf_op jit(solution)/shard_map/ppermute | solution.py:197
  39.3 0.0 collective-permute-done.5.refs_7_
  39.3 1.5 %collective-permute-start.15 = (bf16[96,768]{1,0:T(8,128)(2,1)S(1)}, bf16[96,768]{1,0:T(8,128)(2,1)S(1)}, u32[]{:S(2)}, u32[]{:S(2)}) collective-permute-start(bf16[96,768]{1,0:T(8,128)(2,1)S(1)} %get-tuple-element.75), channel_id=1, source_target_pairs={{0,16},{1,17},{2,18},{3,19},{4,20},{5,21},{6,22},{7,23},{8,24},{9,... | collective-permute-start | bytes 442376 | tf_op jit(solution)/shard_map/ppermute | solution.py:197
  40.8 0.7 collective-permute-done.6.refs_8_
  41.5 0.0 copy-done.1
  41.5 5.3 %shard_map.77 = (f32[2,2,96,384]{3,2,1,0:T(8,128)S(1)}, bf16[96,768]{1,0:T(8,128)(2,1)S(1)}, bf16[96,768]{1,0:T(8,128)(2,1)S(1)}, f32[2,2,96,384]{3,2,1,0:T(8,12...) custom-call(s32[3]{0:T(128)S(1)} %pad_add_fusion.meta.refs_0_, ...), custom_call_target="tpu_custom_call", output_to_operand_aliasing={{10}: (12, {})} | custom-call | tf_op jit(solution)/shard_map/pallas_call | solution.py:260
  46.8 1.5 %collective-permute-start.13 = (bf16[96,768]{1,0:T(8,128)(2,1)S(1)}, bf16[96,768]{1,0:T(8,128)(2,1)S(1)}, u32[]{:S(2)}, u32[]{:S(2)}) collective-permute-start(bf16[96,768]{1,0:T(8,128)(2,1)S(1)} %get-tuple-element.72), channel_id=1, source_target_pairs={{0,20},{1,21},{2,22},{3,23},{4,16},{5,17},{6,18},{7,19},{8,28},{9,... | collective-permute-start | bytes 442376 | tf_op jit(solution)/shard_map/ppermute | solution.py:197
  48.3 0.0 collective-permute-done.9.refs_5_
  48.3 3.3 %collective-permute-start.14 = (bf16[96,768]{1,0:T(8,128)(2,1)S(1)}, bf16[96,768]{1,0:T(8,128)(2,1)S(1)}, u32[]{:S(2)}, u32[]{:S(2)}) collective-permute-start(bf16[96,768]{1,0:T(8,128)(2,1)S(1)} %get-tuple-element.73), channel_id=1, source_target_pairs={{0,22},{1,23},{2,20},{3,21},{4,18},{5,19},{6,16},{7,17},{8,30},{9,... | collective-permute-start | bytes 442376 | tf_op jit(solution)/shard_map/ppermute | solution.py:197
  51.7 0.4 collective-permute-done.10.refs_7_
  52.0 0.2 collective-permute-start.16
  52.2 0.0 collective-permute-done.11.refs_8_
  52.2 5.1 %collective-permute-start.18 = (bf16[96,768]{1,0:T(8,128)(2,1)S(1)}, bf16[96,768]{1,0:T(8,128)(2,1)S(1)}, u32[]{:S(2)}, u32[]{:S(2)}) collective-permute-start(bf16[96,768]{1,0:T(8,128)(2,1)S(1)} %get-tuple-element.82), channel_id=1, source_target_pairs={{0,24},{1,25},{2,26},{3,27},{4,28},{5,29},{6,30},{7,31},{8,16},{9,... | collective-permute-start | bytes 442376 | tf_op jit(solution)/shard_map/ppermute | solution.py:197
  57.3 1.8 %shard_map.78 = (f32[2,8,96,768]{3,2,1,0:T(8,128)}, bf16[96,768]{1,0:T(8,128)(2,1)S(1)}, bf16[96,768]{1,0:T(8,128)(2,1)S(1)}, f32[8,128]{1,0:T(8,128)S(1)}) custom-call(s32[3]{0:T(128)S(1)} %pad_add_fusion.meta.refs_0_, f32[8]{0:T(128)S(1)} %copy-done.1, ...), custom_call_target="tpu_custom_call", output_to_operand_aliasing={{0}: (9, {}), {1}: (10, {}), {2}: (11, {})} | custom-call | tf_op jit(solution)/shard_map/pallas_call | solution.py:260
  59.1 0.0 collective-permute-done.15.refs_7_
  59.1 6.1 %collective-permute-start.12 = (bf16[96,768]{1,0:T(8,128)(2,1)S(1)}, bf16[96,768]{1,0:T(8,128)(2,1)S(1)}, u32[]{:S(2)}, u32[]{:S(2)}) collective-permute-start(bf16[96,768]{1,0:T(8,128)(2,1)S(1)} %get-tuple-element.70), channel_id=1, source_target_pairs={{0,28},{1,29},{2,30},{3,31},{4,24},{5,25},{6,26},{7,27},{8,20},{9,... | collective-permute-start | bytes 442376 | tf_op jit(solution)/shard_map/ppermute | solution.py:197
  65.2 0.0 collective-permute-done.13.refs_4_
  65.2 0.0 collective-permute-start.19
  65.3 0.0 collective-permute-done.14.refs_5_
  65.3 0.3 collective-permute-done.16.refs_8_
  65.5 1.7 %shard_map.79 = (f32[2,8,96,768]{3,2,1,0:T(8,128)}, bf16[96,768]{1,0:T(8,128)(2,1)S(1)}, f32[8,128]{1,0:T(8,128)S(1)}) custom-call(s32[3]{0:T(128)S(1)} %pad_add_fusion.meta.refs_0_, f32[8]{0:T(128)S(1)} %copy-done.1, f32[1,768]{1,0:T(1,128)S(1)} %reshape.3.refs_5_.refs_2_, ...), custom_call_target="tpu_custom_call", output_to_operand_aliasing={{0}: (9, {}), {1}: (10, {})} | custom-call | tf_op jit(solution)/shard_map/pallas_call | solution.py:260
  67.3 3.4 %collective-permute-start.17 = (bf16[96,768]{1,0:T(8,128)(2,1)S(1)}, bf16[96,768]{1,0:T(8,128)(2,1)S(1)}, u32[]{:S(2)}, u32[]{:S(2)}) collective-permute-start(bf16[96,768]{1,0:T(8,128)(2,1)S(1)} %get-tuple-element.80), channel_id=1, source_target_pairs={{0,30},{1,31},{2,28},{3,29},{4,26},{5,27},{6,24},{7,25},{8,22},{9,... | collective-permute-start | bytes 442376 | tf_op jit(solution)/shard_map/ppermute | solution.py:197
  70.7 0.0 collective-permute-done.18.refs_7_
  70.7 1.8 %collective-permute-done.12.refs_4_ = bf16[96,768]{1,0:T(8,128)(2,1)S(1)} collective-permute-done((bf16[96,768]{1,0:T(8,128)(2,1)S(1)}, bf16[96,768]{1,0:T(8,128)(2,1)S(1)}, u32[]{:S(2)}, u32[]{:S(2)}) %collective-permute-start.12) | collective-permute-done | bytes 147488 | tf_op jit(solution)/shard_map/ppermute | solution.py:197
  72.5 0.5 collective-permute-done.19.refs_8_
  73.1 3.7 %collective-permute-done.17.refs_5_ = bf16[96,768]{1,0:T(8,128)(2,1)S(1)} collective-permute-done((bf16[96,768]{1,0:T(8,128)(2,1)S(1)}, bf16[96,768]{1,0:T(8,128)(2,1)S(1)}, u32[]{:S(2)}, u32[]{:S(2)}) %collective-permute-start.17) | collective-permute-done | bytes 147488 | tf_op jit(solution)/shard_map/ppermute | solution.py:197
  76.8 2.3 %shard_map.80 = (f32[2,8,96,768]{3,2,1,0:T(8,128)}, f32[8,128]{1,0:T(8,128)}) custom-call(s32[3]{0:T(128)S(1)} %pad_add_fusion.meta.refs_0_, f32[8]{0:T(128)S(1)} %copy-done.1, f32[1,768]{1,0:T(1,128)S(1)} %reshape.3.refs_5_.refs_2_, f32[2,2,96,384]{3,2,1,0:T(8,128)S(1)} %get-tuple-element.59.refs_3_, ...), custom_call_target="tpu_custom_call", output_to_operand_aliasing={{0}: (9, {})} | custom-call | tf_op jit(solution)/shard_map/pallas_call | solution.py:260
  (1 shorter events, 0.0 us)
Async XLA Ops:
  0.0 16.5 %copy-start = (bf16[96,768]{1,0:T(8,128)(2,1)S(1)}, bf16[96,768]{1,0:T(8,128)(2,1)}, u32[]{:S(2)}) copy-start(bf16[96,768]{1,0:T(8,128)(2,1)} %own.3) | copy-start | bytes 442372
  0.0 6.4 %collective-permute-start = (bf16[2,8,96,768]{3,2,1,0:T(8,128)(2,1)}, bf16[2,8,96,768]{3,2,1,0:T(8,128)(2,1)S(1)}, u32[]{:S(2)}, u32[]{:S(2)}) collective-permute-start(bf16[2,8,96,768]{3,2,1,0:T(8,128)(2,1)} %own.2), channel_id=1, source_target_pairs={{0,1},{1,0},{2,3},{3,2},{4,5},{5,4},{6,7},{7,6},{8,9},{9,8},{10,11... | collective-permute-start | bytes 7077896 | tf_op jit(solution)/shard_map/ppermute | solution.py:197
  0.5 16.0 %collective-permute-start.2 = (bf16[96,768]{1,0:T(8,128)(2,1)}, bf16[96,768]{1,0:T(8,128)(2,1)S(1)}, u32[]{:S(2)}, u32[]{:S(2)}) collective-permute-start(bf16[96,768]{1,0:T(8,128)(2,1)} %own.3), channel_id=1, source_target_pairs={{0,4},{1,5},{2,6},{3,7},{4,0},{5,1},{6,2},{7,3},{8,12},{9,13},{10,... | collective-permute-start | bytes 442376 | tf_op jit(solution)/shard_map/ppermute | solution.py:197
  4.1 12.4 %collective-permute-start.1 = (bf16[96,768]{1,0:T(8,128)(2,1)}, bf16[96,768]{1,0:T(8,128)(2,1)S(1)}, u32[]{:S(2)}, u32[]{:S(2)}) collective-permute-start(bf16[96,768]{1,0:T(8,128)(2,1)} %own.3), channel_id=1, source_target_pairs={{0,2},{1,3},{2,0},{3,1},{4,6},{5,7},{6,4},{7,5},{8,10},{9,11},{10,... | collective-permute-start | bytes 442376 | tf_op jit(solution)/shard_map/ppermute | solution.py:197
  5.7 10.8 %collective-permute-start.3 = (bf16[96,768]{1,0:T(8,128)(2,1)}, bf16[96,768]{1,0:T(8,128)(2,1)S(1)}, u32[]{:S(2)}, u32[]{:S(2)}) collective-permute-start(bf16[96,768]{1,0:T(8,128)(2,1)} %own.3), channel_id=1, source_target_pairs={{0,6},{1,7},{2,4},{3,5},{4,2},{5,3},{6,0},{7,1},{8,14},{9,15},{10,... | collective-permute-start | bytes 442376 | tf_op jit(solution)/shard_map/ppermute | solution.py:197
  6.4 1.4 %copy-start.2 = (bf16[2,8,96,768]{3,2,1,0:T(8,128)(2,1)}, bf16[2,8,96,768]{3,2,1,0:T(8,128)(2,1)S(1)}, u32[]{:S(2)}) copy-start(bf16[2,8,96,768]{3,2,1,0:T(8,128)(2,1)S(1)} %collective-permute-done.sib) | copy-start | bytes 7077892
  16.6 2.1 %collective-permute-start.4 = (bf16[4,96,768]{2,1,0:T(8,128)(2,1)S(1)}, bf16[4,96,768]{2,1,0:T(8,128)(2,1)S(1)}, u32[]{:S(2)}, u32[]{:S(2)}) collective-permute-start(bf16[4,96,768]{2,1,0:T(8,128)(2,1)S(1)} %shard_map.74.refs_3_), channel_id=1, source_target_pairs={{0,1},{1,0},{2,3},{3,2},{4,5},{5,4},{6,7},{7,6},{8,9},{9,8},{10,11... | collective-permute-start | bytes 1769480 | tf_op jit(solution)/shard_map/ppermute | solution.py:197
  20.5 15.2 %collective-permute-start.7 = (bf16[96,768]{1,0:T(8,128)(2,1)S(1)}, bf16[96,768]{1,0:T(8,128)(2,1)S(1)}, u32[]{:S(2)}, u32[]{:S(2)}) collective-permute-start(bf16[96,768]{1,0:T(8,128)(2,1)S(1)} %get-tuple-element.55), channel_id=1, source_target_pairs={{0,4},{1,5},{2,6},{3,7},{4,0},{5,1},{6,2},{7,3},{8,12},{9,13},{10,... | collective-permute-start | bytes 442376 | tf_op jit(solution)/shard_map/ppermute | solution.py:197
  24.9 12.1 %collective-permute-start.8 = (bf16[96,768]{1,0:T(8,128)(2,1)S(1)}, bf16[96,768]{1,0:T(8,128)(2,1)S(1)}, u32[]{:S(2)}, u32[]{:S(2)}) collective-permute-start(bf16[96,768]{1,0:T(8,128)(2,1)S(1)} %get-tuple-element.56), channel_id=1, source_target_pairs={{0,6},{1,7},{2,4},{3,5},{4,2},{5,3},{6,0},{7,1},{8,14},{9,15},{10,... | collective-permute-start | bytes 442376 | tf_op jit(solution)/shard_map/ppermute | solution.py:197
  25.5 11.6 %copy-start.3 = (f32[768]{0:T(1024)S(1)}, f32[768]{0:T(1024)}, u32[]{:S(2)}) copy-start(f32[768]{0:T(1024)} %param.13) | copy-start | bytes 9220
  25.5 16.1 %copy-start.1 = (f32[8]{0:T(128)S(1)}, f32[8]{0:T(128)}, u32[]{:S(2)}) copy-start(f32[8]{0:T(128)} %refs_1_.5) | copy-start | bytes 100
  30.7 8.5 %collective-permute-start.5 = (bf16[96,768]{1,0:T(8,128)(2,1)S(1)}, bf16[96,768]{1,0:T(8,128)(2,1)S(1)}, u32[]{:S(2)}, u32[]{:S(2)}) collective-permute-start(bf16[96,768]{1,0:T(8,128)(2,1)S(1)} %get-tuple-element.52), channel_id=1, source_target_pairs={{0,8},{1,9},{2,10},{3,11},{4,12},{5,13},{6,14},{7,15},{8,0},{9,1},... | collective-permute-start | bytes 442376 | tf_op jit(solution)/shard_map/ppermute | solution.py:197
  32.3 9.2 %collective-permute-start.6 = (bf16[96,768]{1,0:T(8,128)(2,1)S(1)}, bf16[96,768]{1,0:T(8,128)(2,1)S(1)}, u32[]{:S(2)}, u32[]{:S(2)}) collective-permute-start(bf16[96,768]{1,0:T(8,128)(2,1)S(1)} %get-tuple-element.53), channel_id=1, source_target_pairs={{0,10},{1,11},{2,8},{3,9},{4,14},{5,15},{6,12},{7,13},{8,2},{9,3},... | collective-permute-start | bytes 442376 | tf_op jit(solution)/shard_map/ppermute | solution.py:197
  32.4 16.0 %collective-permute-start.9 = (bf16[96,768]{1,0:T(8,128)(2,1)S(1)}, bf16[96,768]{1,0:T(8,128)(2,1)S(1)}, u32[]{:S(2)}, u32[]{:S(2)}) collective-permute-start(bf16[96,768]{1,0:T(8,128)(2,1)S(1)} %get-tuple-element.62), channel_id=1, source_target_pairs={{0,2},{1,3},{2,0},{3,1},{4,6},{5,7},{6,4},{7,5},{8,10},{9,11},{10,... | collective-permute-start | bytes 442376 | tf_op jit(solution)/shard_map/ppermute | solution.py:197
  35.7 16.4 %collective-permute-start.10 = (bf16[96,768]{1,0:T(8,128)(2,1)S(1)}, bf16[96,768]{1,0:T(8,128)(2,1)S(1)}, u32[]{:S(2)}, u32[]{:S(2)}) collective-permute-start(bf16[96,768]{1,0:T(8,128)(2,1)S(1)} %get-tuple-element.64), channel_id=1, source_target_pairs={{0,12},{1,13},{2,14},{3,15},{4,8},{5,9},{6,10},{7,11},{8,4},{9,5},... | collective-permute-start | bytes 442376 | tf_op jit(solution)/shard_map/ppermute | solution.py:197
  37.0 15.2 %collective-permute-start.11 = (bf16[96,768]{1,0:T(8,128)(2,1)S(1)}, bf16[96,768]{1,0:T(8,128)(2,1)S(1)}, u32[]{:S(2)}, u32[]{:S(2)}) collective-permute-start(bf16[96,768]{1,0:T(8,128)(2,1)S(1)} %get-tuple-element.65), channel_id=1, source_target_pairs={{0,14},{1,15},{2,12},{3,13},{4,10},{5,11},{6,8},{7,9},{8,6},{9,7},... | collective-permute-start | bytes 442376 | tf_op jit(solution)/shard_map/ppermute | solution.py:197
  39.3 19.8 %collective-permute-start.15 = (bf16[96,768]{1,0:T(8,128)(2,1)S(1)}, bf16[96,768]{1,0:T(8,128)(2,1)S(1)}, u32[]{:S(2)}, u32[]{:S(2)}) collective-permute-start(bf16[96,768]{1,0:T(8,128)(2,1)S(1)} %get-tuple-element.75), channel_id=1, source_target_pairs={{0,16},{1,17},{2,18},{3,19},{4,20},{5,21},{6,22},{7,23},{8,24},{9,... | collective-permute-start | bytes 442376 | tf_op jit(solution)/shard_map/ppermute | solution.py:197
  46.8 18.4 %collective-permute-start.13 = (bf16[96,768]{1,0:T(8,128)(2,1)S(1)}, bf16[96,768]{1,0:T(8,128)(2,1)S(1)}, u32[]{:S(2)}, u32[]{:S(2)}) collective-permute-start(bf16[96,768]{1,0:T(8,128)(2,1)S(1)} %get-tuple-element.72), channel_id=1, source_target_pairs={{0,20},{1,21},{2,22},{3,23},{4,16},{5,17},{6,18},{7,19},{8,28},{9,... | collective-permute-start | bytes 442376 | tf_op jit(solution)/shard_map/ppermute | solution.py:197
  48.3 16.9 %collective-permute-start.14 = (bf16[96,768]{1,0:T(8,128)(2,1)S(1)}, bf16[96,768]{1,0:T(8,128)(2,1)S(1)}, u32[]{:S(2)}, u32[]{:S(2)}) collective-permute-start(bf16[96,768]{1,0:T(8,128)(2,1)S(1)} %get-tuple-element.73), channel_id=1, source_target_pairs={{0,22},{1,23},{2,20},{3,21},{4,18},{5,19},{6,16},{7,17},{8,30},{9,... | collective-permute-start | bytes 442376 | tf_op jit(solution)/shard_map/ppermute | solution.py:197
  52.0 13.5 %collective-permute-start.16 = (bf16[96,768]{1,0:T(8,128)(2,1)S(1)}, bf16[96,768]{1,0:T(8,128)(2,1)S(1)}, u32[]{:S(2)}, u32[]{:S(2)}) collective-permute-start(bf16[96,768]{1,0:T(8,128)(2,1)S(1)} %get-tuple-element.76), channel_id=1, source_target_pairs={{0,18},{1,19},{2,16},{3,17},{4,22},{5,23},{6,20},{7,21},{8,26},{9,... | collective-permute-start | bytes 442376 | tf_op jit(solution)/shard_map/ppermute | solution.py:197
  52.2 18.5 %collective-permute-start.18 = (bf16[96,768]{1,0:T(8,128)(2,1)S(1)}, bf16[96,768]{1,0:T(8,128)(2,1)S(1)}, u32[]{:S(2)}, u32[]{:S(2)}) collective-permute-start(bf16[96,768]{1,0:T(8,128)(2,1)S(1)} %get-tuple-element.82), channel_id=1, source_target_pairs={{0,24},{1,25},{2,26},{3,27},{4,28},{5,29},{6,30},{7,31},{8,16},{9,... | collective-permute-start | bytes 442376 | tf_op jit(solution)/shard_map/ppermute | solution.py:197
  59.1 13.4 %collective-permute-start.12 = (bf16[96,768]{1,0:T(8,128)(2,1)S(1)}, bf16[96,768]{1,0:T(8,128)(2,1)S(1)}, u32[]{:S(2)}, u32[]{:S(2)}) collective-permute-start(bf16[96,768]{1,0:T(8,128)(2,1)S(1)} %get-tuple-element.70), channel_id=1, source_target_pairs={{0,28},{1,29},{2,30},{3,31},{4,24},{5,25},{6,26},{7,27},{8,20},{9,... | collective-permute-start | bytes 442376 | tf_op jit(solution)/shard_map/ppermute | solution.py:197
  65.2 7.8 %collective-permute-start.19 = (bf16[96,768]{1,0:T(8,128)(2,1)S(1)}, bf16[96,768]{1,0:T(8,128)(2,1)S(1)}, u32[]{:S(2)}, u32[]{:S(2)}) collective-permute-start(bf16[96,768]{1,0:T(8,128)(2,1)S(1)} %get-tuple-element.83), channel_id=1, source_target_pairs={{0,26},{1,27},{2,24},{3,25},{4,30},{5,31},{6,28},{7,29},{8,18},{9,... | collective-permute-start | bytes 442376 | tf_op jit(solution)/shard_map/ppermute | solution.py:197
  67.3 9.5 %collective-permute-start.17 = (bf16[96,768]{1,0:T(8,128)(2,1)S(1)}, bf16[96,768]{1,0:T(8,128)(2,1)S(1)}, u32[]{:S(2)}, u32[]{:S(2)}) collective-permute-start(bf16[96,768]{1,0:T(8,128)(2,1)S(1)} %get-tuple-element.80), channel_id=1, source_target_pairs={{0,30},{1,31},{2,28},{3,29},{4,26},{5,27},{6,24},{7,25},{8,22},{9,... | collective-permute-start | bytes 442376 | tf_op jit(solution)/shard_map/ppermute | solution.py:197

commit v5 on v4

--- a/solution.py
+++ b/solution.py
@@ -99,22 +99,31 @@
         lax.fori_loop(0, 2 * rows // 16, step, 0)
 
 
-def relay_kernel(own, near, middle, far, mask, out):
-    for k, piece in enumerate((own, near, middle, far)):
-        out[k] = piece[...] * mask[k]
+def half_of(z, side, half):
+    return pl.ds(pl.multiple_of(((z // 2) ^ side) * half, half), half)
+
+
+def relay_kernel(meta, own, near, middle, far, mask, near_out, far_out):
+    half = near_out.shape[-1]
+    for side, out in ((0, near_out), (1, far_out)):
+        columns = half_of(meta[1], side, half)
+        for k, piece in enumerate((own, near, middle, far)):
+            out[k] = piece[:, columns] * mask[k, :, columns]
 
 
 def make_tiles(makes, r):
-    meta, x, h, w, flipped, own, sems = (r[name] for name in ("meta", "x", "h", "w", "flipped", "own", "own_sems"))
+    meta, x, h, flipped, own, sems = (r[name] for name in ("meta", "x", "h", "flipped", "own", "own_sems"))
     _, occ_rows, _, _, rows, half = own.shape
     width, chip, pairs = x.shape[-1], CORES * rows, occ_rows * occ_rows
     o, z, core = meta[0], meta[1], meta[2]
     copies = []
     for n, (partner, side) in enumerate(makes):
         first_j = (o ^ partner) * occ_rows
-        columns = pl.ds(pl.multiple_of(((z // 2) ^ side) * half, half), half)
+        columns = half_of(z, side, half)
         ladder = jnp.dot(
-            x[:, pl.ds(first_j, occ_rows)].reshape(pairs * chip, width), w[:, columns], preferred_element_type=jnp.float32
+            x[:, pl.ds(first_j, occ_rows)].reshape(pairs * chip, width),
+            r["w", side][...],
+            preferred_element_type=jnp.float32,
         )
         for i in range(occ_rows):
             for jj in range(occ_rows):
@@ -142,7 +151,7 @@
     stores = []
     for n, (partner, side) in enumerate(ends):
         first_j = (o ^ partner) * occ_rows
-        lanes = pl.ds(pl.multiple_of(((z // 2) ^ side) * half, half), half)
+        lanes = half_of(z, side, half)
         own, one, two = (r["got", partner, side, c] for c in range(3))
         for i in range(occ_rows):
             for jj in range(occ_rows):
@@ -159,12 +168,14 @@
 
 def step_kernel(names, makes, ends, *refs):
     r = dict(zip(names, refs, strict=True))
-    if "mine" in r:
-        z, core = r["meta"][1], r["meta"][2]
-        rows = r["mine"].shape[1]
-        for k in range(4):
-            for piece, at in ((r["mine"], core), (r["theirs"], 1 - core)):
-                r["w"][pl.ds(pl.multiple_of(((z ^ k) * CORES + at) * rows, rows), rows), :] = piece[k]
+    for side in (0, 1):
+        if ("mine", side) in r:
+            z, core = r["meta"][1], r["meta"][2]
+            rows = r["mine", side].shape[1]
+            for k in range(4):
+                for piece, at in ((r["mine", side], core), (r["theirs", side], 1 - core)):
+                    start = pl.multiple_of(((z ^ k) * CORES + at) * rows, rows)
+                    r["w", side][pl.ds(start, rows), :] = piece[k]
     copies = make_tiles(makes, r) if makes else []
     copies += finish_tiles(ends, r) if ends else []
     r["token"][...] = jnp.zeros(r["token"].shape, r["token"].dtype)
@@ -209,11 +220,11 @@
     )(meta, occ_fock.astype(f32), *[in_hbm(a) for a in (amplitudes, sibling, amp_mask, int_mask)])
     relayed = pl.pallas_call(
         relay_kernel,
-        in_specs=[VMEM] * 5,
-        out_specs=VMEM,
-        out_shape=pltpu.VMEM((4, rows, width), bf16),
+        in_specs=[SMEM] + [VMEM] * 5,
+        out_specs=[VMEM] * 2,
+        out_shape=[pltpu.VMEM((4, rows, half), bf16)] * 2,
         compiler_params=params,
-    )(*[in_vmem(a) for a in pieces], in_vmem(wide_int))
+    )(meta, *[in_vmem(a) for a in pieces], in_vmem(wide_int))
 
     sends, arrived, mixed, kept = {}, {}, {}, {}
 
@@ -221,11 +232,13 @@
         ins, outs, scratch, aliases = [("meta", meta, SMEM)], [], [], {}
         if makes:
             ins += [("x", in_vmem(x), VMEM), ("h", in_vmem(h), VMEM)]
-            if "w" in kept:
-                ins.append(("w", in_vmem(kept["w"]), VMEM))
-            else:
-                ins += [("mine", in_vmem(relayed), VMEM), ("theirs", in_vmem(swap(relayed, 1)), VMEM)]
-                outs.append(("w", pltpu.VMEM((width, width), bf16), VMEM))
+            for side in sorted({side for _, side in makes}):
+                if ("w", side) in kept:
+                    ins.append((("w", side), in_vmem(kept["w", side]), VMEM))
+                else:
+                    ins.append((("mine", side), in_vmem(relayed[side]), VMEM))
+                    ins.append((("theirs", side), in_vmem(swap(relayed[side], 1)), VMEM))
+                    outs.append((("w", side), pltpu.VMEM((width, half), bf16), VMEM))
             for partner, side in makes:
                 outs.append((("mixed", partner, side), jax.ShapeDtypeStruct((occ_rows, occ_rows, rows, half), f32), ANY))
                 outs += [(("tile", partner, 2 * side + s), pltpu.VMEM(tile, bf16), VMEM) for s in (0, 1)]

time: 79.3 us -> 79.4 us (level)
  waiting for transfers between devices: 10.8 us -> 9.95 us
    ppermute x20 -> x21, waiting for transfers between devices: 10.8 us -> 9.95 us  [swap(): return lax.ppermute(a, axes, [(d, d ^ k) for d in range(devices)])]
    ppermute x20 -> x21, starting transfers between devices: 39.1 us -> 39.6 us  [swap(): return lax.ppermute(a, axes, [(d, d ^ k) for d in range(devices)])]
  transfers between devices with their start and end apart: 20 -> 21, of which waited for: 8 -> 8; matrix products, arithmetic and copies ran while one was open for 1% -> 1% of each run, Pallas kernels for 29% -> 31%
where the time goes in v5:
time: 79.4 us; the launch traced here: 79.3 us
  starting transfers between devices  39.6 us (50%)
  Pallas kernels  27.5 us (35%)
  waiting for transfers between devices  9.95 us (13%)
  local copies, waits for them, and re-layouts  1.42 us (2%)
    ppermute x21, starting transfers between devices, swap(): return lax.ppermute(a, axes, [(d, d ^ k) for d in range(devices)])  39.6 us
    pallas_call x6, Pallas kernels, step(): pl.pallas_call(functools.partial(step_kernel, in_names + out_names + [nam...  18.2 us
    ppermute x21, waiting for transfers between devices, swap(): return lax.ppermute(a, axes, [(d, d ^ k) for d in range(devices)])  9.95 us
    pallas_call x1, Pallas kernels, paired(): pl.pallas_call(functools.partial(prepare_kernel, block), in_specs=[SMEM,...  8.6 us
  transfers between devices with their start and end apart: 21, of which 8 were waited for; matrix products, arithmetic and copies ran while one was open for 1% of the time, Pallas kernels for 31%

profile of v5, /device:TPU:0, one launch (start us, length us, event | category | flops | bytes accessed | tf_op | source)
XLA Modules:
  0.0 79.3 jit_solution(833573270207485093)
XLA Ops:
  0.0 0.0 copy-start
  0.0 0.5 collective-permute-start
  0.5 3.6 %collective-permute-start.2 = (bf16[96,768]{1,0:T(8,128)(2,1)}, bf16[96,768]{1,0:T(8,128)(2,1)S(1)}, u32[]{:S(2)}, u32[]{:S(2)}) collective-permute-start(bf16[96,768]{1,0:T(8,128)(2,1)} %own.3), channel_id=1, source_target_pairs={{0,4},{1,5},{2,6},{3,7},{4,0},{5,1},{6,2},{7,3},{8,12},{9,13},{10,... | collective-permute-start | bytes 442376 | tf_op jit(solution)/shard_map/ppermute | solution.py:208
  4.1 1.6 %collective-permute-start.1 = (bf16[96,768]{1,0:T(8,128)(2,1)}, bf16[96,768]{1,0:T(8,128)(2,1)S(1)}, u32[]{:S(2)}, u32[]{:S(2)}) collective-permute-start(bf16[96,768]{1,0:T(8,128)(2,1)} %own.3), channel_id=1, source_target_pairs={{0,2},{1,3},{2,0},{3,1},{4,6},{5,7},{6,4},{7,5},{8,10},{9,11},{10,... | collective-permute-start | bytes 442376 | tf_op jit(solution)/shard_map/ppermute | solution.py:208
  5.7 0.0 collective-permute-start.3
  5.7 0.7 convert_element_type.3.fock
  6.4 0.1 pad_add_fusion.meta.refs_0_
  6.4 0.0 collective-permute-done.sib
  6.4 0.0 copy-start.2
  6.4 1.4 %copy-done.2 = bf16[2,8,96,768]{3,2,1,0:T(8,128)(2,1)} copy-done((bf16[2,8,96,768]{3,2,1,0:T(8,128)(2,1)}, bf16[2,8,96,768]{3,2,1,0:T(8,128)(2,1)S(1)}, u32[]{:S(2)}) %copy-start.2) | copy-done | bytes 2359320
  7.9 8.6 %shard_map.73 = (bf16[2,8,2,96,768]{4,3,2,1,0:T(8,128)(2,1)S(1)}, f32[2,8,2,96,768]{4,3,2,1,0:T(8,128)S(1)}, bf16[4,96,768]{2,1,0:T(8,128)(2,1)S(1)}) custom-call(s32[3]{0:T(128)S(1)} %pad_add_fusion.meta.refs_0_, f32[8,8]{1,0:T(8,128)S(1)} %convert_element_type.3.fock, bf16[2,8,96,768]{3,2,1,0:T(8,128)(2,1)} %own.2, bf16[2,8,96,768]{3,2,1,0:T(8,128)(2,1)} %copy-done.2, ...), custom_call_target="tpu_custom_call" | custom-call | tf_op jit(solution)/shard_map/pallas_call | solution.py:213
  16.5 0.0 collective-permute-done.2.middle
  16.5 0.0 collective-permute-done.1.near
  16.5 0.0 collective-permute-done.3.far
  16.5 0.0 copy-done
  16.5 0.7 shard_map.74
  17.2 0.1 collective-permute-start.5
  17.2 0.5 collective-permute-start.4
  17.7 1.1 %collective-permute-done.5.refs_4_ = bf16[4,96,384]{2,1,0:T(8,128)(2,1)S(1)} collective-permute-done((bf16[4,96,384]{2,1,0:T(8,128)(2,1)S(1)}, bf16[4,96,384]{2,1,0:T(8,128)(2,1)S(1)}, u32[]{:S(2)}, u32[]{:S(2)}) %collective-permute-start.5) | collective-permute-done | bytes 294944 | tf_op jit(solution)/shard_map/ppermute | solution.py:208
  18.8 1.8 %shard_map.75 = (bf16[768,384]{1,0:T(8,128)(2,1)S(1)}, f32[2,2,96,384]{3,2,1,0:T(8,128)S(1)}, bf16[96,768]{1,0:T(8,128)(2,1)S(1)}, bf16[96,768]{1,0:T(8,128)(2,1)S(1)}, f32[8,128]{1,0:T(8,128)S(1)}) custom-call(s32[3]{0:T(128)S(1)} %pad_add_fusion.meta.refs_0_, bf16[2,8,2,96,768]{4,3,2,1,0:T(8,128)(2,1)S(1)} %get-tuple-element.49.refs_1_, ...), custom_call_target="tpu_custom_call" | custom-call | tf_op jit(solution)/shard_map/pallas_call | solution.py:273
  20.6 4.5 %collective-permute-start.8 = (bf16[96,768]{1,0:T(8,128)(2,1)S(1)}, bf16[96,768]{1,0:T(8,128)(2,1)S(1)}, u32[]{:S(2)}, u32[]{:S(2)}) collective-permute-start(bf16[96,768]{1,0:T(8,128)(2,1)S(1)} %get-tuple-element.61), channel_id=1, source_target_pairs={{0,4},{1,5},{2,6},{3,7},{4,0},{5,1},{6,2},{7,3},{8,12},{9,13},{10,... | collective-permute-start | bytes 442376 | tf_op jit(solution)/shard_map/ppermute | solution.py:208
  25.1 0.5 collective-permute-start.9
  25.6 0.0 collective-permute-done.4.refs_4_
  25.6 0.0 copy-start.3
  25.6 0.0 copy-start.1
  25.6 5.3 %shard_map.76 = (bf16[768,384]{1,0:T(8,128)(2,1)S(1)}, f32[2,2,96,384]{3,2,1,0:T(8,128)S(1)}, bf16[96,768]{1,0:T(8,128)(2,1)S(1)}, bf16[96,768]{1,0:T(8,128)(2,1...) custom-call(s32[3]{0:T(128)S(1)} %pad_add_fusion.meta.refs_0_, ...), custom_call_target="tpu_custom_call" | custom-call | tf_op jit(solution)/shard_map/pallas_call | solution.py:273
  30.9 1.6 %collective-permute-start.6 = (bf16[96,768]{1,0:T(8,128)(2,1)S(1)}, bf16[96,768]{1,0:T(8,128)(2,1)S(1)}, u32[]{:S(2)}, u32[]{:S(2)}) collective-permute-start(bf16[96,768]{1,0:T(8,128)(2,1)S(1)} %get-tuple-element.58), channel_id=1, source_target_pairs={{0,8},{1,9},{2,10},{3,11},{4,12},{5,13},{6,14},{7,15},{8,0},{9,1},... | collective-permute-start | bytes 442376 | tf_op jit(solution)/shard_map/ppermute | solution.py:208
  32.5 0.1 collective-permute-start.7
  32.5 1.9 %collective-permute-start.10 = (bf16[96,768]{1,0:T(8,128)(2,1)S(1)}, bf16[96,768]{1,0:T(8,128)(2,1)S(1)}, u32[]{:S(2)}, u32[]{:S(2)}) collective-permute-start(bf16[96,768]{1,0:T(8,128)(2,1)S(1)} %get-tuple-element.68), channel_id=1, source_target_pairs={{0,2},{1,3},{2,0},{3,1},{4,6},{5,7},{6,4},{7,5},{8,10},{9,11},{10,... | collective-permute-start | bytes 442376 | tf_op jit(solution)/shard_map/ppermute | solution.py:208
  34.5 1.3 %collective-permute-done.8.refs_11_ = bf16[96,768]{1,0:T(8,128)(2,1)S(1)} collective-permute-done((bf16[96,768]{1,0:T(8,128)(2,1)S(1)}, bf16[96,768]{1,0:T(8,128)(2,1)S(1)}, u32[]{:S(2)}, u32[]{:S(2)}) %collective-permute-start.8) | collective-permute-done | bytes 147488 | tf_op jit(solution)/shard_map/ppermute | solution.py:208
  35.8 1.4 %collective-permute-start.11 = (bf16[96,768]{1,0:T(8,128)(2,1)S(1)}, bf16[96,768]{1,0:T(8,128)(2,1)S(1)}, u32[]{:S(2)}, u32[]{:S(2)}) collective-permute-start(bf16[96,768]{1,0:T(8,128)(2,1)S(1)} %get-tuple-element.70), channel_id=1, source_target_pairs={{0,12},{1,13},{2,14},{3,15},{4,8},{5,9},{6,10},{7,11},{8,4},{9,5},... | collective-permute-start | bytes 442376 | tf_op jit(solution)/shard_map/ppermute | solution.py:208
  37.2 0.0 copy-done.3
  37.2 0.0 collective-permute-done.9.refs_12_
  37.2 2.2 %collective-permute-start.12 = (bf16[96,768]{1,0:T(8,128)(2,1)S(1)}, bf16[96,768]{1,0:T(8,128)(2,1)S(1)}, u32[]{:S(2)}, u32[]{:S(2)}) collective-permute-start(bf16[96,768]{1,0:T(8,128)(2,1)S(1)} %get-tuple-element.71), channel_id=1, source_target_pairs={{0,14},{1,15},{2,12},{3,13},{4,10},{5,11},{6,8},{7,9},{8,6},{9,7},... | collective-permute-start | bytes 442376 | tf_op jit(solution)/shard_map/ppermute | solution.py:208
  39.4 0.0 collective-permute-done.6.refs_8_
  39.4 1.5 %collective-permute-start.16 = (bf16[96,768]{1,0:T(8,128)(2,1)S(1)}, bf16[96,768]{1,0:T(8,128)(2,1)S(1)}, u32[]{:S(2)}, u32[]{:S(2)}) collective-permute-start(bf16[96,768]{1,0:T(8,128)(2,1)S(1)} %get-tuple-element.81), channel_id=1, source_target_pairs={{0,16},{1,17},{2,18},{3,19},{4,20},{5,21},{6,22},{7,23},{8,24},{9,... | collective-permute-start | bytes 442376 | tf_op jit(solution)/shard_map/ppermute | solution.py:208
  40.9 0.8 %collective-permute-done.7.refs_9_ = bf16[96,768]{1,0:T(8,128)(2,1)S(1)} collective-permute-done((bf16[96,768]{1,0:T(8,128)(2,1)S(1)}, bf16[96,768]{1,0:T(8,128)(2,1)S(1)}, u32[]{:S(2)}, u32[]{:S(2)}) %collective-permute-start.7) | collective-permute-done | bytes 147488 | tf_op jit(solution)/shard_map/ppermute | solution.py:208
  41.8 0.0 copy-done.1
  41.8 5.3 %shard_map.77 = (f32[2,2,96,384]{3,2,1,0:T(8,128)S(1)}, bf16[96,768]{1,0:T(8,128)(2,1)S(1)}, bf16[96,768]{1,0:T(8,128)(2,1)S(1)}, f32[2,2,96,384]{3,2,1,0:T(8,12...) custom-call(s32[3]{0:T(128)S(1)} %pad_add_fusion.meta.refs_0_, ...), custom_call_target="tpu_custom_call", output_to_operand_aliasing={{10}: (13, {})} | custom-call | tf_op jit(solution)/shard_map/pallas_call | solution.py:273
  47.0 1.4 %collective-permute-start.14 = (bf16[96,768]{1,0:T(8,128)(2,1)S(1)}, bf16[96,768]{1,0:T(8,128)(2,1)S(1)}, u32[]{:S(2)}, u32[]{:S(2)}) collective-permute-start(bf16[96,768]{1,0:T(8,128)(2,1)S(1)} %get-tuple-element.78), channel_id=1, source_target_pairs={{0,20},{1,21},{2,22},{3,23},{4,16},{5,17},{6,18},{7,19},{8,28},{9,... | collective-permute-start | bytes 442376 | tf_op jit(solution)/shard_map/ppermute | solution.py:208
  48.5 0.0 collective-permute-done.10.refs_5_
  48.5 3.3 %collective-permute-start.15 = (bf16[96,768]{1,0:T(8,128)(2,1)S(1)}, bf16[96,768]{1,0:T(8,128)(2,1)S(1)}, u32[]{:S(2)}, u32[]{:S(2)}) collective-permute-start(bf16[96,768]{1,0:T(8,128)(2,1)S(1)} %get-tuple-element.79), channel_id=1, source_target_pairs={{0,22},{1,23},{2,20},{3,21},{4,18},{5,19},{6,16},{7,17},{8,30},{9,... | collective-permute-start | bytes 442376 | tf_op jit(solution)/shard_map/ppermute | solution.py:208
  51.8 0.4 collective-permute-done.11.refs_7_
  52.2 0.2 collective-permute-start.17
  52.5 0.0 collective-permute-done.12.refs_8_
  52.5 5.1 %collective-permute-start.19 = (bf16[96,768]{1,0:T(8,128)(2,1)S(1)}, bf16[96,768]{1,0:T(8,128)(2,1)S(1)}, u32[]{:S(2)}, u32[]{:S(2)}) collective-permute-start(bf16[96,768]{1,0:T(8,128)(2,1)S(1)} %get-tuple-element.88), channel_id=1, source_target_pairs={{0,24},{1,25},{2,26},{3,27},{4,28},{5,29},{6,30},{7,31},{8,16},{9,... | collective-permute-start | bytes 442376 | tf_op jit(solution)/shard_map/ppermute | solution.py:208
  57.5 1.8 %shard_map.78 = (f32[2,8,96,768]{3,2,1,0:T(8,128)}, bf16[96,768]{1,0:T(8,128)(2,1)S(1)}, bf16[96,768]{1,0:T(8,128)(2,1)S(1)}, f32[8,128]{1,0:T(8,128)S(1)}) custom-call(s32[3]{0:T(128)S(1)} %pad_add_fusion.meta.refs_0_, f32[8]{0:T(128)S(1)} %copy-done.1, ...), custom_call_target="tpu_custom_call", output_to_operand_aliasing={{0}: (9, {}), {1}: (10, {}), {2}: (11, {})} | custom-call | tf_op jit(solution)/shard_map/pallas_call | solution.py:273
  59.3 0.0 collective-permute-done.16.refs_7_
  59.3 6.1 %collective-permute-start.13 = (bf16[96,768]{1,0:T(8,128)(2,1)S(1)}, bf16[96,768]{1,0:T(8,128)(2,1)S(1)}, u32[]{:S(2)}, u32[]{:S(2)}) collective-permute-start(bf16[96,768]{1,0:T(8,128)(2,1)S(1)} %get-tuple-element.76), channel_id=1, source_target_pairs={{0,28},{1,29},{2,30},{3,31},{4,24},{5,25},{6,26},{7,27},{8,20},{9,... | collective-permute-start | bytes 442376 | tf_op jit(solution)/shard_map/ppermute | solution.py:208
  65.4 0.0 collective-permute-done.14.refs_4_
  65.4 0.0 collective-permute-start.20
  65.4 0.0 collective-permute-done.15.refs_5_
  65.4 0.2 collective-permute-done.17.refs_8_
  65.6 1.8 %shard_map.79 = (f32[2,8,96,768]{3,2,1,0:T(8,128)}, bf16[96,768]{1,0:T(8,128)(2,1)S(1)}, f32[8,128]{1,0:T(8,128)S(1)}) custom-call(s32[3]{0:T(128)S(1)} %pad_add_fusion.meta.refs_0_, f32[8]{0:T(128)S(1)} %copy-done.1, f32[1,768]{1,0:T(1,128)S(1)} %reshape.3.refs_6_.refs_2_, ...), custom_call_target="tpu_custom_call", output_to_operand_aliasing={{0}: (9, {}), {1}: (10, {})} | custom-call | tf_op jit(solution)/shard_map/pallas_call | solution.py:273
  67.4 3.5 %collective-permute-start.18 = (bf16[96,768]{1,0:T(8,128)(2,1)S(1)}, bf16[96,768]{1,0:T(8,128)(2,1)S(1)}, u32[]{:S(2)}, u32[]{:S(2)}) collective-permute-start(bf16[96,768]{1,0:T(8,128)(2,1)S(1)} %get-tuple-element.86), channel_id=1, source_target_pairs={{0,30},{1,31},{2,28},{3,29},{4,26},{5,27},{6,24},{7,25},{8,22},{9,... | collective-permute-start | bytes 442376 | tf_op jit(solution)/shard_map/ppermute | solution.py:208
  70.9 0.0 collective-permute-done.19.refs_7_
  70.9 1.4 %collective-permute-done.13.refs_4_ = bf16[96,768]{1,0:T(8,128)(2,1)S(1)} collective-permute-done((bf16[96,768]{1,0:T(8,128)(2,1)S(1)}, bf16[96,768]{1,0:T(8,128)(2,1)S(1)}, u32[]{:S(2)}, u32[]{:S(2)}) %collective-permute-start.13) | collective-permute-done | bytes 147488 | tf_op jit(solution)/shard_map/ppermute | solution.py:208
  72.3 0.8 %collective-permute-done.20.refs_8_ = bf16[96,768]{1,0:T(8,128)(2,1)S(1)} collective-permute-done((bf16[96,768]{1,0:T(8,128)(2,1)S(1)}, bf16[96,768]{1,0:T(8,128)(2,1)S(1)}, u32[]{:S(2)}, u32[]{:S(2)}) %collective-permute-start.20) | collective-permute-done | bytes 147488 | tf_op jit(solution)/shard_map/ppermute | solution.py:208
  73.1 3.8 %collective-permute-done.18.refs_5_ = bf16[96,768]{1,0:T(8,128)(2,1)S(1)} collective-permute-done((bf16[96,768]{1,0:T(8,128)(2,1)S(1)}, bf16[96,768]{1,0:T(8,128)(2,1)S(1)}, u32[]{:S(2)}, u32[]{:S(2)}) %collective-permute-start.18) | collective-permute-done | bytes 147488 | tf_op jit(solution)/shard_map/ppermute | solution.py:208
  76.9 2.3 %shard_map.80 = (f32[2,8,96,768]{3,2,1,0:T(8,128)}, f32[8,128]{1,0:T(8,128)}) custom-call(s32[3]{0:T(128)S(1)} %pad_add_fusion.meta.refs_0_, f32[8]{0:T(128)S(1)} %copy-done.1, f32[1,768]{1,0:T(1,128)S(1)} %reshape.3.refs_6_.refs_2_, f32[2,2,96,384]{3,2,1,0:T(8,128)S(1)} %get-tuple-element.65.refs_3_, ...), custom_call_target="tpu_custom_call", output_to_operand_aliasing={{0}: (9, {})} | custom-call | tf_op jit(solution)/shard_map/pallas_call | solution.py:273
  (1 shorter events, 0.0 us)
Async XLA Ops:
  0.0 16.5 %copy-start = (bf16[96,768]{1,0:T(8,128)(2,1)S(1)}, bf16[96,768]{1,0:T(8,128)(2,1)}, u32[]{:S(2)}) copy-start(bf16[96,768]{1,0:T(8,128)(2,1)} %own.3) | copy-start | bytes 442372
  0.0 6.4 %collective-permute-start = (bf16[2,8,96,768]{3,2,1,0:T(8,128)(2,1)}, bf16[2,8,96,768]{3,2,1,0:T(8,128)(2,1)S(1)}, u32[]{:S(2)}, u32[]{:S(2)}) collective-permute-start(bf16[2,8,96,768]{3,2,1,0:T(8,128)(2,1)} %own.2), channel_id=1, source_target_pairs={{0,1},{1,0},{2,3},{3,2},{4,5},{5,4},{6,7},{7,6},{8,9},{9,8},{10,11... | collective-permute-start | bytes 7077896 | tf_op jit(solution)/shard_map/ppermute | solution.py:208
  0.5 16.0 %collective-permute-start.2 = (bf16[96,768]{1,0:T(8,128)(2,1)}, bf16[96,768]{1,0:T(8,128)(2,1)S(1)}, u32[]{:S(2)}, u32[]{:S(2)}) collective-permute-start(bf16[96,768]{1,0:T(8,128)(2,1)} %own.3), channel_id=1, source_target_pairs={{0,4},{1,5},{2,6},{3,7},{4,0},{5,1},{6,2},{7,3},{8,12},{9,13},{10,... | collective-permute-start | bytes 442376 | tf_op jit(solution)/shard_map/ppermute | solution.py:208
  4.1 12.4 %collective-permute-start.1 = (bf16[96,768]{1,0:T(8,128)(2,1)}, bf16[96,768]{1,0:T(8,128)(2,1)S(1)}, u32[]{:S(2)}, u32[]{:S(2)}) collective-permute-start(bf16[96,768]{1,0:T(8,128)(2,1)} %own.3), channel_id=1, source_target_pairs={{0,2},{1,3},{2,0},{3,1},{4,6},{5,7},{6,4},{7,5},{8,10},{9,11},{10,... | collective-permute-start | bytes 442376 | tf_op jit(solution)/shard_map/ppermute | solution.py:208
  5.7 10.8 %collective-permute-start.3 = (bf16[96,768]{1,0:T(8,128)(2,1)}, bf16[96,768]{1,0:T(8,128)(2,1)S(1)}, u32[]{:S(2)}, u32[]{:S(2)}) collective-permute-start(bf16[96,768]{1,0:T(8,128)(2,1)} %own.3), channel_id=1, source_target_pairs={{0,6},{1,7},{2,4},{3,5},{4,2},{5,3},{6,0},{7,1},{8,14},{9,15},{10,... | collective-permute-start | bytes 442376 | tf_op jit(solution)/shard_map/ppermute | solution.py:208
  6.4 1.4 %copy-start.2 = (bf16[2,8,96,768]{3,2,1,0:T(8,128)(2,1)}, bf16[2,8,96,768]{3,2,1,0:T(8,128)(2,1)S(1)}, u32[]{:S(2)}) copy-start(bf16[2,8,96,768]{3,2,1,0:T(8,128)(2,1)S(1)} %collective-permute-done.sib) | copy-start | bytes 7077892
  17.2 1.6 %collective-permute-start.5 = (bf16[4,96,384]{2,1,0:T(8,128)(2,1)S(1)}, bf16[4,96,384]{2,1,0:T(8,128)(2,1)S(1)}, u32[]{:S(2)}, u32[]{:S(2)}) collective-permute-start(bf16[4,96,384]{2,1,0:T(8,128)(2,1)S(1)} %get-tuple-element.53.refs_3_), channel_id=1, source_target_pairs={{0,1},{1,0},{2,3},{3,2},{4,5},{5,4},{6,7},{7,6},{8,9},{9,8},{10,11... | collective-permute-start | bytes 884744 | tf_op jit(solution)/shard_map/ppermute | solution.py:208
  17.2 8.4 %collective-permute-start.4 = (bf16[4,96,384]{2,1,0:T(8,128)(2,1)S(1)}, bf16[4,96,384]{2,1,0:T(8,128)(2,1)S(1)}, u32[]{:S(2)}, u32[]{:S(2)}) collective-permute-start(bf16[4,96,384]{2,1,0:T(8,128)(2,1)S(1)} %get-tuple-element.52.refs_3_), channel_id=1, source_target_pairs={{0,1},{1,0},{2,3},{3,2},{4,5},{5,4},{6,7},{7,6},{8,9},{9,8},{10,11... | collective-permute-start | bytes 884744 | tf_op jit(solution)/shard_map/ppermute | solution.py:208
  20.6 15.2 %collective-permute-start.8 = (bf16[96,768]{1,0:T(8,128)(2,1)S(1)}, bf16[96,768]{1,0:T(8,128)(2,1)S(1)}, u32[]{:S(2)}, u32[]{:S(2)}) collective-permute-start(bf16[96,768]{1,0:T(8,128)(2,1)S(1)} %get-tuple-element.61), channel_id=1, source_target_pairs={{0,4},{1,5},{2,6},{3,7},{4,0},{5,1},{6,2},{7,3},{8,12},{9,13},{10,... | collective-permute-start | bytes 442376 | tf_op jit(solution)/shard_map/ppermute | solution.py:208
  25.1 12.1 %collective-permute-start.9 = (bf16[96,768]{1,0:T(8,128)(2,1)S(1)}, bf16[96,768]{1,0:T(8,128)(2,1)S(1)}, u32[]{:S(2)}, u32[]{:S(2)}) collective-permute-start(bf16[96,768]{1,0:T(8,128)(2,1)S(1)} %get-tuple-element.62), channel_id=1, source_target_pairs={{0,6},{1,7},{2,4},{3,5},{4,2},{5,3},{6,0},{7,1},{8,14},{9,15},{10,... | collective-permute-start | bytes 442376 | tf_op jit(solution)/shard_map/ppermute | solution.py:208
  25.6 11.6 %copy-start.3 = (f32[768]{0:T(1024)S(1)}, f32[768]{0:T(1024)}, u32[]{:S(2)}) copy-start(f32[768]{0:T(1024)} %param.13) | copy-start | bytes 9220
  25.6 16.2 %copy-start.1 = (f32[8]{0:T(128)S(1)}, f32[8]{0:T(128)}, u32[]{:S(2)}) copy-start(f32[8]{0:T(128)} %refs_1_.5) | copy-start | bytes 100
  30.9 8.5 %collective-permute-start.6 = (bf16[96,768]{1,0:T(8,128)(2,1)S(1)}, bf16[96,768]{1,0:T(8,128)(2,1)S(1)}, u32[]{:S(2)}, u32[]{:S(2)}) collective-permute-start(bf16[96,768]{1,0:T(8,128)(2,1)S(1)} %get-tuple-element.58), channel_id=1, source_target_pairs={{0,8},{1,9},{2,10},{3,11},{4,12},{5,13},{6,14},{7,15},{8,0},{9,1},... | collective-permute-start | bytes 442376 | tf_op jit(solution)/shard_map/ppermute | solution.py:208
  32.5 9.3 %collective-permute-start.7 = (bf16[96,768]{1,0:T(8,128)(2,1)S(1)}, bf16[96,768]{1,0:T(8,128)(2,1)S(1)}, u32[]{:S(2)}, u32[]{:S(2)}) collective-permute-start(bf16[96,768]{1,0:T(8,128)(2,1)S(1)} %get-tuple-element.59), channel_id=1, source_target_pairs={{0,10},{1,11},{2,8},{3,9},{4,14},{5,15},{6,12},{7,13},{8,2},{9,3},... | collective-permute-start | bytes 442376 | tf_op jit(solution)/shard_map/ppermute | solution.py:208
  32.5 15.9 %collective-permute-start.10 = (bf16[96,768]{1,0:T(8,128)(2,1)S(1)}, bf16[96,768]{1,0:T(8,128)(2,1)S(1)}, u32[]{:S(2)}, u32[]{:S(2)}) collective-permute-start(bf16[96,768]{1,0:T(8,128)(2,1)S(1)} %get-tuple-element.68), channel_id=1, source_target_pairs={{0,2},{1,3},{2,0},{3,1},{4,6},{5,7},{6,4},{7,5},{8,10},{9,11},{10,... | collective-permute-start | bytes 442376 | tf_op jit(solution)/shard_map/ppermute | solution.py:208
  35.8 16.4 %collective-permute-start.11 = (bf16[96,768]{1,0:T(8,128)(2,1)S(1)}, bf16[96,768]{1,0:T(8,128)(2,1)S(1)}, u32[]{:S(2)}, u32[]{:S(2)}) collective-permute-start(bf16[96,768]{1,0:T(8,128)(2,1)S(1)} %get-tuple-element.70), channel_id=1, source_target_pairs={{0,12},{1,13},{2,14},{3,15},{4,8},{5,9},{6,10},{7,11},{8,4},{9,5},... | collective-permute-start | bytes 442376 | tf_op jit(solution)/shard_map/ppermute | solution.py:208
  37.2 15.2 %collective-permute-start.12 = (bf16[96,768]{1,0:T(8,128)(2,1)S(1)}, bf16[96,768]{1,0:T(8,128)(2,1)S(1)}, u32[]{:S(2)}, u32[]{:S(2)}) collective-permute-start(bf16[96,768]{1,0:T(8,128)(2,1)S(1)} %get-tuple-element.71), channel_id=1, source_target_pairs={{0,14},{1,15},{2,12},{3,13},{4,10},{5,11},{6,8},{7,9},{8,6},{9,7},... | collective-permute-start | bytes 442376 | tf_op jit(solution)/shard_map/ppermute | solution.py:208
  39.4 19.9 %collective-permute-start.16 = (bf16[96,768]{1,0:T(8,128)(2,1)S(1)}, bf16[96,768]{1,0:T(8,128)(2,1)S(1)}, u32[]{:S(2)}, u32[]{:S(2)}) collective-permute-start(bf16[96,768]{1,0:T(8,128)(2,1)S(1)} %get-tuple-element.81), channel_id=1, source_target_pairs={{0,16},{1,17},{2,18},{3,19},{4,20},{5,21},{6,22},{7,23},{8,24},{9,... | collective-permute-start | bytes 442376 | tf_op jit(solution)/shard_map/ppermute | solution.py:208
  47.0 18.4 %collective-permute-start.14 = (bf16[96,768]{1,0:T(8,128)(2,1)S(1)}, bf16[96,768]{1,0:T(8,128)(2,1)S(1)}, u32[]{:S(2)}, u32[]{:S(2)}) collective-permute-start(bf16[96,768]{1,0:T(8,128)(2,1)S(1)} %get-tuple-element.78), channel_id=1, source_target_pairs={{0,20},{1,21},{2,22},{3,23},{4,16},{5,17},{6,18},{7,19},{8,28},{9,... | collective-permute-start | bytes 442376 | tf_op jit(solution)/shard_map/ppermute | solution.py:208
  48.5 17.0 %collective-permute-start.15 = (bf16[96,768]{1,0:T(8,128)(2,1)S(1)}, bf16[96,768]{1,0:T(8,128)(2,1)S(1)}, u32[]{:S(2)}, u32[]{:S(2)}) collective-permute-start(bf16[96,768]{1,0:T(8,128)(2,1)S(1)} %get-tuple-element.79), channel_id=1, source_target_pairs={{0,22},{1,23},{2,20},{3,21},{4,18},{5,19},{6,16},{7,17},{8,30},{9,... | collective-permute-start | bytes 442376 | tf_op jit(solution)/shard_map/ppermute | solution.py:208
  52.2 13.4 %collective-permute-start.17 = (bf16[96,768]{1,0:T(8,128)(2,1)S(1)}, bf16[96,768]{1,0:T(8,128)(2,1)S(1)}, u32[]{:S(2)}, u32[]{:S(2)}) collective-permute-start(bf16[96,768]{1,0:T(8,128)(2,1)S(1)} %get-tuple-element.82), channel_id=1, source_target_pairs={{0,18},{1,19},{2,16},{3,17},{4,22},{5,23},{6,20},{7,21},{8,26},{9,... | collective-permute-start | bytes 442376 | tf_op jit(solution)/shard_map/ppermute | solution.py:208
  52.5 18.4 %collective-permute-start.19 = (bf16[96,768]{1,0:T(8,128)(2,1)S(1)}, bf16[96,768]{1,0:T(8,128)(2,1)S(1)}, u32[]{:S(2)}, u32[]{:S(2)}) collective-permute-start(bf16[96,768]{1,0:T(8,128)(2,1)S(1)} %get-tuple-element.88), channel_id=1, source_target_pairs={{0,24},{1,25},{2,26},{3,27},{4,28},{5,29},{6,30},{7,31},{8,16},{9,... | collective-permute-start | bytes 442376 | tf_op jit(solution)/shard_map/ppermute | solution.py:208
  59.3 12.9 %collective-permute-start.13 = (bf16[96,768]{1,0:T(8,128)(2,1)S(1)}, bf16[96,768]{1,0:T(8,128)(2,1)S(1)}, u32[]{:S(2)}, u32[]{:S(2)}) collective-permute-start(bf16[96,768]{1,0:T(8,128)(2,1)S(1)} %get-tuple-element.76), channel_id=1, source_target_pairs={{0,28},{1,29},{2,30},{3,31},{4,24},{5,25},{6,26},{7,27},{8,20},{9,... | collective-permute-start | bytes 442376 | tf_op jit(solution)/shard_map/ppermute | solution.py:208
  65.4 7.7 %collective-permute-start.20 = (bf16[96,768]{1,0:T(8,128)(2,1)S(1)}, bf16[96,768]{1,0:T(8,128)(2,1)S(1)}, u32[]{:S(2)}, u32[]{:S(2)}) collective-permute-start(bf16[96,768]{1,0:T(8,128)(2,1)S(1)} %get-tuple-element.89), channel_id=1, source_target_pairs={{0,26},{1,27},{2,24},{3,25},{4,30},{5,31},{6,28},{7,29},{8,18},{9,... | collective-permute-start | bytes 442376 | tf_op jit(solution)/shard_map/ppermute | solution.py:208
  67.4 9.5 %collective-permute-start.18 = (bf16[96,768]{1,0:T(8,128)(2,1)S(1)}, bf16[96,768]{1,0:T(8,128)(2,1)S(1)}, u32[]{:S(2)}, u32[]{:S(2)}) collective-permute-start(bf16[96,768]{1,0:T(8,128)(2,1)S(1)} %get-tuple-element.86), channel_id=1, source_target_pairs={{0,30},{1,31},{2,28},{3,29},{4,26},{5,27},{6,24},{7,25},{8,22},{9,... | collective-permute-start | bytes 442376 | tf_op jit(solution)/shard_map/ppermute | solution.py:208

commit v6 on v4

--- a/solution.py
+++ b/solution.py
@@ -105,12 +105,11 @@
 
 
 def make_tiles(makes, r):
-    meta, x, h, w, flipped, own, sems = (r[name] for name in ("meta", "x", "h", "w", "flipped", "own", "own_sems"))
-    _, occ_rows, _, _, rows, half = own.shape
+    meta, x, h, w, flipped, own = (r[name] for name in ("meta", "x", "h", "w", "flipped", "own"))
+    occ_rows, _, _, rows, half = own.shape
     width, chip, pairs = x.shape[-1], CORES * rows, occ_rows * occ_rows
     o, z, core = meta[0], meta[1], meta[2]
-    copies = []
-    for n, (partner, side) in enumerate(makes):
+    for partner, side in makes:
         first_j = (o ^ partner) * occ_rows
         columns = pl.ds(pl.multiple_of(((z // 2) ^ side) * half, half), half)
         ladder = jnp.dot(
@@ -120,14 +119,12 @@
             for jj in range(occ_rows):
                 m = i * occ_rows + jj
                 mixed = ladder[m * chip : (m + 1) * chip] + h[i, first_j + jj, :, :, columns].reshape(chip, half)
-                own[n, i, jj] = mixed.reshape(CORES, rows, half)
+                own[i, jj] = mixed.reshape(CORES, rows, half)
+                r["mixed", partner, side][i, jj] = own[i, jj, core]
                 flipped[:, m * chip : (m + 1) * chip] = mixed.astype(jnp.bfloat16).T
-        copies.append(pltpu.make_async_copy(own.at[n, :, :, core], r["mixed", partner, side], sems.at[n]))
-        copies[-1].start()
         for s in (0, 1):
             start = pl.multiple_of((((z & 1) ^ s) * CORES + core) * rows, rows)
             r["tile", partner, 2 * side + s][...] = flipped[pl.ds(start, rows), :]
-    return copies
 
 
 def finish_tiles(ends, r):
@@ -165,8 +162,9 @@
         for k in range(4):
             for piece, at in ((r["mine"], core), (r["theirs"], 1 - core)):
                 r["w"][pl.ds(pl.multiple_of(((z ^ k) * CORES + at) * rows, rows), rows), :] = piece[k]
-    copies = make_tiles(makes, r) if makes else []
-    copies += finish_tiles(ends, r) if ends else []
+    if makes:
+        make_tiles(makes, r)
+    copies = finish_tiles(ends, r) if ends else []
     r["token"][...] = jnp.zeros(r["token"].shape, r["token"].dtype)
     for copy in copies:
         copy.wait()
@@ -227,12 +225,11 @@
                 ins += [("mine", in_vmem(relayed), VMEM), ("theirs", in_vmem(swap(relayed, 1)), VMEM)]
                 outs.append(("w", pltpu.VMEM((width, width), bf16), VMEM))
             for partner, side in makes:
-                outs.append((("mixed", partner, side), jax.ShapeDtypeStruct((occ_rows, occ_rows, rows, half), f32), ANY))
+                outs.append((("mixed", partner, side), pltpu.VMEM((occ_rows, occ_rows, rows, half), f32), VMEM))
                 outs += [(("tile", partner, 2 * side + s), pltpu.VMEM(tile, bf16), VMEM) for s in (0, 1)]
             scratch += [
                 ("flipped", pltpu.VMEM((half, pairs * chip), bf16)),
-                ("own", pltpu.VMEM((len(makes), occ_rows, occ_rows, CORES, rows, half), f32)),
-                ("own_sems", pltpu.SemaphoreType.DMA((len(makes),))),
+                ("own", pltpu.VMEM((occ_rows, occ_rows, CORES, rows, half), f32)),
             ]
         if ends:
             count = len(ends)

time: 79.3 us -> 79.7 us (level)
  waiting for transfers between devices: 10.8 us -> 16.8 us
  Pallas kernels: 26.9 us -> 24 us
  starting transfers between devices: 39.1 us -> 36.4 us
    ppermute x20, waiting for transfers between devices: 10.8 us -> 16.8 us  [swap(): return lax.ppermute(a, axes, [(d, d ^ k) for d in range(devices)])]
    pallas_call x6, Pallas kernels: 18.2 us -> 15.4 us  [step(): pl.pallas_call(functools.partial(step_kernel, in_names + out_names + [nam...]
    ppermute x20, starting transfers between devices: 39.1 us -> 36.4 us  [swap(): return lax.ppermute(a, axes, [(d, d ^ k) for d in range(devices)])]
  transfers between devices with their start and end apart: 20 -> 20, of which waited for: 8 -> 5; matrix products, arithmetic and copies ran while one was open for 1% -> 1% of each run, Pallas kernels for 29% -> 25%
where the time goes in v6:
time: 79.7 us; the launch traced here: 79.5 us
  starting transfers between devices  36.4 us (46%)
  Pallas kernels  24 us (30%)
  waiting for transfers between devices  16.8 us (21%)
  local copies, waits for them, and re-layouts  1.42 us (2%)
    ppermute x20, starting transfers between devices, swap(): return lax.ppermute(a, axes, [(d, d ^ k) for d in range(devices)])  36.4 us
    ppermute x20, waiting for transfers between devices, swap(): return lax.ppermute(a, axes, [(d, d ^ k) for d in range(devices)])  16.8 us
    pallas_call x6, Pallas kernels, step(): pl.pallas_call(functools.partial(step_kernel, in_names + out_names + [nam...  15.4 us
    pallas_call x1, Pallas kernels, paired(): pl.pallas_call(functools.partial(prepare_kernel, block), in_specs=[SMEM,...  8.6 us
  transfers between devices with their start and end apart: 20, of which 5 were waited for; matrix products, arithmetic and copies ran while one was open for 1% of the time, Pallas kernels for 25%

profile of v6, /device:TPU:0, one launch (start us, length us, event | category | flops | bytes accessed | tf_op | source)
XLA Modules:
  0.0 79.5 jit_solution(10042245241787528471)
XLA Ops:
  0.0 0.0 copy-start
  0.0 0.5 collective-permute-start
  0.5 3.6 %collective-permute-start.2 = (bf16[96,768]{1,0:T(8,128)(2,1)}, bf16[96,768]{1,0:T(8,128)(2,1)S(1)}, u32[]{:S(2)}, u32[]{:S(2)}) collective-permute-start(bf16[96,768]{1,0:T(8,128)(2,1)} %own.3), channel_id=1, source_target_pairs={{0,4},{1,5},{2,6},{3,7},{4,0},{5,1},{6,2},{7,3},{8,12},{9,13},{10,... | collective-permute-start | bytes 442376 | tf_op jit(solution)/shard_map/ppermute | solution.py:195
  4.1 1.6 %collective-permute-start.1 = (bf16[96,768]{1,0:T(8,128)(2,1)}, bf16[96,768]{1,0:T(8,128)(2,1)S(1)}, u32[]{:S(2)}, u32[]{:S(2)}) collective-permute-start(bf16[96,768]{1,0:T(8,128)(2,1)} %own.3), channel_id=1, source_target_pairs={{0,2},{1,3},{2,0},{3,1},{4,6},{5,7},{6,4},{7,5},{8,10},{9,11},{10,... | collective-permute-start | bytes 442376 | tf_op jit(solution)/shard_map/ppermute | solution.py:195
  5.7 0.0 collective-permute-start.3
  5.7 0.7 convert_element_type.3.fock
  6.4 0.1 pad_add_fusion.meta.refs_0_
  6.4 0.0 collective-permute-done.sib
  6.4 0.0 copy-start.2
  6.4 1.4 %copy-done.2 = bf16[2,8,96,768]{3,2,1,0:T(8,128)(2,1)} copy-done((bf16[2,8,96,768]{3,2,1,0:T(8,128)(2,1)}, bf16[2,8,96,768]{3,2,1,0:T(8,128)(2,1)S(1)}, u32[]{:S(2)}) %copy-start.2) | copy-done | bytes 2359320
  7.9 8.6 %shard_map.73 = (bf16[2,8,2,96,768]{4,3,2,1,0:T(8,128)(2,1)S(1)}, f32[2,8,2,96,768]{4,3,2,1,0:T(8,128)S(1)}, bf16[4,96,768]{2,1,0:T(8,128)(2,1)S(1)}) custom-call(s32[3]{0:T(128)S(1)} %pad_add_fusion.meta.refs_0_, f32[8,8]{1,0:T(8,128)S(1)} %convert_element_type.3.fock, bf16[2,8,96,768]{3,2,1,0:T(8,128)(2,1)} %own.2, bf16[2,8,96,768]{3,2,1,0:T(8,128)(2,1)} %copy-done.2, ...), custom_call_target="tpu_custom_call" | custom-call | tf_op jit(solution)/shard_map/pallas_call | solution.py:200
  16.5 0.0 collective-permute-done.2.middle
  16.5 0.0 collective-permute-done.1.near
  16.5 0.0 collective-permute-done.3.far
  16.5 0.0 copy-done
  16.5 0.1 shard_map.74.refs_3_
  16.6 0.1 collective-permute-start.4
  16.7 2.0 %collective-permute-done.4.refs_4_ = bf16[4,96,768]{2,1,0:T(8,128)(2,1)S(1)} collective-permute-done((bf16[4,96,768]{2,1,0:T(8,128)(2,1)S(1)}, bf16[4,96,768]{2,1,0:T(8,128)(2,1)S(1)}, u32[]{:S(2)}, u32[]{:S(2)}) %collective-permute-start.4) | collective-permute-done | bytes 589856 | tf_op jit(solution)/shard_map/ppermute | solution.py:195
  18.6 1.7 %shard_map.75 = (bf16[768,768]{1,0:T(8,128)(2,1)S(1)}, f32[2,2,96,384]{3,2,1,0:T(8,128)S(1)}, bf16[96,768]{1,0:T(8,128)(2,1)S(1)}, bf16[96,768]{1,0:T(8,128)(2,1)S(1)}, f32[8,128]{1,0:T(8,128)S(1)}) custom-call(s32[3]{0:T(128)S(1)} %pad_add_fusion.meta.refs_0_, bf16[2,8,2,96,768]{4,3,2,1,0:T(8,128)(2,1)S(1)} %get-tuple-element.46.refs_1_, ...), custom_call_target="tpu_custom_call" | custom-call | tf_op jit(solution)/shard_map/pallas_call | solution.py:257
  20.4 4.5 %collective-permute-start.7 = (bf16[96,768]{1,0:T(8,128)(2,1)S(1)}, bf16[96,768]{1,0:T(8,128)(2,1)S(1)}, u32[]{:S(2)}, u32[]{:S(2)}) collective-permute-start(bf16[96,768]{1,0:T(8,128)(2,1)S(1)} %get-tuple-element.55), channel_id=1, source_target_pairs={{0,4},{1,5},{2,6},{3,7},{4,0},{5,1},{6,2},{7,3},{8,12},{9,13},{10,... | collective-permute-start | bytes 442376 | tf_op jit(solution)/shard_map/ppermute | solution.py:195
  24.9 0.5 collective-permute-start.8
  25.4 0.0 copy-start.3
  25.4 0.0 copy-start.1
  25.4 3.6 %shard_map.76 = (f32[2,2,96,384]{3,2,1,0:T(8,128)S(1)}, bf16[96,768]{1,0:T(8,128)(2,1)S(1)}, bf16[96,768]{1,0:T(8,128)(2,1)S(1)}, f32[2,2,96,384]{3,2,1,0:T(8,12...) custom-call(s32[3]{0:T(128)S(1)} %pad_add_fusion.meta.refs_0_, ...), custom_call_target="tpu_custom_call" | custom-call | tf_op jit(solution)/shard_map/pallas_call | solution.py:257
  29.1 1.6 %collective-permute-start.5 = (bf16[96,768]{1,0:T(8,128)(2,1)S(1)}, bf16[96,768]{1,0:T(8,128)(2,1)S(1)}, u32[]{:S(2)}, u32[]{:S(2)}) collective-permute-start(bf16[96,768]{1,0:T(8,128)(2,1)S(1)} %get-tuple-element.52), channel_id=1, source_target_pairs={{0,8},{1,9},{2,10},{3,11},{4,12},{5,13},{6,14},{7,15},{8,0},{9,1},... | collective-permute-start | bytes 442376 | tf_op jit(solution)/shard_map/ppermute | solution.py:195
  30.6 0.1 collective-permute-start.6
  30.7 1.9 %collective-permute-start.9 = (bf16[96,768]{1,0:T(8,128)(2,1)S(1)}, bf16[96,768]{1,0:T(8,128)(2,1)S(1)}, u32[]{:S(2)}, u32[]{:S(2)}) collective-permute-start(bf16[96,768]{1,0:T(8,128)(2,1)S(1)} %get-tuple-element.62), channel_id=1, source_target_pairs={{0,2},{1,3},{2,0},{3,1},{4,6},{5,7},{6,4},{7,5},{8,10},{9,11},{10,... | collective-permute-start | bytes 442376 | tf_op jit(solution)/shard_map/ppermute | solution.py:195
  32.6 3.0 %collective-permute-done.7.refs_10_ = bf16[96,768]{1,0:T(8,128)(2,1)S(1)} collective-permute-done((bf16[96,768]{1,0:T(8,128)(2,1)S(1)}, bf16[96,768]{1,0:T(8,128)(2,1)S(1)}, u32[]{:S(2)}, u32[]{:S(2)}) %collective-permute-start.7) | collective-permute-done | bytes 147488 | tf_op jit(solution)/shard_map/ppermute | solution.py:195
  35.7 0.5 collective-permute-start.10
  36.1 0.0 copy-done.3
  36.1 0.0 collective-permute-done.8.refs_11_
  36.1 3.1 %collective-permute-start.11 = (bf16[96,768]{1,0:T(8,128)(2,1)S(1)}, bf16[96,768]{1,0:T(8,128)(2,1)S(1)}, u32[]{:S(2)}, u32[]{:S(2)}) collective-permute-start(bf16[96,768]{1,0:T(8,128)(2,1)S(1)} %get-tuple-element.65), channel_id=1, source_target_pairs={{0,14},{1,15},{2,12},{3,13},{4,10},{5,11},{6,8},{7,9},{8,6},{9,7},... | collective-permute-start | bytes 442376 | tf_op jit(solution)/shard_map/ppermute | solution.py:195
  39.2 0.0 collective-permute-done.5.refs_7_
  39.2 1.5 %collective-permute-start.15 = (bf16[96,768]{1,0:T(8,128)(2,1)S(1)}, bf16[96,768]{1,0:T(8,128)(2,1)S(1)}, u32[]{:S(2)}, u32[]{:S(2)}) collective-permute-start(bf16[96,768]{1,0:T(8,128)(2,1)S(1)} %get-tuple-element.75), channel_id=1, source_target_pairs={{0,16},{1,17},{2,18},{3,19},{4,20},{5,21},{6,22},{7,23},{8,24},{9,... | collective-permute-start | bytes 442376 | tf_op jit(solution)/shard_map/ppermute | solution.py:195
  40.7 0.0 collective-permute-done.6.refs_8_
  40.7 0.0 copy-done.1
  40.7 4.1 %shard_map.77 = (f32[2,2,96,384]{3,2,1,0:T(8,128)S(1)}, bf16[96,768]{1,0:T(8,128)(2,1)S(1)}, bf16[96,768]{1,0:T(8,128)(2,1)S(1)}, f32[2,2,96,384]{3,2,1,0:T(8,12...) custom-call(s32[3]{0:T(128)S(1)} %pad_add_fusion.meta.refs_0_, ...), custom_call_target="tpu_custom_call", output_to_operand_aliasing={{10}: (12, {})} | custom-call | tf_op jit(solution)/shard_map/pallas_call | solution.py:257
  44.9 2.5 %collective-permute-start.13 = (bf16[96,768]{1,0:T(8,128)(2,1)S(1)}, bf16[96,768]{1,0:T(8,128)(2,1)S(1)}, u32[]{:S(2)}, u32[]{:S(2)}) collective-permute-start(bf16[96,768]{1,0:T(8,128)(2,1)S(1)} %get-tuple-element.72), channel_id=1, source_target_pairs={{0,20},{1,21},{2,22},{3,23},{4,16},{5,17},{6,18},{7,19},{8,28},{9,... | collective-permute-start | bytes 442376 | tf_op jit(solution)/shard_map/ppermute | solution.py:195
  47.4 0.0 collective-permute-done.9.refs_5_
  47.4 3.1 %collective-permute-start.14 = (bf16[96,768]{1,0:T(8,128)(2,1)S(1)}, bf16[96,768]{1,0:T(8,128)(2,1)S(1)}, u32[]{:S(2)}, u32[]{:S(2)}) collective-permute-start(bf16[96,768]{1,0:T(8,128)(2,1)S(1)} %get-tuple-element.73), channel_id=1, source_target_pairs={{0,22},{1,23},{2,20},{3,21},{4,18},{5,19},{6,16},{7,17},{8,30},{9,... | collective-permute-start | bytes 442376 | tf_op jit(solution)/shard_map/ppermute | solution.py:195
  50.4 4.5 %collective-permute-done.10.refs_7_ = bf16[96,768]{1,0:T(8,128)(2,1)S(1)} collective-permute-done((bf16[96,768]{1,0:T(8,128)(2,1)S(1)}, bf16[96,768]{1,0:T(8,128)(2,1)S(1)}, u32[]{:S(2)}, u32[]{:S(2)}) %collective-permute-start.10) | collective-permute-done | bytes 147488 | tf_op jit(solution)/shard_map/ppermute | solution.py:195
  54.9 0.0 collective-permute-start.16
  54.9 0.0 collective-permute-done.11.refs_8_
  54.9 2.1 %collective-permute-start.18 = (bf16[96,768]{1,0:T(8,128)(2,1)S(1)}, bf16[96,768]{1,0:T(8,128)(2,1)S(1)}, u32[]{:S(2)}, u32[]{:S(2)}) collective-permute-start(bf16[96,768]{1,0:T(8,128)(2,1)S(1)} %get-tuple-element.82), channel_id=1, source_target_pairs={{0,24},{1,25},{2,26},{3,27},{4,28},{5,29},{6,30},{7,31},{8,16},{9,... | collective-permute-start | bytes 442376 | tf_op jit(solution)/shard_map/ppermute | solution.py:195
  57.0 1.8 %shard_map.78 = (f32[2,8,96,768]{3,2,1,0:T(8,128)}, bf16[96,768]{1,0:T(8,128)(2,1)S(1)}, bf16[96,768]{1,0:T(8,128)(2,1)S(1)}, f32[8,128]{1,0:T(8,128)S(1)}) custom-call(s32[3]{0:T(128)S(1)} %pad_add_fusion.meta.refs_0_, f32[8]{0:T(128)S(1)} %copy-done.1, ...), custom_call_target="tpu_custom_call", output_to_operand_aliasing={{0}: (9, {}), {1}: (10, {}), {2}: (11, {})} | custom-call | tf_op jit(solution)/shard_map/pallas_call | solution.py:257
  58.7 0.0 collective-permute-done.15.refs_7_
  58.7 6.5 %collective-permute-start.12 = (bf16[96,768]{1,0:T(8,128)(2,1)S(1)}, bf16[96,768]{1,0:T(8,128)(2,1)S(1)}, u32[]{:S(2)}, u32[]{:S(2)}) collective-permute-start(bf16[96,768]{1,0:T(8,128)(2,1)S(1)} %get-tuple-element.70), channel_id=1, source_target_pairs={{0,28},{1,29},{2,30},{3,31},{4,24},{5,25},{6,26},{7,27},{8,20},{9,... | collective-permute-start | bytes 442376 | tf_op jit(solution)/shard_map/ppermute | solution.py:195
  65.2 0.0 collective-permute-done.13.refs_4_
  65.2 0.0 collective-permute-start.19
  65.2 0.0 collective-permute-done.14.refs_5_
  65.2 0.0 collective-permute-done.16.refs_8_
  65.2 1.7 %shard_map.79 = (f32[2,8,96,768]{3,2,1,0:T(8,128)}, bf16[96,768]{1,0:T(8,128)(2,1)S(1)}, f32[8,128]{1,0:T(8,128)S(1)}) custom-call(s32[3]{0:T(128)S(1)} %pad_add_fusion.meta.refs_0_, f32[8]{0:T(128)S(1)} %copy-done.1, f32[1,768]{1,0:T(1,128)S(1)} %reshape.3.refs_5_.refs_2_, ...), custom_call_target="tpu_custom_call", output_to_operand_aliasing={{0}: (9, {}), {1}: (10, {})} | custom-call | tf_op jit(solution)/shard_map/pallas_call | solution.py:257
  67.0 2.9 %collective-permute-start.17 = (bf16[96,768]{1,0:T(8,128)(2,1)S(1)}, bf16[96,768]{1,0:T(8,128)(2,1)S(1)}, u32[]{:S(2)}, u32[]{:S(2)}) collective-permute-start(bf16[96,768]{1,0:T(8,128)(2,1)S(1)} %get-tuple-element.80), channel_id=1, source_target_pairs={{0,30},{1,31},{2,28},{3,29},{4,26},{5,27},{6,24},{7,25},{8,22},{9,... | collective-permute-start | bytes 442376 | tf_op jit(solution)/shard_map/ppermute | solution.py:195
  69.9 0.0 collective-permute-done.18.refs_7_
  69.9 5.4 %collective-permute-done.12.refs_4_ = bf16[96,768]{1,0:T(8,128)(2,1)S(1)} collective-permute-done((bf16[96,768]{1,0:T(8,128)(2,1)S(1)}, bf16[96,768]{1,0:T(8,128)(2,1)S(1)}, u32[]{:S(2)}, u32[]{:S(2)}) %collective-permute-start.12) | collective-permute-done | bytes 147488 | tf_op jit(solution)/shard_map/ppermute | solution.py:195
  75.4 0.0 collective-permute-done.19.refs_8_
  75.4 1.8 %collective-permute-done.17.refs_5_ = bf16[96,768]{1,0:T(8,128)(2,1)S(1)} collective-permute-done((bf16[96,768]{1,0:T(8,128)(2,1)S(1)}, bf16[96,768]{1,0:T(8,128)(2,1)S(1)}, u32[]{:S(2)}, u32[]{:S(2)}) %collective-permute-start.17) | collective-permute-done | bytes 147488 | tf_op jit(solution)/shard_map/ppermute | solution.py:195
  77.1 2.3 %shard_map.80 = (f32[2,8,96,768]{3,2,1,0:T(8,128)}, f32[8,128]{1,0:T(8,128)}) custom-call(s32[3]{0:T(128)S(1)} %pad_add_fusion.meta.refs_0_, f32[8]{0:T(128)S(1)} %copy-done.1, f32[1,768]{1,0:T(1,128)S(1)} %reshape.3.refs_5_.refs_2_, f32[2,2,96,384]{3,2,1,0:T(8,128)S(1)} %get-tuple-element.59.refs_3_, ...), custom_call_target="tpu_custom_call", output_to_operand_aliasing={{0}: (9, {})} | custom-call | tf_op jit(solution)/shard_map/pallas_call | solution.py:257
  (1 shorter events, 0.0 us)
Async XLA Ops:
  0.0 16.5 %copy-start = (bf16[96,768]{1,0:T(8,128)(2,1)S(1)}, bf16[96,768]{1,0:T(8,128)(2,1)}, u32[]{:S(2)}) copy-start(bf16[96,768]{1,0:T(8,128)(2,1)} %own.3) | copy-start | bytes 442372
  0.0 6.4 %collective-permute-start = (bf16[2,8,96,768]{3,2,1,0:T(8,128)(2,1)}, bf16[2,8,96,768]{3,2,1,0:T(8,128)(2,1)S(1)}, u32[]{:S(2)}, u32[]{:S(2)}) collective-permute-start(bf16[2,8,96,768]{3,2,1,0:T(8,128)(2,1)} %own.2), channel_id=1, source_target_pairs={{0,1},{1,0},{2,3},{3,2},{4,5},{5,4},{6,7},{7,6},{8,9},{9,8},{10,11... | collective-permute-start | bytes 7077896 | tf_op jit(solution)/shard_map/ppermute | solution.py:195
  0.5 16.0 %collective-permute-start.2 = (bf16[96,768]{1,0:T(8,128)(2,1)}, bf16[96,768]{1,0:T(8,128)(2,1)S(1)}, u32[]{:S(2)}, u32[]{:S(2)}) collective-permute-start(bf16[96,768]{1,0:T(8,128)(2,1)} %own.3), channel_id=1, source_target_pairs={{0,4},{1,5},{2,6},{3,7},{4,0},{5,1},{6,2},{7,3},{8,12},{9,13},{10,... | collective-permute-start | bytes 442376 | tf_op jit(solution)/shard_map/ppermute | solution.py:195
  4.1 12.4 %collective-permute-start.1 = (bf16[96,768]{1,0:T(8,128)(2,1)}, bf16[96,768]{1,0:T(8,128)(2,1)S(1)}, u32[]{:S(2)}, u32[]{:S(2)}) collective-permute-start(bf16[96,768]{1,0:T(8,128)(2,1)} %own.3), channel_id=1, source_target_pairs={{0,2},{1,3},{2,0},{3,1},{4,6},{5,7},{6,4},{7,5},{8,10},{9,11},{10,... | collective-permute-start | bytes 442376 | tf_op jit(solution)/shard_map/ppermute | solution.py:195
  5.7 10.8 %collective-permute-start.3 = (bf16[96,768]{1,0:T(8,128)(2,1)}, bf16[96,768]{1,0:T(8,128)(2,1)S(1)}, u32[]{:S(2)}, u32[]{:S(2)}) collective-permute-start(bf16[96,768]{1,0:T(8,128)(2,1)} %own.3), channel_id=1, source_target_pairs={{0,6},{1,7},{2,4},{3,5},{4,2},{5,3},{6,0},{7,1},{8,14},{9,15},{10,... | collective-permute-start | bytes 442376 | tf_op jit(solution)/shard_map/ppermute | solution.py:195
  6.4 1.4 %copy-start.2 = (bf16[2,8,96,768]{3,2,1,0:T(8,128)(2,1)}, bf16[2,8,96,768]{3,2,1,0:T(8,128)(2,1)S(1)}, u32[]{:S(2)}) copy-start(bf16[2,8,96,768]{3,2,1,0:T(8,128)(2,1)S(1)} %collective-permute-done.sib) | copy-start | bytes 7077892
  16.6 2.1 %collective-permute-start.4 = (bf16[4,96,768]{2,1,0:T(8,128)(2,1)S(1)}, bf16[4,96,768]{2,1,0:T(8,128)(2,1)S(1)}, u32[]{:S(2)}, u32[]{:S(2)}) collective-permute-start(bf16[4,96,768]{2,1,0:T(8,128)(2,1)S(1)} %shard_map.74.refs_3_), channel_id=1, source_target_pairs={{0,1},{1,0},{2,3},{3,2},{4,5},{5,4},{6,7},{7,6},{8,9},{9,8},{10,11... | collective-permute-start | bytes 1769480 | tf_op jit(solution)/shard_map/ppermute | solution.py:195
  20.4 15.3 %collective-permute-start.7 = (bf16[96,768]{1,0:T(8,128)(2,1)S(1)}, bf16[96,768]{1,0:T(8,128)(2,1)S(1)}, u32[]{:S(2)}, u32[]{:S(2)}) collective-permute-start(bf16[96,768]{1,0:T(8,128)(2,1)S(1)} %get-tuple-element.55), channel_id=1, source_target_pairs={{0,4},{1,5},{2,6},{3,7},{4,0},{5,1},{6,2},{7,3},{8,12},{9,13},{10,... | collective-permute-start | bytes 442376 | tf_op jit(solution)/shard_map/ppermute | solution.py:195
  24.9 11.3 %collective-permute-start.8 = (bf16[96,768]{1,0:T(8,128)(2,1)S(1)}, bf16[96,768]{1,0:T(8,128)(2,1)S(1)}, u32[]{:S(2)}, u32[]{:S(2)}) collective-permute-start(bf16[96,768]{1,0:T(8,128)(2,1)S(1)} %get-tuple-element.56), channel_id=1, source_target_pairs={{0,6},{1,7},{2,4},{3,5},{4,2},{5,3},{6,0},{7,1},{8,14},{9,15},{10,... | collective-permute-start | bytes 442376 | tf_op jit(solution)/shard_map/ppermute | solution.py:195
  25.4 10.7 %copy-start.3 = (f32[768]{0:T(1024)S(1)}, f32[768]{0:T(1024)}, u32[]{:S(2)}) copy-start(f32[768]{0:T(1024)} %param.13) | copy-start | bytes 9220
  25.4 15.3 %copy-start.1 = (f32[8]{0:T(128)S(1)}, f32[8]{0:T(128)}, u32[]{:S(2)}) copy-start(f32[8]{0:T(128)} %refs_1_.5) | copy-start | bytes 100
  29.1 10.2 %collective-permute-start.5 = (bf16[96,768]{1,0:T(8,128)(2,1)S(1)}, bf16[96,768]{1,0:T(8,128)(2,1)S(1)}, u32[]{:S(2)}, u32[]{:S(2)}) collective-permute-start(bf16[96,768]{1,0:T(8,128)(2,1)S(1)} %get-tuple-element.52), channel_id=1, source_target_pairs={{0,8},{1,9},{2,10},{3,11},{4,12},{5,13},{6,14},{7,15},{8,0},{9,1},... | collective-permute-start | bytes 442376 | tf_op jit(solution)/shard_map/ppermute | solution.py:195
  30.6 10.1 %collective-permute-start.6 = (bf16[96,768]{1,0:T(8,128)(2,1)S(1)}, bf16[96,768]{1,0:T(8,128)(2,1)S(1)}, u32[]{:S(2)}, u32[]{:S(2)}) collective-permute-start(bf16[96,768]{1,0:T(8,128)(2,1)S(1)} %get-tuple-element.53), channel_id=1, source_target_pairs={{0,10},{1,11},{2,8},{3,9},{4,14},{5,15},{6,12},{7,13},{8,2},{9,3},... | collective-permute-start | bytes 442376 | tf_op jit(solution)/shard_map/ppermute | solution.py:195
  30.7 16.7 %collective-permute-start.9 = (bf16[96,768]{1,0:T(8,128)(2,1)S(1)}, bf16[96,768]{1,0:T(8,128)(2,1)S(1)}, u32[]{:S(2)}, u32[]{:S(2)}) collective-permute-start(bf16[96,768]{1,0:T(8,128)(2,1)S(1)} %get-tuple-element.62), channel_id=1, source_target_pairs={{0,2},{1,3},{2,0},{3,1},{4,6},{5,7},{6,4},{7,5},{8,10},{9,11},{10,... | collective-permute-start | bytes 442376 | tf_op jit(solution)/shard_map/ppermute | solution.py:195
  35.7 19.2 %collective-permute-start.10 = (bf16[96,768]{1,0:T(8,128)(2,1)S(1)}, bf16[96,768]{1,0:T(8,128)(2,1)S(1)}, u32[]{:S(2)}, u32[]{:S(2)}) collective-permute-start(bf16[96,768]{1,0:T(8,128)(2,1)S(1)} %get-tuple-element.64), channel_id=1, source_target_pairs={{0,12},{1,13},{2,14},{3,15},{4,8},{5,9},{6,10},{7,11},{8,4},{9,5},... | collective-permute-start | bytes 442376 | tf_op jit(solution)/shard_map/ppermute | solution.py:195
  36.1 18.8 %collective-permute-start.11 = (bf16[96,768]{1,0:T(8,128)(2,1)S(1)}, bf16[96,768]{1,0:T(8,128)(2,1)S(1)}, u32[]{:S(2)}, u32[]{:S(2)}) collective-permute-start(bf16[96,768]{1,0:T(8,128)(2,1)S(1)} %get-tuple-element.65), channel_id=1, source_target_pairs={{0,14},{1,15},{2,12},{3,13},{4,10},{5,11},{6,8},{7,9},{8,6},{9,7},... | collective-permute-start | bytes 442376 | tf_op jit(solution)/shard_map/ppermute | solution.py:195
  39.2 19.5 %collective-permute-start.15 = (bf16[96,768]{1,0:T(8,128)(2,1)S(1)}, bf16[96,768]{1,0:T(8,128)(2,1)S(1)}, u32[]{:S(2)}, u32[]{:S(2)}) collective-permute-start(bf16[96,768]{1,0:T(8,128)(2,1)S(1)} %get-tuple-element.75), channel_id=1, source_target_pairs={{0,16},{1,17},{2,18},{3,19},{4,20},{5,21},{6,22},{7,23},{8,24},{9,... | collective-permute-start | bytes 442376 | tf_op jit(solution)/shard_map/ppermute | solution.py:195
  44.9 20.3 %collective-permute-start.13 = (bf16[96,768]{1,0:T(8,128)(2,1)S(1)}, bf16[96,768]{1,0:T(8,128)(2,1)S(1)}, u32[]{:S(2)}, u32[]{:S(2)}) collective-permute-start(bf16[96,768]{1,0:T(8,128)(2,1)S(1)} %get-tuple-element.72), channel_id=1, source_target_pairs={{0,20},{1,21},{2,22},{3,23},{4,16},{5,17},{6,18},{7,19},{8,28},{9,... | collective-permute-start | bytes 442376 | tf_op jit(solution)/shard_map/ppermute | solution.py:195
  47.4 17.8 %collective-permute-start.14 = (bf16[96,768]{1,0:T(8,128)(2,1)S(1)}, bf16[96,768]{1,0:T(8,128)(2,1)S(1)}, u32[]{:S(2)}, u32[]{:S(2)}) collective-permute-start(bf16[96,768]{1,0:T(8,128)(2,1)S(1)} %get-tuple-element.73), channel_id=1, source_target_pairs={{0,22},{1,23},{2,20},{3,21},{4,18},{5,19},{6,16},{7,17},{8,30},{9,... | collective-permute-start | bytes 442376 | tf_op jit(solution)/shard_map/ppermute | solution.py:195
  54.9 10.3 %collective-permute-start.16 = (bf16[96,768]{1,0:T(8,128)(2,1)S(1)}, bf16[96,768]{1,0:T(8,128)(2,1)S(1)}, u32[]{:S(2)}, u32[]{:S(2)}) collective-permute-start(bf16[96,768]{1,0:T(8,128)(2,1)S(1)} %get-tuple-element.76), channel_id=1, source_target_pairs={{0,18},{1,19},{2,16},{3,17},{4,22},{5,23},{6,20},{7,21},{8,26},{9,... | collective-permute-start | bytes 442376 | tf_op jit(solution)/shard_map/ppermute | solution.py:195
  54.9 15.0 %collective-permute-start.18 = (bf16[96,768]{1,0:T(8,128)(2,1)S(1)}, bf16[96,768]{1,0:T(8,128)(2,1)S(1)}, u32[]{:S(2)}, u32[]{:S(2)}) collective-permute-start(bf16[96,768]{1,0:T(8,128)(2,1)S(1)} %get-tuple-element.82), channel_id=1, source_target_pairs={{0,24},{1,25},{2,26},{3,27},{4,28},{5,29},{6,30},{7,31},{8,16},{9,... | collective-permute-start | bytes 442376 | tf_op jit(solution)/shard_map/ppermute | solution.py:195
  58.7 16.6 %collective-permute-start.12 = (bf16[96,768]{1,0:T(8,128)(2,1)S(1)}, bf16[96,768]{1,0:T(8,128)(2,1)S(1)}, u32[]{:S(2)}, u32[]{:S(2)}) collective-permute-start(bf16[96,768]{1,0:T(8,128)(2,1)S(1)} %get-tuple-element.70), channel_id=1, source_target_pairs={{0,28},{1,29},{2,30},{3,31},{4,24},{5,25},{6,26},{7,27},{8,20},{9,... | collective-permute-start | bytes 442376 | tf_op jit(solution)/shard_map/ppermute | solution.py:195
  65.2 10.2 %collective-permute-start.19 = (bf16[96,768]{1,0:T(8,128)(2,1)S(1)}, bf16[96,768]{1,0:T(8,128)(2,1)S(1)}, u32[]{:S(2)}, u32[]{:S(2)}) collective-permute-start(bf16[96,768]{1,0:T(8,128)(2,1)S(1)} %get-tuple-element.83), channel_id=1, source_target_pairs={{0,26},{1,27},{2,24},{3,25},{4,30},{5,31},{6,28},{7,29},{8,18},{9,... | collective-permute-start | bytes 442376 | tf_op jit(solution)/shard_map/ppermute | solution.py:195
  67.0 10.2 %collective-permute-start.17 = (bf16[96,768]{1,0:T(8,128)(2,1)S(1)}, bf16[96,768]{1,0:T(8,128)(2,1)S(1)}, u32[]{:S(2)}, u32[]{:S(2)}) collective-permute-start(bf16[96,768]{1,0:T(8,128)(2,1)S(1)} %get-tuple-element.80), channel_id=1, source_target_pairs={{0,30},{1,31},{2,28},{3,29},{4,26},{5,27},{6,24},{7,25},{8,22},{9,... | collective-permute-start | bytes 442376 | tf_op jit(solution)/shard_map/ppermute | solution.py:195
